TPU v7x, 256 devices: a whole 4x4x8 slice. The times are simulated.
256 devices in a mesh: dp: 128 (over z, y, x), ctx: 2 (over core).
Axes of the slice: x: 4, y: 4, z: 8, core: 2. Of those that a mesh axis runs over, the one named last changes fastest.
Arguments:
- queries: bfloat16 [128, 512, 2048], P('dp', 'ctx'), may hold values from -24 to 24
- keys: bfloat16 [128, 512, 2048], P('dp', 'ctx'), may hold values from -24 to 24
- values: bfloat16 [128, 512, 2048], P('dp', 'ctx'), may hold values from -6 to 6
- residual: bfloat16 [128, 512, 2048], P('dp', 'ctx'), may hold values from -6 to 6
- grad_out: bfloat16 [128, 512, 2048], P('dp', 'ctx'), may hold values from -6 to 6
- latents: bfloat16 [128, 2, 32, 128], P('dp', 'ctx'), may hold values from -6 to 6
- image_starts: int32 [128, 2], P('dp'), may hold values from 0 to 384, as said below
- w_first: bfloat16 [32, 512], replicated, may hold values from -1 to 1
- w_second: bfloat16 [512, 2048], replicated, may hold values from -0.25 to 0.25
Outputs:
- layer_out: bfloat16 [128, 512, 2048], P('dp', 'ctx')
- grad_queries: bfloat16 [128, 512, 2048], P('dp', 'ctx')
- grad_keys: bfloat16 [128, 512, 2048], P('dp', 'ctx')
- grad_values: bfloat16 [128, 512, 2048], P('dp', 'ctx')
- grad_w_first: float32 [32, 512], replicated
- grad_w_second: float32 [512, 2048], P(None, 'ctx')
Inputs may be any that keep to these rules, and one draw needn't show every extreme that they name: `image_starts`: within a document the spans of 128 positions that start at these offsets never intersect; one span starts at 0 and one ends at 512; entry i belongs to the image held as latents[:, i].
All inputs are finite; a program needn't handle non-finite values.
Results may differ from a plain program's by a relative error of at most 0.011.
Values may be sent and summed in bfloat16 or wider, within the bound.
No kernel may reach another device: no remote copies, remote signals or barrier semaphores. Data moves between devices by JAX's collectives and lax.ppermute only.
A program may use at most 128 MiB of HBM per device.

v0:
```python
import jax
import jax.numpy as jnp
from jax import lax
from jax.sharding import PartitionSpec as P

HEADS = 16


def locate(positions, span_starts, span_len):
    inside = (positions[:, None] >= span_starts[None, :]) & (
        positions[:, None] < span_starts[None, :] + span_len
    )
    hit_table = inside.astype(jnp.int32)
    is_image = jnp.sum(hit_table, axis=1) > 0
    slot_ids = jnp.arange(span_starts.shape[0], dtype=jnp.int32)
    image_id = jnp.where(is_image, jnp.sum(hit_table * slot_ids[None, :], axis=1), -1)
    offset = positions - jnp.sum(hit_table * span_starts[None, :], axis=1)
    slot_index = jnp.where(is_image, image_id * span_len + offset, 0)
    return (image_id, is_image, slot_index)


def allowed(query_pos, query_img, key_pos, key_img):
    causal = key_pos[None, :] <= query_pos[:, None]
    same_image = (query_img[:, None] == key_img[None, :]) & (query_img[:, None] >= 0)
    return causal | same_image


def encode(patch_rows, w_first, w_second):
    pre_act = jnp.dot(patch_rows, w_first, preferred_element_type=jnp.float32)
    hidden = jax.nn.silu(pre_act).astype(jnp.bfloat16)
    embedding = jnp.dot(hidden, w_second, preferred_element_type=jnp.float32).astype(jnp.bfloat16)
    return (pre_act, hidden, embedding)


def encode_grads(patch_rows, pre_act, hidden, grad_embed, w_second):
    back_hidden = lax.dot_general(
        grad_embed, w_second, (((1,), (1,)), ((), ())), preferred_element_type=jnp.float32
    )
    gate_sig = jax.nn.sigmoid(pre_act)
    grad_pre = (back_hidden * gate_sig * (1.0 + pre_act * (1.0 - gate_sig))).astype(jnp.bfloat16)
    grad_second = lax.dot_general(
        hidden, grad_embed, (((0,), (0,)), ((), ())), preferred_element_type=jnp.float32
    )
    grad_first = lax.dot_general(
        patch_rows, grad_pre, (((0,), (0,)), ((), ())), preferred_element_type=jnp.float32
    )
    return (grad_first, grad_second)


def local(queries, keys, values, residual, grad_out, latents, image_starts, w_first, w_second):
    tok_count = queries.shape[1]
    model_width = queries.shape[2]
    head_count = HEADS
    head_size = model_width // head_count
    span_len = latents.shape[3]
    ctx_index = lax.axis_index("ctx")
    ctx_count = lax.axis_size("ctx")
    seq_len = tok_count * ctx_count
    score_scale = head_size ** (-0.5)
    span_starts = image_starts[0]
    positions = ctx_index * tok_count + jnp.arange(tok_count, dtype=jnp.int32)
    image_id, is_image, slot_index = locate(positions, span_starts, span_len)
    every_pos = jnp.arange(seq_len, dtype=jnp.int32)
    every_img, every_flag, every_slot = locate(every_pos, span_starts, span_len)
    query_rows = queries[0]
    key_rows = keys[0]
    value_rows = values[0]
    grad_rows = grad_out[0]
    own_patches = jnp.transpose(latents[0, 0])
    pre_act, hidden, embedding = encode(own_patches, w_first, w_second)
    every_embed = lax.all_gather(embedding, "ctx", axis=0, tiled=True)
    mixed = jnp.where(is_image[:, None], every_embed[slot_index], residual[0])
    key_all, value_all = (
        lax.all_gather(key_rows, "ctx", axis=0, tiled=True),
        lax.all_gather(value_rows, "ctx", axis=0, tiled=True),
    )
    query_heads = query_rows.reshape(tok_count, head_count, head_size)
    key_heads = key_all.reshape(seq_len, head_count, head_size)
    value_heads = value_all.reshape(seq_len, head_count, head_size)
    grad_heads = grad_rows.reshape(tok_count, head_count, head_size)
    visible = allowed(positions, image_id, every_pos, every_img)[None]
    scores = (
        jnp.einsum("thd,shd->hts", query_heads, key_heads, preferred_element_type=jnp.float32)
        * score_scale
    )
    scores = jnp.where(visible, scores, -1e30)
    row_max = jnp.max(scores, axis=2, keepdims=True)
    weights = jnp.where(visible, jnp.exp(scores - row_max), 0.0)
    totals = jnp.sum(weights, axis=2, keepdims=True)
    probs = (weights / totals).astype(jnp.bfloat16)
    attended = jnp.einsum("hts,shd->thd", probs, value_heads, preferred_element_type=jnp.float32)
    layer_rows = (mixed.astype(jnp.float32) + attended.reshape(tok_count, model_width)).astype(
        jnp.bfloat16
    )
    log_total = row_max + jnp.log(totals)
    out_dot = jnp.sum(grad_heads.astype(jnp.float32) * attended, axis=2)
    back_probs = jnp.where(visible, jnp.exp(scores - log_total), 0.0)
    grad_probs = jnp.einsum(
        "thd,shd->hts", grad_heads, value_heads, preferred_element_type=jnp.float32
    )
    grad_scores = (back_probs * (grad_probs - jnp.transpose(out_dot)[:, :, None])).astype(
        jnp.bfloat16
    )
    grad_q = (
        jnp.einsum("hts,shd->thd", grad_scores, key_heads, preferred_element_type=jnp.float32)
        * score_scale
    ).astype(jnp.bfloat16)
    own_keys = key_rows.reshape(tok_count, head_count, head_size)
    own_values = value_rows.reshape(tok_count, head_count, head_size)
    every_log, every_dot = (
        lax.all_gather(jnp.transpose(log_total[:, :, 0]), "ctx", axis=0, tiled=True),
        lax.all_gather(out_dot, "ctx", axis=0, tiled=True),
    )
    piece_query = lax.all_gather(query_rows, "ctx", axis=0, tiled=True)
    piece_grad = lax.all_gather(grad_rows, "ctx", axis=0, tiled=True)
    row_count = piece_query.shape[0]
    piece_pos = jnp.arange(row_count, dtype=jnp.int32)
    piece_img, piece_flag, piece_slot = locate(piece_pos, span_starts, span_len)
    seen = allowed(piece_pos, piece_img, positions, image_id)[None]
    piece_heads = piece_query.reshape(row_count, head_count, head_size)
    piece_grads = piece_grad.reshape(row_count, head_count, head_size)
    piece_scores = (
        jnp.einsum("thd,shd->hts", piece_heads, own_keys, preferred_element_type=jnp.float32)
        * score_scale
    )
    piece_scores = jnp.where(seen, piece_scores, -1e30)
    piece_probs = jnp.where(seen, jnp.exp(piece_scores - jnp.transpose(every_log)[:, :, None]), 0.0)
    piece_dprobs = jnp.einsum(
        "thd,shd->hts", piece_grads, own_values, preferred_element_type=jnp.float32
    )
    piece_dscores = (piece_probs * (piece_dprobs - jnp.transpose(every_dot)[:, :, None])).astype(
        jnp.bfloat16
    )
    new_keys = jnp.einsum(
        "hts,thd->shd", piece_dscores, piece_heads, preferred_element_type=jnp.float32
    )
    new_values = jnp.einsum(
        "hts,thd->shd",
        piece_probs.astype(jnp.bfloat16),
        piece_grads,
        preferred_element_type=jnp.float32,
    )
    grad_k = (new_keys * score_scale).astype(jnp.bfloat16).reshape(tok_count, model_width)
    grad_v = new_values.astype(jnp.bfloat16).reshape(tok_count, model_width)
    slot_range = jnp.arange(ctx_count * span_len, dtype=jnp.int32)
    selector = ((slot_range[:, None] == slot_index[None, :]) & is_image[None, :]).astype(
        jnp.bfloat16
    )
    contrib = jnp.dot(selector, grad_rows, preferred_element_type=jnp.float32).astype(jnp.bfloat16)
    own_grad = lax.psum_scatter(contrib, "ctx", scatter_dimension=0, tiled=True).astype(jnp.float32)
    grad_first, grad_second = encode_grads(
        own_patches, pre_act, hidden, own_grad.astype(jnp.bfloat16), w_second
    )
    doc_count = lax.axis_size("dp")
    sum_first, sum_second = lax.psum((grad_first, grad_second), ("dp", "ctx"))
    column_count = sum_second.shape[1] // ctx_count
    shard_second = lax.dynamic_slice_in_dim(sum_second, ctx_index * column_count, column_count, 1)
    return (
        layer_rows[None],
        grad_q.reshape(tok_count, model_width)[None],
        grad_k[None],
        grad_v[None],
        sum_first / doc_count,
        shard_second / doc_count,
    )


def solution(mesh):
    placed = (
        P("dp", "ctx", None),
        P("dp", "ctx", None),
        P("dp", "ctx", None),
        P("dp", "ctx", None),
        P("dp", "ctx", None),
        P("dp", "ctx", None, None),
        P("dp", None),
        P(),
        P(),
    )
    return jax.shard_map(
        local,
        mesh=mesh,
        in_specs=placed,
        out_specs=(
            P("dp", "ctx", None),
            P("dp", "ctx", None),
            P("dp", "ctx", None),
            P("dp", "ctx", None),
            P(),
            P(None, "ctx"),
        ),
        check_vma=False,
    )
```

profile of v0, /device:TPU:32, one launch (start us, length us, event | category | flops | bytes accessed | tf_op | source)
XLA Modules:
  0.0 410.0 jit_solution(5079552847384580282)
XLA Ops:
  10.1 2.3 copy.55
  14.8 2.3 copy.63
  20.3 2.4 copy.78
  25.0 2.4 all-gather.10.cloned.1.call-done
  27.4 4.7 %gather_fusion = bf16[256,2048]{1,0:T(8,128)(2,1)} fusion(bf16[256,2048]{1,0:T(8,128)(2,1)} %all-gather.10.cloned.1.call-done, s32[1024]{0:T(1024)S(1)} %pad_clamp_fusion), kind=kCustom, calls=%fused_computation | custom fusion | bytes 2098176 | tf_op jit(solution)/shard_map/gather | solution.py:72
  32.1 14.7 %all-gather.12.cloned.1.call-done = bf16[1,512,2048]{1,2,0:T(8,128)(2,1)} async-done(((bf16[1,256,2048]{1,2,0:T(8,128)(2,1)}), bf16[1,512,2048]{1,2,0:T(8,128)(2,1)}) %all-gather.12.cloned.1.call-update) | async-done | bytes 2097168 | tf_op jit(solution)/shard_map/all_gather | solution.py:74
  46.8 3.4 fusion.2
  50.2 2.6 fusion
  54.7 11.2 %all-gather.14.cloned.1.call-done = bf16[1,512,2048]{2,1,0:T(8,128)(2,1)} async-done(((bf16[1,256,2048]{2,1,0:T(8,128)(2,1)}), bf16[1,512,2048]{2,1,0:T(8,128)(2,1)}) %all-gather.14.cloned.1.call-update) | async-done | bytes 2097168 | tf_op jit(solution)/shard_map/all_gather | solution.py:75
  65.8 3.9 copy.58
  69.8 8.1 %fusion.15 = (f32[256,16]{0,1:T(8,128)}, f32[16,256,128]{1,2,0:T(8,128)}) fusion(bf16[256,16,128]{0,2,1:T(8,128)(2,1)S(1)} %bitcast.71, bf16[512,16,128]{0,2,1:T(8,128)(2,1)} %bitcast.74, f32[16,256,512]{2,1,0:T(8,128)} %copy-done.1, f32[16,256]{1,0:T(8,128)} %copy-done.9, f32[16,256]{1,0:T(8,128)S(1)} %get-tuple-element.42, pred[256,512]{1,0:T(8,128)(4,1)S(1)} %fusion.30), kind=kOutput, calls=%fused_computation.22 | convolution fusion | flops 551022592 | bytes 13811712 | tf_op jit(solution)/shard_map/hts,shd->thd/dot_general | solution.py:91
  77.9 2.9 copy.59
  80.8 8.3 %multiply_convert_fusion.5 = bf16[16,256,128]{1,2,0:T(8,128)(2,1)} fusion(bf16[512,16,128]{0,2,1:T(8,128)(2,1)} %bitcast.78, f32[16,256,512]{2,1,0:T(8,128)} %copy-done.1, f32[16,256]{1,0:T(8,128)} %bitcast.89, f32[16,256]{1,0:T(8,128)S(1)} %copy-done.10, pred[256,512]{1,0:T(8,128)(4,1)S(1)} %fusion.30, bf16[256,16,128]{0,2,1:T(8,128)(2,1)S(1)} %bitcast.72, ...), kind=kOutput, calls=%fused_computation.25 | convolution fusion | flops 1089470464 | bytes 14843904 | tf_op jit(solution)/shard_map/hts,shd->thd/dot_general | solution.py:105
  89.1 2.3 copy.69
  91.4 3.4 all_gather.27
  96.9 2.8 fusion.22
  99.7 3.8 fusion.58
  103.5 6.1 %fusion.26 = f32[16,512,256]{2,1,0:T(8,128)} fusion(bf16[512,16,128]{0,2,1:T(8,128)(2,1)} %bitcast.79, bf16[256,16,128]{2,1,0:T(8,128)(2,1)S(1)} %bitcast.73), kind=kOutput, calls=%fused_computation.36 | convolution fusion | flops 536870912 | bytes 11534336 | tf_op jit(solution)/shard_map/thd,shd->hts/dot_general | solution.py:123
  109.7 11.8 %all-gather.18.cloned.1.call-done = bf16[1,512,2048]{1,2,0:T(8,128)(2,1)} async-done(((bf16[1,256,2048]{1,2,0:T(8,128)(2,1)}), bf16[1,512,2048]{1,2,0:T(8,128)(2,1)}) %all-gather.18.cloned.1.call-update) | async-done | bytes 2097168 | tf_op jit(solution)/shard_map/all_gather | solution.py:115
  121.5 7.9 %multiply_convert_fusion.4 = bf16[16,256,128]{1,2,0:T(8,128)(2,1)} fusion(bf16[512,16,128]{0,2,1:T(8,128)(2,1)} %bitcast.80, f32[16,512,256]{2,1,0:T(8,128)} %fusion.26, f32[16,512]{1,0:T(8,128)S(1)} %bitcast.88, f32[16,512]{1,0:T(8,128)S(1)} %bitcast.86, pred[512,256]{1,0:T(8,128)(4,1)S(1)} %copy-done.8, bf16[512,16,128]{0,2,1:T(8,128)(2,1)} %bitcast.95, ...), kind=kOutput, calls=%fused_computation.24 | convolution fusion | flops 1089470464 | bytes 14876672 | tf_op jit(solution)/shard_map/hts,thd->shd/dot_general | solution.py:134
  131.7 6.4 %fusion.16 = bf16[16,256,128]{1,2,0:T(8,128)(2,1)} fusion(bf16[512,16,128]{0,2,1:T(8,128)(2,1)} %bitcast.96, f32[16,512,256]{2,1,0:T(8,128)} %fusion.26, f32[16,512]{1,0:T(8,128)S(1)} %bitcast.87, pred[512,256]{1,0:T(8,128)(4,1)S(1)} %copy-done.8), kind=kOutput, calls=%fused_computation.27 | convolution fusion | flops 547880960 | bytes 11698176 | tf_op jit(solution)/shard_map/hts,thd->shd/dot_general | solution.py:137
  140.4 3.6 add_convert_fusion
  143.9 254.6 %all-reduce.3.cloned.1.call-done = (f32[32,512]{1,0:T(8,128)}, f32[512,2048]{1,0:T(8,128)}) async-done(((f32[32,512]{1,0:T(8,128)}, f32[512,2048]{1,0:T(8,128)}), (f32[32,512]{1,0:T(8,128)}, f32[512,2048]{1,0:T(8,128)})) %all-reduce.3.cloned.1.call-update) | async-done | bytes 4259856 | tf_op jit(solution)/shard_map/psum | solution.py:155
  400.0 3.2 dynamic-slice_multiply_fusion
  (70 shorter events, 20.6 us)
Async XLA Ops:
  7.2 1.6 copy-start
  7.2 6.0 %copy-start.15 = (s32[1,2]{1,0:T(1,128)S(1)}, s32[1,2]{1,0:T(1,128)}, u32[]{:S(2)}) copy-start(s32[1,2]{1,0:T(1,128)} %param.15) | copy-start | bytes 28
  7.2 6.2 %copy-start.2 = (bf16[1,256,2048]{2,1,0:T(8,128)(2,1)S(1)}, bf16[1,256,2048]{2,1,0:T(8,128)(2,1)}, u32[]{:S(2)}) copy-start(bf16[1,256,2048]{2,1,0:T(8,128)(2,1)} %param.13) | copy-start | bytes 3145732
  7.2 20.2 %all-gather.10.cloned.1.call-start = ((), (), s32[]{:S(2)}) async-start(), calls=%async_computation.1 | async-start | bytes 1572864 | tf_op jit(solution)/shard_map/all_gather | solution.py:71
  10.1 36.7 %all-gather.12.cloned.1.call-start = ((), (), s32[]{:S(2)}) async-start(), calls=%async_computation.3 | async-start | bytes 3145728 | tf_op jit(solution)/shard_map/all_gather | solution.py:74
  12.4 53.4 %all-gather.14.cloned.1.call-start = ((), (), s32[]{:S(2)}) async-start(), calls=%async_computation.4 | async-start | bytes 3145728 | tf_op jit(solution)/shard_map/all_gather | solution.py:75
  13.1 83.8 %reduce-scatter.2.cloned.1.call-start = ((), (), s32[]{:S(2)}) async-start(), calls=%async_computation.2 | async-start | bytes 1572864 | tf_op jit(solution)/shard_map/reduce_scatter | solution.py:150
  13.3 6.9 %copy-start.13 = (pred[256]{0:T(512)(128)(4,1)}, pred[256]{0:T(512)(128)(4,1)S(1)}, u32[]{:S(2)}) copy-start(pred[256]{0:T(512)(128)(4,1)S(1)} %get-tuple-element.39) | copy-start | bytes 772
  14.8 88.8 %all-gather.16.cloned.1.call-start = ((), (), s32[]{:S(2)}) async-start(), calls=%async_computation.5 | async-start | bytes 3145728 | tf_op jit(solution)/shard_map/all_gather | solution.py:114
  17.2 104.4 %all-gather.18.cloned.1.call-start = ((), (), s32[]{:S(2)}) async-start(), calls=%async_computation.6 | async-start | bytes 3145728 | tf_op jit(solution)/shard_map/all_gather | solution.py:115
  18.5 380.0 %all-reduce.3.cloned.1.call-start = ((), (), s32[]{:S(2)}) async-start(), calls=%async_computation.7 | async-start | bytes 8519680 | tf_op jit(solution)/shard_map/psum | solution.py:155
  18.6 5.2 %copy-start.3 = (bf16[1,256,2048]{2,1,0:T(8,128)(2,1)S(1)}, bf16[1,256,2048]{2,1,0:T(8,128)(2,1)}, u32[]{:S(2)}) copy-start(bf16[1,256,2048]{2,1,0:T(8,128)(2,1)} %param.11) | copy-start | bytes 3145732
  50.2 3.2 copy-start.1
  53.4 0.6 copy-start.9
  54.0 15.7 %copy-start.4 = (bf16[1,256,2048]{1,2,0:T(8,128)(2,1)S(1)}, bf16[1,256,2048]{1,2,0:T(8,128)(2,1)}, u32[]{:S(2)}) copy-start(bf16[1,256,2048]{1,2,0:T(8,128)(2,1)} %copy.60) | copy-start | bytes 3145732
  77.9 2.9 copy-start.10
  96.9 6.6 %copy-start.6 = (bf16[32,8,16,128]{3,2,1,0:T(8,128)(2,1)S(1)}, bf16[32,8,16,128]{3,2,1,0:T(8,128)(2,1)}, u32[]{:S(2)}) copy-start(bf16[32,8,16,128]{3,2,1,0:T(8,128)(2,1)} %copy.78) | copy-start | bytes 3145732
  109.7 11.9 %copy-start.7 = (bf16[32,8,16,128]{3,2,1,0:T(8,128)(2,1)S(1)}, bf16[32,8,16,128]{3,2,1,0:T(8,128)(2,1)}, u32[]{:S(2)}) copy-start(bf16[32,8,16,128]{3,2,1,0:T(8,128)(2,1)} %copy.79) | copy-start | bytes 3145732
  109.7 11.9 %copy-start.8 = (pred[512,256]{1,0:T(8,128)(4,1)S(1)}, pred[512,256]{1,0:T(8,128)(4,1)}, u32[]{:S(2)}) copy-start(pred[512,256]{1,0:T(8,128)(4,1)} %fusion.31) | copy-start | bytes 393220
  109.7 11.9 %copy-start.11 = (f32[512,16]{0,1:T(8,128)S(1)}, f32[512,16]{0,1:T(8,128)}, u32[]{:S(2)}) copy-start(f32[512,16]{0,1:T(8,128)} %all_gather.25) | copy-start | bytes 98308
  109.7 11.9 %copy-start.12 = (f32[512,16]{0,1:T(8,128)S(1)}, f32[512,16]{0,1:T(8,128)}, u32[]{:S(2)}) copy-start(f32[512,16]{0,1:T(8,128)} %all_gather.27) | copy-start | bytes 98308
  131.7 8.7 %copy-start.5 = (bf16[256,2048]{1,0:T(8,128)(2,1)S(1)}, bf16[256,2048]{1,0:T(8,128)(2,1)}, u32[]{:S(2)}) copy-start(bf16[256,2048]{1,0:T(8,128)(2,1)} %gather_fusion) | copy-start | bytes 3145732
  131.7 8.7 %copy-start.14 = (pred[256]{0:T(512)(128)(4,1)S(1)}, pred[256]{0:T(512)(128)(4,1)}, u32[]{:S(2)}) copy-start(pred[256]{0:T(512)(128)(4,1)} %copy-done.13) | copy-start | bytes 772
Sparse Core Ops, SparseCore 0:
  10.4 16.9 all-gather.9
  29.8 16.9 all-gather.11
  48.6 17.1 all-gather.13
  68.2 15.1 reduce-scatter.1
  85.1 16.9 all-gather.15
  104.5 16.9 all-gather.17
  128.5 269.9 all-reduce.2
where the time goes:
time: 413 us; the launch traced here: 410 us
  waiting for transfers between devices  295 us (71%)
  matrix products  50.6 us (12%)
  local copies, waits for them, and re-layouts  31.1 us (8%)
  between operations  14.3 us (3%)
  other arithmetic  12.8 us (3%)
  blocking collectives  5.57 us (1%)
    psum x1, waiting for transfers between devices, local(): sum_first, sum_second = lax.psum((grad_first, grad_second), ('dp', 'ctx'))  255 us
    unnamed x41, local copies, waits for them, and re-layouts  19.5 us
    all_gather x1, waiting for transfers between devices, local(): lax.all_gather(key_rows, 'ctx', axis=0, tiled=True)  14.7 us
    all_gather x1, waiting for transfers between devices, local(): piece_grad = lax.all_gather(grad_rows, 'ctx', axis=0, tiled=True)  11.8 us
    all_gather x1, waiting for transfers between devices, local(): lax.all_gather(value_rows, 'ctx', axis=0, tiled=True)  11.2 us
    dot_general x1, matrix products, local(): jnp.einsum('hts,shd->thd', grad_scores, key_heads, preferred_element_type...  8.29 us
  transfers between devices with their start and end apart: 7, of which 5 were waited for; matrix products, arithmetic and copies ran while one was open for 21% of the time, Pallas kernels for 0%

commit v1 on v0

v1 whole, which is shorter than its diff:
```python
import math

import jax
import jax.numpy as jnp
from jax import lax
from jax.experimental import pallas as pl
from jax.experimental.pallas import tpu as pltpu
from jax.sharding import Mesh
from jax.sharding import PartitionSpec as P

HEAD = 128
SPAN = 128
ROWS = 256
HALF = 1024
WIDTH = 2048
SEQ = 512
CH = 512
HEADS = 8
GROUP = 2
SHARDS = 128
VMEM = 56 * 1024 * 1024

F32 = jnp.float32
BF16 = jnp.bfloat16


def dot(a, b, ca, cb):
    return lax.dot_general(a, b, (((ca,), (cb,)), ((), ())), preferred_element_type=F32)


def whole(shape):
    return pl.BlockSpec(shape, lambda *_: (0,) * len(shape))


def call(body, meta, args, in_specs, out_specs, out_shape, grid=(1,), scratch=(), aliases=None):
    return pl.pallas_call(
        body,
        grid_spec=pltpu.PrefetchScalarGridSpec(
            num_scalar_prefetch=1,
            grid=grid,
            in_specs=in_specs,
            out_specs=out_specs,
            scratch_shapes=scratch,
        ),
        out_shape=out_shape,
        input_output_aliases=aliases or {},
        compiler_params=pltpu.CompilerParams(vmem_limit_bytes=VMEM),
    )(meta, *args)


def sigmoid(v):
    return 1.0 / (1.0 + jnp.exp(-v))


def eye(n):
    rows = lax.broadcasted_iota(jnp.int32, (n, n), 0)
    cols = lax.broadcasted_iota(jnp.int32, (n, n), 1)
    return (rows == cols).astype(F32).astype(BF16)


def weight_body(meta, lat, w1, w2, g_own, g_oth, out, hid_t, first):
    step = pl.program_id(0)

    @pl.when(step == 0)
    def _():
        patches = jnp.concatenate([lat[0], lat[1]], axis=1)
        pre = dot(w1[...], patches, 0, 0)
        sig = sigmoid(pre)
        hid_t[...] = (pre * sig).astype(BF16)
        grads = jnp.concatenate([g_own[...], g_oth[...]], axis=0)
        back = dot(w2[...], grads, 1, 1)
        grad_pre = (back * sig * (1.0 + pre * (1.0 - sig))).astype(BF16)
        first[...] = dot(patches, grad_pre, 1, 1)

    half = pl.ds(pl.multiple_of(meta[0] * HALF, HALF), HALF)
    grads = jnp.concatenate([g_own[:, half], g_oth[:, half]], axis=0)
    strip = dot(hid_t[pl.ds(pl.multiple_of(step * 128, 128), 128), :], grads, 1, 0)
    rows = first[pl.ds(pl.multiple_of(step * 8, 8), 8), :]
    for i in range(8):
        for m in range(4):
            line = strip[16 * i : 16 * i + 16]
            out[4 * i + m, 0:16] = line[:, 256 * m : 256 * m + 128]
            out[4 * i + m, 16:32] = line[:, 256 * m + 128 : 256 * m + 256]
            out[4 * i + m, 32:40] = rows[:, 128 * m : 128 * m + 128]


def finish_body(meta, got, second, first):
    for i in range(8):
        for m in range(4):
            j = 4 * i + m
            second[16 * i : 16 * i + 16, 256 * m : 256 * m + 128] = got[j, 0:16].astype(F32) * (1.0 / 128.0)
            second[16 * i : 16 * i + 16, 256 * m + 128 : 256 * m + 256] = got[j, 16:32].astype(F32) * (1.0 / 128.0)
    for m in range(4):
        first[:, 128 * m : 128 * m + 128] = got[m, 32:48].astype(F32)[0:8] * (1.0 / 128.0)


def one_head(q, k, v, g, unit, unit_wide):
    scale = HEAD ** -0.5
    power = scale * math.log2(math.e)
    k_t = dot(unit, k, 1, 1).astype(BF16)
    v_t = dot(unit, v, 1, 1).astype(BF16)
    att, dq, dk, dv = [], [], [], []
    for b in range(2):
        seen = ROWS * (b + 1)
        qb = q[ROWS * b : ROWS * b + ROWS]
        gb = g[ROWS * b : ROWS * b + ROWS]
        scores = dot(k[0:seen], qb, 1, 1)
        key_pos = lax.broadcasted_iota(jnp.int32, (ROWS, ROWS), 0)
        query_pos = lax.broadcasted_iota(jnp.int32, (ROWS, ROWS), 1)
        if b == 0:
            limit = jnp.where(query_pos < SPAN, SPAN - 1, query_pos)
        else:
            limit = jnp.where(query_pos < SPAN, query_pos, ROWS - 1)
        last = jnp.where(key_pos <= limit, scores[seen - ROWS : seen], -1e30)
        scores = last if b == 0 else jnp.concatenate([scores[0:ROWS], last], axis=0)
        top = jnp.max(scores, axis=0, keepdims=True)
        e = jnp.exp2((scores - top) * power)
        p = e * (1.0 / jnp.sum(e, axis=0, keepdims=True))
        pb = p.astype(BF16)
        att_t = dot(v_t[:, 0:seen], pb, 1, 0).astype(BF16)
        att.append(dot(unit_wide, att_t, 1, 1))
        u = p * dot(v[0:seen], gb, 1, 1)
        ds = (u - p * jnp.sum(u, axis=0, keepdims=True)).astype(BF16)
        dq_t = (dot(k_t[:, 0:seen], ds, 1, 0) * scale).astype(BF16)
        dq.append(dot(unit_wide, dq_t, 1, 1).astype(BF16))
        dk.append(dot(ds, qb, 1, 0))
        dv.append(dot(pb, gb, 1, 0))
    dk = [((dk[0] + dk[1][0:ROWS]) * scale).astype(BF16), (dk[1][ROWS:SEQ] * scale).astype(BF16)]
    dv = [(dv[0] + dv[1][0:ROWS]).astype(BF16), dv[1][ROWS:SEQ].astype(BF16)]
    return att, dq, dk, dv


def hidden_of(lat, w1):
    pre = dot(lat, w1, 0, 0)
    return (pre * sigmoid(pre)).astype(BF16)


def attention_body(meta, q_own, q_oth, k_own, k_oth, v_own, v_oth, g_own, g_img, g_txt, text, lat, w1, w2,
                   lay_out, dq_out, dk_out, dv_out, att_send, dq_send, dk_send, dv_send,
                   q, k, v, g, att, dq, dk, dv, hid):
    ctx = meta[0]
    own = pl.multiple_of(ctx * ROWS, ROWS)
    oth = pl.multiple_of(ROWS - ctx * ROWS, ROWS)

    @pl.when(pl.program_id(0) == 0)
    def _():
        hid[...] = hidden_of(lat[0], w1[...])

    for full, a, b in ((q, q_own, q_oth), (k, k_own, k_oth), (v, v_own, v_oth)):
        full[pl.ds(own, ROWS), :] = a[...]
        full[pl.ds(oth, ROWS), :] = b[...]
    g[pl.ds(own, ROWS), :] = g_own[...]
    g[pl.ds(pl.multiple_of(oth + SPAN - ctx * SPAN, SPAN), SPAN), :] = g_img[...]
    g[pl.ds(pl.multiple_of(oth + ctx * SPAN, SPAN), SPAN), :] = g_txt[...]
    unit = eye(HEAD)
    unit_wide = eye(ROWS)
    for h in range(GROUP):
        cols = slice(HEAD * h, HEAD * h + HEAD)
        parts = one_head(q[:, cols], k[:, cols], v[:, cols], g[:, cols], unit, unit_wide)
        for full, halves in zip((att, dq, dk, dv), parts):
            full[0:ROWS, cols] = halves[0].astype(BF16)
            full[ROWS:SEQ, cols] = halves[1].astype(BF16)
    mine = pl.ds(own, ROWS)
    theirs = pl.ds(oth, ROWS)
    for full, keep, send in ((dq, dq_out, dq_send), (dk, dk_out, dk_send), (dv, dv_out, dv_send)):
        keep[...] = full[mine, :]
        send[...] = full[theirs, :]
    att_send[...] = att[theirs, :]
    add_residual(ctx, lay_out, att[mine, :], hid[...], w2[...], text[...])


def add_residual(ctx, lay_out, att, hid, w2, text):
    lay_out[...] = att
    image_rows = pl.ds(pl.multiple_of(ctx * SPAN, SPAN), SPAN)
    text_rows = pl.ds(pl.multiple_of(SPAN - ctx * SPAN, SPAN), SPAN)
    embedding = dot(hid, w2, 1, 0).astype(BF16).astype(F32)
    lay_out[image_rows, :] = (embedding + lay_out[image_rows, :].astype(F32)).astype(BF16)
    lay_out[text_rows, :] = (text.astype(F32) + lay_out[text_rows, :].astype(F32)).astype(BF16)


def merge_body(meta, text, lat, w1, w2, att, dq, dk, dv, lay_in, dq_in, dk_in, dv_in, lay_out, dq_out, dk_out, dv_out):
    add_residual(meta[0], lay_out, att[...], hidden_of(lat[0], w1[...]), w2[...], text[...])
    dq_out[...] = dq[...]
    dk_out[...] = dk[...]
    dv_out[...] = dv[...]


def local(queries, keys, values, residual, grad_out, latents, image_starts, w_first, w_second):
    ctx = lax.axis_index("ctx").astype(jnp.int32)
    meta = ctx[None]
    swap = [(0, 1), (1, 0)]

    def swapped(value):
        return lax.ppermute(value, "ctx", swap)

    def their_half(value):
        return lax.dynamic_slice_in_dim(value[0], (1 - ctx) * HALF, HALF, 1)

    q_rows, k_rows, v_rows, g_rows, r_rows = queries[0], keys[0], values[0], grad_out[0], residual[0]
    lat_own = latents[0, 0]
    lat_oth = swapped(lat_own)
    g_img = swapped(lax.dynamic_slice_in_dim(g_rows, ctx * SPAN, SPAN, 0))
    g_txt = swapped(lax.dynamic_slice(g_rows, ((1 - ctx) * SPAN, (1 - ctx) * HALF), (SPAN, HALF)))
    k_oth = swapped(their_half(keys))
    q_oth = swapped(their_half(queries))
    v_oth = swapped(their_half(values))
    in_order = image_starts[0, 0] == 0
    lat = jnp.where(in_order, jnp.stack([lat_own, lat_oth]), jnp.stack([lat_oth, lat_own]))

    struct = jax.ShapeDtypeStruct
    image_spec = pl.BlockSpec((SPAN, WIDTH), lambda i, m: (m[0], 0))
    payload = call(
        weight_body, meta, (lat, w_first, w_second, g_rows, g_img),
        [whole((2, 32, SPAN)), whole((32, CH)), whole((CH, WIDTH)), image_spec, whole((SPAN, WIDTH))],
        pl.BlockSpec((32, 40, 128), lambda i, m: (i, 0, 0)), struct((SHARDS, 40, 128), F32), grid=(4,),
        scratch=[pltpu.VMEM((CH, 2 * SPAN), BF16), pltpu.VMEM((32, CH), F32)],
    )
    dp = ("z", "y", "x")
    shard = lax.psum_scatter(payload, dp, scatter_dimension=0, tiled=False)

    cols = GROUP * HEAD
    steps = HEADS // GROUP
    own_spec = pl.BlockSpec((ROWS, cols), lambda i, m: (0, m[0] * steps + i))
    oth_spec = pl.BlockSpec((ROWS, cols), lambda i, m: (0, i))
    big = struct((ROWS, WIDTH), BF16)
    small = struct((ROWS, HALF), BF16)
    result = call(
        attention_body, meta,
        (q_rows, q_oth, k_rows, k_oth, v_rows, v_oth, g_rows, g_img, g_txt, r_rows, lat, w_first, w_second),
        [own_spec, oth_spec] * 3
        + [own_spec, pl.BlockSpec((SPAN, cols), lambda i, m: (0, m[0] * steps + i)),
           pl.BlockSpec((SPAN, cols), lambda i, m: (0, i)),
           pl.BlockSpec((SPAN, cols), lambda i, m: (1 - m[0], m[0] * steps + i)),
           whole((2, 32, SPAN)), whole((32, CH)), pl.BlockSpec((CH, cols), lambda i, m: (0, m[0] * steps + i))],
        [own_spec] * 4 + [oth_spec] * 4,
        [big] * 4 + [small] * 4,
        grid=(steps,),
        scratch=[pltpu.VMEM((SEQ, cols), BF16)] * 8 + [pltpu.VMEM((SPAN, CH), BF16)],
    )
    shard, *result = lax.optimization_barrier((shard, *result))
    shard = jnp.pad(shard, ((0, 8), (0, 0))).astype(BF16)
    got = lax.all_gather(shard, dp)
    sum_second, sum_first = call(
        finish_body, meta, (got,), [pl.BlockSpec((32, 48, 128), lambda i, m: (i, 0, 0))],
        [pl.BlockSpec((128, HALF), lambda i, m: (i, 0)), pl.BlockSpec((8, CH), lambda i, m: (i, 0))],
        [struct((CH, HALF), F32), struct((32, CH), F32)], grid=(4,),
    )

    sent = [swapped(value) for value in result[4:]]
    half_spec = pl.BlockSpec((ROWS, HALF), lambda i, m: (0, 1 - m[0]))
    outs = call(
        merge_body, meta, (r_rows, lat, w_first, w_second, *sent, *result[:4]),
        [pl.BlockSpec((SPAN, HALF), lambda i, m: (1 - m[0], 1 - m[0])), whole((2, 32, SPAN)), whole((32, CH)),
         pl.BlockSpec((CH, HALF), lambda i, m: (0, 1 - m[0]))]
        + [whole((ROWS, HALF))] * 4 + [pl.BlockSpec(memory_space=pl.ANY)] * 4,
        [half_spec] * 4, [big] * 4, aliases={9 + i: i for i in range(4)},
    )
    return (*[value[None] for value in outs], sum_first, sum_second)


def solution(mesh):
    axes = Mesh(mesh.devices.reshape(8, 4, 4, 2), ("z", "y", "x", "ctx"))
    dp = ("z", "y", "x")
    rows = P(dp, "ctx", None)
    return jax.shard_map(
        local,
        mesh=axes,
        in_specs=(rows, rows, rows, rows, rows, P(dp, "ctx", None, None), P(dp, None), P(), P()),
        out_specs=(rows, rows, rows, rows, P(), P(None, "ctx")),
        check_vma=False,
    )
```

time: 413 us -> 834 us (2.02)
  waiting for transfers between devices: 295 us -> 775 us
  matrix products: 50.6 us -> 0 us
  Pallas kernels: 0 us -> 30.6 us
  local copies, waits for them, and re-layouts: 31.1 us -> 8.38 us
  other arithmetic: 12.8 us -> 2.11 us
    unnamed x7 -> x3, waiting for transfers between devices: 0.78 us -> 638 us
    psum x1 -> x0, waiting for transfers between devices: 255 us -> none  [local(): sum_first, sum_second = lax.psum((grad_first, grad_second), ('dp', 'ctx'))]
    all_gather x5 -> x1, waiting for transfers between devices: 40.1 us -> 131 us  [local(): got = lax.all_gather(shard, dp)]
    dot_general x11 -> x0, matrix products: 50.6 us -> none  [the longest x1 8.29 us: local(): jnp.einsum('hts,shd->thd', grad_scores, key_heads, preferred_element_type...]
    pallas_call x0 -> x4, Pallas kernels: none -> 30.6 us  [call(): pl.pallas_call(body, grid_spec=pltpu.PrefetchScalarGridSpec(num_scalar_pr...]
    unnamed x41 -> x24, local copies, waits for them, and re-layouts: 19.5 us -> 4.02 us
  transfers between devices with their start and end apart: 7 -> 12, of which waited for: 5 -> 8; matrix products, arithmetic and copies ran while one was open for 21% -> 0% of each run, Pallas kernels for 0% -> 3%
where the time goes in v1:
time: 834 us; the launch traced here: 833 us
  waiting for transfers between devices  775 us (93%)
  Pallas kernels  30.6 us (4%)
  between operations  14.8 us (2%)
  local copies, waits for them, and re-layouts  8.38 us (1%)
    unnamed x3, waiting for transfers between devices  638 us
    all_gather x1, waiting for transfers between devices, local(): got = lax.all_gather(shard, dp)  131 us
    pallas_call x4, Pallas kernels, call(): pl.pallas_call(body, grid_spec=pltpu.PrefetchScalarGridSpec(num_scalar_pr...  30.6 us
  transfers between devices with their start and end apart: 12, of which 8 were waited for; matrix products, arithmetic and copies ran while one was open for 0% of the time, Pallas kernels for 3%

profile of v1, /device:TPU:32, one launch (start us, length us, event | category | flops | bytes accessed | tf_op | source)
XLA Modules:
  0.0 833.4 jit_solution(3727364202972853689)
XLA Ops:
  7.2 1.1 dynamic-slice_bitcast_fusion.3
  9.5 1.0 collective-permute-done
  10.5 1.4 maximum_select_fusion.lat
  11.9 0.8 copy-done.3
  12.7 5.4 shard_map.136
  18.2 1.1 copy-done
  19.3 0.8 dynamic-slice_bitcast_fusion.2
  20.3 0.8 dynamic-slice_bitcast_fusion.1
  21.8 1.0 dynamic-slice_bitcast_fusion.4
  23.2 1.2 collective-permute-done.5.g_txt
  24.4 0.7 copy-done.11
  25.6 17.8 %shard_map.137 = (bf16[256,2048]{1,0:T(8,128)(2,1)}, bf16[256,2048]{1,0:T(8,128)(2,1)}, bf16[256,2048]{1,0:T(8,128)(2,1)}, bf16[256,2048]{1,0:T(8,128)(2,1)}, bf...) custom-call(s32[1]{0:T(128)} %bitcast.meta, ...), custom_call_target="tpu_custom_call" | custom-call | tf_op jit(solution)/shard_map/pallas_call | solution.py:36
  43.4 638.1 %reduce-scatter.5.cloned.1.call-done = f32[1,40,128]{2,1,0:T(8,128)} async-done(((f32[128,40,128]{2,1,0:T(8,128)}), f32[1,40,128]{2,1,0:T(8,128)}) %reduce-scatter.5.cloned.1.call-update) | async-done | bytes 20496
  681.5 0.7 convert.4
  682.3 0.6 pad.5
  683.0 0.5 collective-permute-start.7
  684.0 1.1 collective-permute-done.6.att
  685.1 0.7 collective-permute-done.7.dq
  685.9 0.7 collective-permute-done.8.dk
  686.6 0.7 collective-permute-done.9.dv
  687.4 0.8 copy-done.10
  688.2 3.7 shard_map.138
  691.9 131.0 %all-gather.3.cloned.1.call-done = bf16[6144,128]{1,0:T(8,128)(2,1)} async-done(((bf16[48,128]{1,0:T(8,128)(2,1)}), bf16[6144,128]{1,0:T(8,128)(2,1)}) %all-gather.3.cloned.1.call-update) | async-done | bytes 1572880 | tf_op jit(solution)/shard_map/all_gather | solution.py:242
  822.9 3.7 shard_map.139
  (38 shorter events, 3.2 us)
Async XLA Ops:
  7.2 674.4 %reduce-scatter.5.cloned.1.call-start = ((), (), s32[]{:S(2)}) async-start(), calls=%async_computation.2 | async-start | bytes 2641920
  8.3 3.6 collective-permute-start.1
  8.4 2.1 collective-permute-start
  11.9 0.8 copy-start.3
  18.1 1.2 copy-start
  18.1 2.2 copy-start.1
  18.1 3.4 copy-start.2
  18.1 804.8 %all-gather.3.cloned.1.call-start = ((), (), s32[]{:S(2)}) async-start(), calls=%async_computation.1 | async-start | bytes 1585152 | tf_op jit(solution)/shard_map/all_gather | solution.py:242
  20.1 4.2 collective-permute-start.2
  21.1 3.3 collective-permute-start.3
  21.5 2.8 collective-permute-start.4
  22.7 1.6 collective-permute-start.5
  24.3 0.7 copy-start.11
  24.4 0.9 copy-start.4
  24.4 1.1 copy-start.5
  24.4 1.2 copy-start.6
  682.9 2.2 collective-permute-start.6
  683.0 2.9 collective-permute-start.7
  683.5 3.1 collective-permute-start.8
  683.6 3.8 collective-permute-start.9
  685.1 2.3 copy-start.7
  685.9 1.5 copy-start.8
  686.6 0.8 copy-start.9
  687.4 0.8 copy-start.10
Sparse Core Ops, SparseCore 0:
  18.2 663.2 reduce-scatter.4
  685.5 137.3 all-gather.2

commit v2 on v1

v2 whole, which is shorter than its diff:
```python
import math

import jax
import jax.numpy as jnp
from jax import lax
from jax.experimental import pallas as pl
from jax.experimental.pallas import tpu as pltpu
from jax.sharding import Mesh
from jax.sharding import PartitionSpec as P

HEAD = 128
SPAN = 128
ROWS = 256
HALF = 1024
WIDTH = 2048
SEQ = 512
CH = 512
HEADS = 8
GROUP = 4
VMEM = 56 * 1024 * 1024

F32 = jnp.float32
BF16 = jnp.bfloat16


def dot(a, b, ca, cb):
    return lax.dot_general(a, b, (((ca,), (cb,)), ((), ())), preferred_element_type=F32)


def whole(shape):
    return pl.BlockSpec(shape, lambda *_: (0,) * len(shape))


def call(body, scalars, args, in_specs, out_specs, out_shape, grid=(1,), scratch=(), aliases=None):
    return pl.pallas_call(
        body,
        grid_spec=pltpu.PrefetchScalarGridSpec(
            num_scalar_prefetch=len(scalars),
            grid=grid,
            in_specs=in_specs,
            out_specs=out_specs,
            scratch_shapes=scratch,
        ),
        out_shape=out_shape,
        input_output_aliases=aliases or {},
        compiler_params=pltpu.CompilerParams(vmem_limit_bytes=VMEM),
    )(*scalars, *args)


def sigmoid(v):
    return 1.0 / (1.0 + jnp.exp(-v))


def eye(n):
    rows = lax.broadcasted_iota(jnp.int32, (n, n), 0)
    cols = lax.broadcasted_iota(jnp.int32, (n, n), 1)
    return (rows == cols).astype(F32).astype(BF16)


def pick(starts, lat_own, lat_oth):
    in_order = starts[0] == 0
    one, two = lat_own[...].astype(F32), lat_oth[...].astype(F32)
    return jnp.where(in_order, one, two).astype(BF16), jnp.where(in_order, two, one).astype(BF16)


def weight_body(ctx_ref, starts, lat_own, lat_oth, w1, w2_hbm, g_own, g_oth, out, w2, grads, sems):
    ctx = ctx_ref[0]
    own_rows = pl.ds(pl.multiple_of(ctx * SPAN, SPAN), SPAN)
    oth_rows = pl.ds(pl.multiple_of(SPAN - ctx * SPAN, SPAN), SPAN)
    copies = [
        pltpu.make_async_copy(g_own.at[own_rows, :], grads.at[0:SPAN, :], sems.at[0]),
        pltpu.make_async_copy(g_oth.at[oth_rows, :], grads.at[SPAN:ROWS, :], sems.at[1]),
        pltpu.make_async_copy(w2_hbm, w2, sems.at[2]),
    ]
    for copy in copies:
        copy.start()
    patches = jnp.concatenate(pick(starts, lat_own, lat_oth), axis=1)
    pre = dot(w1[...], patches, 0, 0)
    sig = sigmoid(pre)
    hid_t = (pre * sig).astype(BF16)
    copies[0].wait()
    copies[1].wait()
    half = grads[:, pl.ds(pl.multiple_of(ctx * HALF, HALF), HALF)]
    for j in range(16):
        strip = dot(hid_t[32 * j : 32 * j + 32], half, 1, 0).astype(BF16)
        for t in range(16):
            out[j, t] = strip[16 * (t // 8) : 16 * (t // 8) + 16, 128 * (t % 8) : 128 * (t % 8) + 128]
    copies[2].wait()
    back = dot(w2[...], grads[...], 1, 1)
    grad_pre = (back * sig * (1.0 + pre * (1.0 - sig))).astype(BF16)
    first = dot(patches, grad_pre, 1, 1)
    zeros = jnp.zeros((8, 128), F32)
    for j in range(16):
        tile = first[8 * (j // 4) : 8 * (j // 4) + 8, 128 * (j % 4) : 128 * (j % 4) + 128]
        out[j, 16] = jnp.concatenate([tile, zeros], axis=0).astype(BF16)


def depth_sum_body(got, low, high):
    total = got[0].astype(F32)
    for z in range(1, 8):
        total = total + got[z].astype(F32)
    low[...] = total[0:8].astype(BF16)
    high[...] = total[8:17].astype(BF16)


def finish_body(low, high, second, first):
    for j in range(4):
        for t in range(8):
            cols = slice(128 * t, 128 * t + 128)
            second[32 * j : 32 * j + 16, cols] = low[j, t].astype(F32) * (1.0 / 128.0)
            second[32 * j + 16 : 32 * j + 32, cols] = high[j, t].astype(F32) * (1.0 / 128.0)
        first[:, 128 * j : 128 * j + 128] = high[j, 8].astype(F32)[0:8] * (1.0 / 128.0)


def chain(q, k, v, g, att, dq, dk, dv, cols, b, unit, shared):
    scale = HEAD ** -0.5
    power = scale * math.log2(math.e)
    seen = ROWS * (b + 1)
    rows = slice(ROWS * b, ROWS * b + ROWS)
    qb = q[rows, cols]
    gb = g[rows, cols]
    scores = dot(k[0:seen, cols], qb, 1, 1)
    dp = dot(v[0:seen, cols], gb, 1, 1)
    if b == 1:
        shared["k_t"] = dot(unit, k[:, cols], 1, 1).astype(BF16)
        shared["v_t"] = dot(unit, v[:, cols], 1, 1).astype(BF16)
    yield
    key_pos = lax.broadcasted_iota(jnp.int32, (ROWS, ROWS), 0)
    query_pos = lax.broadcasted_iota(jnp.int32, (ROWS, ROWS), 1)
    if b == 0:
        limit = jnp.where(query_pos < SPAN, SPAN - 1, query_pos)
    else:
        limit = jnp.where(query_pos < SPAN, query_pos, ROWS - 1)
    last = jnp.where(key_pos <= limit, scores[seen - ROWS : seen], -1e30)
    scores = last if b == 0 else jnp.concatenate([scores[0:ROWS], last], axis=0)
    top = jnp.max(scores, axis=0, keepdims=True)
    yield
    e = jnp.exp2((scores - top) * power)
    total = jnp.sum(e, axis=0, keepdims=True)
    yield
    p = e * (1.0 / total)
    pb = p.astype(BF16)
    u = p * dp
    out_dot = jnp.sum(u, axis=0, keepdims=True)
    yield
    ds = (u - p * out_dot).astype(BF16)
    att_t = dot(shared["v_t"][:, 0:seen], pb, 1, 0)
    new_v = dot(pb, gb, 1, 0)
    yield
    dq_t = dot(shared["k_t"][:, 0:seen], ds, 1, 0) * scale
    new_k = dot(ds, qb, 1, 0)
    att[rows, cols] = jnp.transpose(att_t).astype(BF16)
    yield
    dq[rows, cols] = jnp.transpose(dq_t).astype(BF16)
    if b == 1:
        shared["dk"] = new_k[0:ROWS]
        shared["dv"] = new_v[0:ROWS]
    else:
        new_k = new_k + shared["dk"]
        new_v = new_v + shared["dv"]
    dk[rows, cols] = (new_k[seen - ROWS : seen] * scale).astype(BF16)
    dv[rows, cols] = new_v[seen - ROWS : seen].astype(BF16)


def hidden_of(lat, w1):
    pre = dot(lat, w1, 0, 0)
    return (pre * sigmoid(pre)).astype(BF16)


def attention_body(ctx_ref, starts, q_own, q_oth, k_own, k_oth, v_own, v_oth, g_own, g_oth, text, lat_own, lat_oth, w1, w2,
                   lay_out, dq_out, dk_out, dv_out, att_send, dq_send, dk_send, dv_send,
                   q, k, v, g, att, dq, dk, dv, hid):
    ctx = ctx_ref[0]
    own = pl.multiple_of(ctx * ROWS, ROWS)
    oth = pl.multiple_of(ROWS - ctx * ROWS, ROWS)

    @pl.when(pl.program_id(0) == 0)
    def _():
        hid[...] = hidden_of(pick(starts, lat_own, lat_oth)[0], w1[...])

    for full, a, b in ((q, q_own, q_oth), (k, k_own, k_oth), (v, v_own, v_oth), (g, g_own, g_oth)):
        full[pl.ds(own, ROWS), :] = a[...]
        full[pl.ds(oth, ROWS), :] = b[...]
    unit = eye(HEAD)
    waiting = []
    for h in range(GROUP):
        cols = slice(HEAD * h, HEAD * h + HEAD)
        shared = {}
        for b in (1, 0):
            waiting.append(chain(q, k, v, g, att, dq, dk, dv, cols, b, unit, shared))
    running = []
    while waiting or running:
        if waiting:
            running.append(waiting.pop(0))
        running = [item for item in running if next(item, "end") != "end"]
    mine = pl.ds(own, ROWS)
    theirs = pl.ds(oth, ROWS)
    for full, keep, send in ((dq, dq_out, dq_send), (dk, dk_out, dk_send), (dv, dv_out, dv_send)):
        keep[...] = full[mine, :]
        send[...] = full[theirs, :]
    att_send[...] = att[theirs, :]
    add_residual(ctx, lay_out, att[mine, :], hid[...], w2[...], text[...])


def add_residual(ctx, lay_out, att, hid, w2, text):
    lay_out[...] = att
    image_rows = pl.ds(pl.multiple_of(ctx * SPAN, SPAN), SPAN)
    text_rows = pl.ds(pl.multiple_of(SPAN - ctx * SPAN, SPAN), SPAN)
    embedding = dot(hid, w2, 1, 0).astype(BF16).astype(F32)
    lay_out[image_rows, :] = (embedding + lay_out[image_rows, :].astype(F32)).astype(BF16)
    lay_out[text_rows, :] = (text.astype(F32) + lay_out[text_rows, :].astype(F32)).astype(BF16)


def merge_body(ctx_ref, starts, text, lat_own, lat_oth, w1, w2, att, dq, dk, dv, lay_in, dq_in, dk_in, dv_in,
               lay_out, dq_out, dk_out, dv_out, hid):
    @pl.when(pl.program_id(0) == 0)
    def _():
        hid[...] = hidden_of(pick(starts, lat_own, lat_oth)[0], w1[...])

    add_residual(ctx_ref[0], lay_out, att[...], hid[...], w2[...], text[...])
    dq_out[...] = dq[...]
    dk_out[...] = dk[...]
    dv_out[...] = dv[...]


def local(queries, keys, values, residual, grad_out, latents, image_starts, w_first, w_second):
    ctx = lax.axis_index("ctx").astype(jnp.int32)
    scalars = (ctx[None], image_starts.reshape(2))
    swap = [(0, 1), (1, 0)]

    def swapped(value):
        return lax.ppermute(value, "ctx", swap)

    q_rows, k_rows, v_rows, g_rows, r_rows = queries[0], keys[0], values[0], grad_out[0], residual[0]
    lat_own = latents[0, 0]
    lat_oth = swapped(lat_own)
    g_oth, q_oth, k_oth, v_oth = [swapped(value) for value in (g_rows, q_rows, k_rows, v_rows)]

    struct = jax.ShapeDtypeStruct
    anywhere = pl.BlockSpec(memory_space=pl.ANY)
    lat_spec = whole((32, SPAN))
    payload = call(
        weight_body, scalars, (lat_own, lat_oth, w_first, w_second, g_rows, g_oth),
        [lat_spec, lat_spec, whole((32, CH)), anywhere, anywhere, anywhere],
        whole((16, 17, 16, 128)), struct((16, 17, 16, 128), BF16),
        scratch=[pltpu.VMEM((CH, WIDTH), BF16), pltpu.VMEM((ROWS, WIDTH), BF16), pltpu.SemaphoreType.DMA((3,))],
    )
    plane = ("y", "x")
    got = lax.all_to_all(payload, plane, 0, 0, tiled=False)

    cols = GROUP * HEAD
    steps = HEADS // GROUP
    own_spec = pl.BlockSpec((ROWS, cols), lambda i, c, s: (0, c[0] * steps + i))
    send_spec = pl.BlockSpec((ROWS, cols), lambda i, c, s: (0, i))
    big = struct((ROWS, WIDTH), BF16)
    small = struct((ROWS, HALF), BF16)
    result = call(
        attention_body, scalars,
        (q_rows, q_oth, k_rows, k_oth, v_rows, v_oth, g_rows, g_oth, r_rows, lat_own, lat_oth, w_first, w_second),
        [own_spec] * 8
        + [pl.BlockSpec((SPAN, cols), lambda i, c, s: (1 - c[0], c[0] * steps + i)),
           lat_spec, lat_spec, whole((32, CH)), pl.BlockSpec((CH, cols), lambda i, c, s: (0, c[0] * steps + i))],
        [own_spec] * 4 + [send_spec] * 4,
        [big] * 4 + [small] * 4,
        grid=(steps,),
        scratch=[pltpu.VMEM((SEQ, cols), BF16)] * 8 + [pltpu.VMEM((SPAN, CH), BF16)],
    )
    sent = [swapped(value) for value in result[4:]]

    total = got[0].astype(F32)
    for j in range(1, 16):
        total = total + got[j].astype(F32)
    got = lax.all_gather(total.astype(BF16), "z")
    got, *sent = lax.optimization_barrier((got, *sent))
    near = pl.BlockSpec(memory_space=pltpu.VMEM)
    low, high = pl.pallas_call(
        depth_sum_body, in_specs=[near], out_specs=[near, near],
        out_shape=[pltpu.VMEM((8, 16, 128), BF16), pltpu.VMEM((9, 16, 128), BF16)],
    )(pltpu.with_memory_space_constraint(got, pltpu.VMEM))
    low, high = lax.all_gather(low, plane), lax.all_gather(high, plane)
    sum_second, sum_first = call(
        finish_body, (), (low, high),
        [pl.BlockSpec((4, 8, 16, 128), lambda i: (i, 0, 0, 0)), pl.BlockSpec((4, 9, 16, 128), lambda i: (i, 0, 0, 0))],
        [pl.BlockSpec((128, HALF), lambda i: (i, 0)), pl.BlockSpec((8, CH), lambda i: (i, 0))],
        [struct((CH, HALF), F32), struct((32, CH), F32)], grid=(4,),
    )

    parts = 2
    width = HALF // parts
    half_spec = pl.BlockSpec((ROWS, width), lambda i, c, s: (0, (1 - c[0]) * parts + i))
    outs = call(
        merge_body, scalars, (r_rows, lat_own, lat_oth, w_first, w_second, *sent, *result[:4]),
        [pl.BlockSpec((SPAN, width), lambda i, c, s: (1 - c[0], (1 - c[0]) * parts + i)), lat_spec, lat_spec,
         whole((32, CH)), pl.BlockSpec((CH, width), lambda i, c, s: (0, (1 - c[0]) * parts + i))]
        + [pl.BlockSpec((ROWS, width), lambda i, c, s: (0, i))] * 4 + [anywhere] * 4,
        [half_spec] * 4, [big] * 4, grid=(parts,), scratch=[pltpu.VMEM((SPAN, CH), BF16)],
        aliases={11 + i: i for i in range(4)},
    )
    return (*[value[None] for value in outs], sum_first, sum_second)


def solution(mesh):
    axes = Mesh(mesh.devices.reshape(8, 4, 4, 2), ("z", "y", "x", "ctx"))
    dp = ("z", "y", "x")
    rows = P(dp, "ctx", None)
    return jax.shard_map(
        local,
        mesh=axes,
        in_specs=(rows, rows, rows, rows, rows, P(dp, "ctx", None, None), P(dp, None), P(), P()),
        out_specs=(rows, rows, rows, rows, P(), P(None, "ctx")),
        check_vma=False,
    )
```

time: 834 us -> 125 us (0.15)
  waiting for transfers between devices: 775 us -> 10.9 us
  blocking collectives: 0 us -> 77.1 us
  between operations: 14.8 us -> 0.78 us
    unnamed x3 -> x0, waiting for transfers between devices: 638 us -> none
    all_gather x1 -> x0, waiting for transfers between devices: 131 us -> none  [local(): got = lax.all_gather(shard, dp)]
    all_gather x0 -> x3, blocking collectives: none -> 77.1 us  [the longest x2 49 us: local(): low, high = (lax.all_gather(low, plane), lax.all_gather(high, plane))]
  transfers between devices with their start and end apart: 12 -> 10, of which waited for: 8 -> 2; matrix products, arithmetic and copies ran while one was open for 0% -> 0% of each run, Pallas kernels for 3% -> 13%
where the time goes in v2:
time: 125 us
  blocking collectives  77.1 us (62%)
  Pallas kernels  24.5 us (20%)
  waiting for transfers between devices  10.9 us (9%)
  starting transfers between devices  9.36 us (7%)
  local copies, waits for them, and re-layouts  1.94 us (2%)
    all_gather x2, blocking collectives, local(): low, high = (lax.all_gather(low, plane), lax.all_gather(high, plane))  49 us
    all_gather x1, blocking collectives, local(): got = lax.all_gather(total.astype(BF16), 'z')  28.1 us
    pallas_call x4, Pallas kernels, call(): pl.pallas_call(body, grid_spec=pltpu.PrefetchScalarGridSpec(num_scalar_pr...  24.4 us
    all_to_all x1, starting transfers between devices, local(): got = lax.all_to_all(payload, plane, 0, 0, tiled=False)  7.06 us
    all_to_all x1, waiting for transfers between devices, local(): got = lax.all_to_all(payload, plane, 0, 0, tiled=False)  6.11 us
    ppermute x9, waiting for transfers between devices, swapped(): return lax.ppermute(value, 'ctx', swap)  4.79 us
  transfers between devices with their start and end apart: 10, of which 2 were waited for; matrix products, arithmetic and copies ran while one was open for 0% of the time, Pallas kernels for 13%

profile of v2, /device:TPU:32, one launch (start us, length us, event | category | flops | bytes accessed | tf_op | source)
XLA Modules:
  0.0 124.7 jit_solution(15049742174592586434)
XLA Ops:
  0.6 0.1 collective-permute-start.1
  0.7 0.5 collective-permute-start.2
  1.2 0.1 collective-permute-start.3
  1.3 0.4 collective-permute-start.4
  1.7 0.1 collective-permute-start
  1.8 4.8 %collective-permute-done.lat_oth = bf16[32,128]{1,0:T(8,128)(2,1)S(1)} collective-permute-done((bf16[32,128]{1,0:T(8,128)(2,1)}, bf16[32,128]{1,0:T(8,128)(2,1)S(1)}, u32[]{:S(2)}, u32[]{:S(2)}) %collective-permute-start) | collective-permute-done | bytes 8224 | tf_op jit(solution)/shard_map/ppermute | solution.py:232
  6.6 0.6 copy-done.6
  7.2 0.4 copy-done
  7.6 6.3 %shard_map.136 = bf16[16,17,16,128]{3,2,1,0:T(8,128)(2,1)} custom-call(s32[1]{0:T(128)} %bitcast.ctx_ref, s32[2]{0:T(128)} %bitcast.35, bf16[32,128]{1,0:T(8,128)(2,1)} %bitcast.32, bf16[32,128]{1,0:T(8,128)(2,1)} %copy-done.6, bf16[32,512]{1,0:T(8,128)(2,1)} %w1.5, bf16[512,2048]{1,0:T(8,128)(2,1)} %w2.3, bf16[256,2048]{1,0:T(8,128)(2,1)} %bitcast.17, ...), custom_call_target="tpu_custom_call" | custom-call | tf_op jit(solution)/shard_map/pallas_call | solution.py:35
  13.9 7.1 %all-to-all-start = ((bf16[16,17,16,128]{3,2,1,0:T(8,128)(2,1)}), bf16[16,17,16,128]{3,2,1,0:T(8,128)(2,1)S(1)}, u32[]{:S(2)}, u32[]{:S(2)}) async-start(bf16[16,17,16,128]{3,2,1,0:T(8,128)(2,1)} %shard_map.136), calls=%async_computation | async-start | bytes 2228224 | tf_op jit(solution)/shard_map/all_to_all | solution.py:249
  21.0 0.9 copy-done.1
  21.9 10.4 %shard_map.137 = (bf16[256,2048]{1,0:T(8,128)(2,1)}, bf16[256,2048]{1,0:T(8,128)(2,1)}, bf16[256,2048]{1,0:T(8,128)(2,1)}, bf16[256,2048]{1,0:T(8,128)(2,1)}, bf...) custom-call(s32[1]{0:T(128)} %bitcast.ctx_ref, ...), custom_call_target="tpu_custom_call" | custom-call | tf_op jit(solution)/shard_map/pallas_call | solution.py:35
  32.3 0.1 collective-permute-start.5
  32.4 0.5 collective-permute-start.6
  32.9 0.1 collective-permute-start.7
  33.0 0.4 collective-permute-start.8
  33.5 6.1 %all-to-all-done = bf16[16,17,16,128]{3,2,1,0:T(8,128)(2,1)S(1)} async-done(((bf16[16,17,16,128]{3,2,1,0:T(8,128)(2,1)}), bf16[16,17,16,128]{3,2,1,0:T(8,128)(2,1)S(1)}, u32[]{:S(2)}, u32[]{:S(2)}) %all-to-all-start) | async-done | bytes 1114144 | tf_op jit(solution)/shard_map/all_to_all | solution.py:249
  39.6 0.2 add_convert_fusion
  39.7 28.1 %all_gather.16.got = bf16[8,17,16,128]{3,2,1,0:T(8,128)(2,1)S(1)} all-gather(bf16[1,17,16,128]{3,2,1,0:T(8,128)(2,1)S(1)} %add_convert_fusion), channel_id=1, replica_groups=mesh['z'=8,'y'=4,'x'=4,'ctx'=2] {'z'}, dimensions={0}, use_global_device_ids=true | all-gather | bytes 626688 | tf_op jit(solution)/shard_map/all_gather | solution.py:273
  67.9 0.1 shard_map.139
  68.0 23.5 %all-gather = bf16[128,16,128]{2,1,0:T(8,128)(2,1)} all-gather(bf16[8,16,128]{2,1,0:T(8,128)(2,1)S(1)} %get-tuple-element.44), channel_id=2, replica_groups=mesh['z'=8,'y'=4,'x'=4,'ctx'=2] {'y','x'}, dimensions={0}, use_global_device_ids=true | all-gather | bytes 557056 | tf_op jit(solution)/shard_map/all_gather | solution.py:280
  91.4 25.5 %all-gather.1 = bf16[144,16,128]{2,1,0:T(8,128)(2,1)} all-gather(bf16[9,16,128]{2,1,0:T(8,128)(2,1)S(1)} %get-tuple-element.45), channel_id=3, replica_groups=mesh['z'=8,'y'=4,'x'=4,'ctx'=2] {'y','x'}, dimensions={0}, use_global_device_ids=true | all-gather | bytes 626688 | tf_op jit(solution)/shard_map/all_gather | solution.py:280
  116.9 3.6 %shard_map.140 = (f32[512,1024]{1,0:T(8,128)}, f32[32,512]{1,0:T(8,128)}) custom-call(bf16[16,8,16,128]{3,2,1,0:T(8,128)(2,1)} %bitcast.20, bf16[16,9,16,128]{3,2,1,0:T(8,128)(2,1)} %bitcast.19), custom_call_target="tpu_custom_call" | custom-call | tf_op jit(solution)/shard_map/pallas_call | solution.py:35
  120.6 4.1 %shard_map.138 = (bf16[256,2048]{1,0:T(8,128)(2,1)}, bf16[256,2048]{1,0:T(8,128)(2,1)}, bf16[256,2048]{1,0:T(8,128)(2,1)}, bf16[256,2048]{1,0:T(8,128)(2,1)}) custom-call(s32[1]{0:T(128)} %bitcast.ctx_ref, s32[2]{0:T(128)} %bitcast.37, bf16[256,2048]{1,0:T(8,128)(2,1)} %bitcast.15, ...), custom_call_target="tpu_custom_call", output_to_operand_aliasing={{0}: (11, {}), {1}: (12, {}), {2}: (13, {}), {3}: (14, {})} | custom-call | tf_op jit(solution)/shard_map/pallas_call | solution.py:35
  (19 shorter events, 0.0 us)
Async XLA Ops:
  0.6 6.0 %collective-permute-start.1 = (bf16[256,2048]{1,0:T(8,128)(2,1)}, bf16[256,2048]{1,0:T(8,128)(2,1)S(1)}, u32[]{:S(2)}, u32[]{:S(2)}) collective-permute-start(bf16[256,2048]{1,0:T(8,128)(2,1)} %bitcast.16), channel_id=1, source_target_pairs={{0,1},{1,0},{2,3},{3,2},{4,5},{5,4},{6,7},{7,6},{8,9},{9,8},{10,11... | collective-permute-start | bytes 3145736 | tf_op jit(solution)/shard_map/ppermute | solution.py:232
  0.7 20.2 %collective-permute-start.2 = (bf16[256,2048]{1,0:T(8,128)(2,1)}, bf16[256,2048]{1,0:T(8,128)(2,1)S(1)}, u32[]{:S(2)}, u32[]{:S(2)}) collective-permute-start(bf16[256,2048]{1,0:T(8,128)(2,1)} %bitcast.21), channel_id=1, source_target_pairs={{0,1},{1,0},{2,3},{3,2},{4,5},{5,4},{6,7},{7,6},{8,9},{9,8},{10,11... | collective-permute-start | bytes 3145736 | tf_op jit(solution)/shard_map/ppermute | solution.py:232
  1.2 19.7 %collective-permute-start.3 = (bf16[256,2048]{1,0:T(8,128)(2,1)}, bf16[256,2048]{1,0:T(8,128)(2,1)}, u32[]{:S(2)}, u32[]{:S(2)}) collective-permute-start(bf16[256,2048]{1,0:T(8,128)(2,1)} %bitcast.23), channel_id=1, source_target_pairs={{0,1},{1,0},{2,3},{3,2},{4,5},{5,4},{6,7},{7,6},{8,9},{9,8},{10,11... | collective-permute-start | bytes 3145736 | tf_op jit(solution)/shard_map/ppermute | solution.py:232
  1.3 19.6 %collective-permute-start.4 = (bf16[256,2048]{1,0:T(8,128)(2,1)}, bf16[256,2048]{1,0:T(8,128)(2,1)}, u32[]{:S(2)}, u32[]{:S(2)}) collective-permute-start(bf16[256,2048]{1,0:T(8,128)(2,1)} %bitcast.25), channel_id=1, source_target_pairs={{0,1},{1,0},{2,3},{3,2},{4,5},{5,4},{6,7},{7,6},{8,9},{9,8},{10,11... | collective-permute-start | bytes 3145736 | tf_op jit(solution)/shard_map/ppermute | solution.py:232
  1.7 4.9 %collective-permute-start = (bf16[32,128]{1,0:T(8,128)(2,1)}, bf16[32,128]{1,0:T(8,128)(2,1)S(1)}, u32[]{:S(2)}, u32[]{:S(2)}) collective-permute-start(bf16[32,128]{1,0:T(8,128)(2,1)} %bitcast.31), channel_id=1, source_target_pairs={{0,1},{1,0},{2,3},{3,2},{4,5},{5,4},{6,7},{7,6},{8,9},{9,8},{10,11... | collective-permute-start | bytes 24584 | tf_op jit(solution)/shard_map/ppermute | solution.py:232
  6.6 0.6 copy-start.6
  6.6 1.0 copy-start
  13.9 25.7 %all-to-all-start = ((bf16[16,17,16,128]{3,2,1,0:T(8,128)(2,1)}), bf16[16,17,16,128]{3,2,1,0:T(8,128)(2,1)S(1)}, u32[]{:S(2)}, u32[]{:S(2)}) async-start(bf16[16,17,16,128]{3,2,1,0:T(8,128)(2,1)} %shard_map.136), calls=%async_computation | async-start | bytes 2228224 | tf_op jit(solution)/shard_map/all_to_all | solution.py:249
  20.9 1.0 copy-start.1
  32.3 35.5 %collective-permute-start.5 = (bf16[256,1024]{1,0:T(8,128)(2,1)}, bf16[256,1024]{1,0:T(8,128)(2,1)S(1)}, u32[]{:S(2)}, u32[]{:S(2)}) collective-permute-start(bf16[256,1024]{1,0:T(8,128)(2,1)} %get-tuple-element.27), channel_id=1, source_target_pairs={{0,1},{1,0},{2,3},{3,2},{4,5},{5,4},{6,7},{7,6},{8,9},{9,8},{10,11... | collective-permute-start | bytes 1572872 | tf_op jit(solution)/shard_map/ppermute | solution.py:232
  32.4 35.4 %collective-permute-start.6 = (bf16[256,1024]{1,0:T(8,128)(2,1)}, bf16[256,1024]{1,0:T(8,128)(2,1)S(1)}, u32[]{:S(2)}, u32[]{:S(2)}) collective-permute-start(bf16[256,1024]{1,0:T(8,128)(2,1)} %get-tuple-element.28), channel_id=1, source_target_pairs={{0,1},{1,0},{2,3},{3,2},{4,5},{5,4},{6,7},{7,6},{8,9},{9,8},{10,11... | collective-permute-start | bytes 1572872 | tf_op jit(solution)/shard_map/ppermute | solution.py:232
  32.9 34.9 %collective-permute-start.7 = (bf16[256,1024]{1,0:T(8,128)(2,1)}, bf16[256,1024]{1,0:T(8,128)(2,1)S(1)}, u32[]{:S(2)}, u32[]{:S(2)}) collective-permute-start(bf16[256,1024]{1,0:T(8,128)(2,1)} %get-tuple-element.29), channel_id=1, source_target_pairs={{0,1},{1,0},{2,3},{3,2},{4,5},{5,4},{6,7},{7,6},{8,9},{9,8},{10,11... | collective-permute-start | bytes 1572872 | tf_op jit(solution)/shard_map/ppermute | solution.py:232
  33.0 34.8 %collective-permute-start.8 = (bf16[256,1024]{1,0:T(8,128)(2,1)}, bf16[256,1024]{1,0:T(8,128)(2,1)S(1)}, u32[]{:S(2)}, u32[]{:S(2)}) collective-permute-start(bf16[256,1024]{1,0:T(8,128)(2,1)} %get-tuple-element.30), channel_id=1, source_target_pairs={{0,1},{1,0},{2,3},{3,2},{4,5},{5,4},{6,7},{7,6},{8,9},{9,8},{10,11... | collective-permute-start | bytes 1572872 | tf_op jit(solution)/shard_map/ppermute | solution.py:232
  67.8 52.8 %copy-start.2 = (bf16[256,1024]{1,0:T(8,128)(2,1)}, bf16[256,1024]{1,0:T(8,128)(2,1)S(1)}, u32[]{:S(2)}) copy-start(bf16[256,1024]{1,0:T(8,128)(2,1)S(1)} %collective-permute-done.5.att) | copy-start | bytes 1572868
  67.8 52.8 %copy-start.3 = (bf16[256,1024]{1,0:T(8,128)(2,1)}, bf16[256,1024]{1,0:T(8,128)(2,1)S(1)}, u32[]{:S(2)}) copy-start(bf16[256,1024]{1,0:T(8,128)(2,1)S(1)} %collective-permute-done.6.dq) | copy-start | bytes 1572868
  67.9 52.8 %copy-start.4 = (bf16[256,1024]{1,0:T(8,128)(2,1)}, bf16[256,1024]{1,0:T(8,128)(2,1)S(1)}, u32[]{:S(2)}) copy-start(bf16[256,1024]{1,0:T(8,128)(2,1)S(1)} %collective-permute-done.7.dk) | copy-start | bytes 1572868
  67.9 52.7 %copy-start.5 = (bf16[256,1024]{1,0:T(8,128)(2,1)}, bf16[256,1024]{1,0:T(8,128)(2,1)S(1)}, u32[]{:S(2)}) copy-start(bf16[256,1024]{1,0:T(8,128)(2,1)S(1)} %collective-permute-done.8.dv) | copy-start | bytes 1572868

commit v3 on v2

--- a/solution.py
+++ b/solution.py
@@ -69,23 +69,24 @@
     oth_rows = pl.ds(pl.multiple_of(SPAN - ctx * SPAN, SPAN), SPAN)
     copies = [
         pltpu.make_async_copy(g_own.at[own_rows, :], grads.at[0:SPAN, :], sems.at[0]),
-        pltpu.make_async_copy(g_oth.at[oth_rows, :], grads.at[SPAN:ROWS, :], sems.at[1]),
-        pltpu.make_async_copy(w2_hbm, w2, sems.at[2]),
+        pltpu.make_async_copy(w2_hbm, w2, sems.at[1]),
     ]
     for copy in copies:
         copy.start()
+    grads[SPAN:ROWS, :] = g_oth[oth_rows, :]
     patches = jnp.concatenate(pick(starts, lat_own, lat_oth), axis=1)
     pre = dot(w1[...], patches, 0, 0)
     sig = sigmoid(pre)
     hid_t = (pre * sig).astype(BF16)
     copies[0].wait()
+    for n in range(4):
+        half = grads[:, pl.ds(pl.multiple_of(ctx * HALF, HALF) + 256 * n, 256)]
+        strip = dot(hid_t, half, 1, 0).astype(BF16)
+        for j in range(16):
+            for i in range(4):
+                rows = 32 * j + 16 * (i // 2)
+                out[j, 8 * (i // 2) + 2 * n + i % 2] = strip[rows : rows + 16, 128 * (i % 2) : 128 * (i % 2) + 128]
     copies[1].wait()
-    half = grads[:, pl.ds(pl.multiple_of(ctx * HALF, HALF), HALF)]
-    for j in range(16):
-        strip = dot(hid_t[32 * j : 32 * j + 32], half, 1, 0).astype(BF16)
-        for t in range(16):
-            out[j, t] = strip[16 * (t // 8) : 16 * (t // 8) + 16, 128 * (t % 8) : 128 * (t % 8) + 128]
-    copies[2].wait()
     back = dot(w2[...], grads[...], 1, 1)
     grad_pre = (back * sig * (1.0 + pre * (1.0 - sig))).astype(BF16)
     first = dot(patches, grad_pre, 1, 1)
@@ -95,21 +96,50 @@
         out[j, 16] = jnp.concatenate([tile, zeros], axis=0).astype(BF16)
 
 
-def depth_sum_body(got, low, high):
+def plane_sum_body(got, out):
+    total = got[0].astype(F32)
+    for j in range(1, 16):
+        total = total + got[j].astype(F32)
+    total = total.astype(BF16)
+    for z in range(8):
+        out[z, 0:2] = total[2 * z : 2 * z + 2]
+        out[z, 2] = total[16]
+
+
+def depth_sum_body(got, main, first):
     total = got[0].astype(F32)
     for z in range(1, 8):
         total = total + got[z].astype(F32)
-    low[...] = total[0:8].astype(BF16)
-    high[...] = total[8:17].astype(BF16)
-
-
-def finish_body(low, high, second, first):
-    for j in range(4):
-        for t in range(8):
-            cols = slice(128 * t, 128 * t + 128)
-            second[32 * j : 32 * j + 16, cols] = low[j, t].astype(F32) * (1.0 / 128.0)
-            second[32 * j + 16 : 32 * j + 32, cols] = high[j, t].astype(F32) * (1.0 / 128.0)
-        first[:, 128 * j : 128 * j + 128] = high[j, 8].astype(F32)[0:8] * (1.0 / 128.0)
+    total = total.astype(BF16)
+    for z in range(8):
+        main[z] = total[0:2]
+    first[...] = total[2]
+
+
+def join_body(main, first, out):
+    for j in range(16):
+        for z in range(8):
+            out[j, 2 * z : 2 * z + 2] = main[z]
+        out[j, 16] = first[...]
+
+
+def finish_body(got, second, first, second_near, first_near, sems):
+    copies = []
+    for n in range(4):
+        for j in range(4 * n, 4 * n + 4):
+            for t in range(16):
+                rows = 32 * j + 16 * (t // 8)
+                cols = 128 * (t % 8)
+                second_near[rows : rows + 16, cols : cols + 128] = got[j, t].astype(F32) * (1.0 / 128.0)
+            cols = 128 * (j % 4)
+            first_near[8 * n : 8 * n + 8, cols : cols + 128] = got[j, 16].astype(F32)[0:8] * (1.0 / 128.0)
+        part = pl.ds(128 * n, 128)
+        copies.append(pltpu.make_async_copy(second_near.at[part, :], second.at[part, :], sems.at[n]))
+        copies[-1].start()
+    copies.append(pltpu.make_async_copy(first_near, first, sems.at[4]))
+    copies[-1].start()
+    for copy in copies:
+        copy.wait()
 
 
 def chain(q, k, v, g, att, dq, dk, dv, cols, b, unit, shared):
@@ -234,16 +264,29 @@
     q_rows, k_rows, v_rows, g_rows, r_rows = queries[0], keys[0], values[0], grad_out[0], residual[0]
     lat_own = latents[0, 0]
     lat_oth = swapped(lat_own)
-    g_oth, q_oth, k_oth, v_oth = [swapped(value) for value in (g_rows, q_rows, k_rows, v_rows)]
+    g_oth = swapped(g_rows)
+    lat_oth, g_oth, *rows = lax.optimization_barrier((lat_oth, g_oth, q_rows, k_rows, v_rows))
+    q_oth, k_oth, v_oth = [swapped(value) for value in rows]
 
     struct = jax.ShapeDtypeStruct
     anywhere = pl.BlockSpec(memory_space=pl.ANY)
+    near = pl.BlockSpec(memory_space=pltpu.VMEM)
+
+    def place_near(value):
+        return pltpu.with_memory_space_constraint(value, pltpu.VMEM)
+
+    def near_call(body, args, outs):
+        return pl.pallas_call(
+            body, in_specs=[near] * len(args), out_specs=[near] * len(outs),
+            out_shape=[pltpu.VMEM(shape, BF16) for shape in outs],
+        )(*[place_near(value) for value in args])
+
     lat_spec = whole((32, SPAN))
-    payload = call(
-        weight_body, scalars, (lat_own, lat_oth, w_first, w_second, g_rows, g_oth),
-        [lat_spec, lat_spec, whole((32, CH)), anywhere, anywhere, anywhere],
-        whole((16, 17, 16, 128)), struct((16, 17, 16, 128), BF16),
-        scratch=[pltpu.VMEM((CH, WIDTH), BF16), pltpu.VMEM((ROWS, WIDTH), BF16), pltpu.SemaphoreType.DMA((3,))],
+    payload, = call(
+        weight_body, scalars, (lat_own, place_near(lat_oth), w_first, w_second, g_rows, place_near(g_oth)),
+        [lat_spec, near, whole((32, CH)), anywhere, anywhere, near],
+        [near], [pltpu.VMEM((16, 17, 16, 128), BF16)],
+        scratch=[pltpu.VMEM((CH, WIDTH), BF16), pltpu.VMEM((ROWS, WIDTH), BF16), pltpu.SemaphoreType.DMA((2,))],
     )
     plane = ("y", "x")
     got = lax.all_to_all(payload, plane, 0, 0, tiled=False)
@@ -267,23 +310,19 @@
     )
     sent = [swapped(value) for value in result[4:]]
 
-    total = got[0].astype(F32)
-    for j in range(1, 16):
-        total = total + got[j].astype(F32)
-    got = lax.all_gather(total.astype(BF16), "z")
+    part, = near_call(plane_sum_body, (got,), [(8, 3, 16, 128)])
+    got = lax.all_to_all(part, "z", 0, 0, tiled=False)
     got, *sent = lax.optimization_barrier((got, *sent))
-    near = pl.BlockSpec(memory_space=pltpu.VMEM)
-    low, high = pl.pallas_call(
-        depth_sum_body, in_specs=[near], out_specs=[near, near],
-        out_shape=[pltpu.VMEM((8, 16, 128), BF16), pltpu.VMEM((9, 16, 128), BF16)],
-    )(pltpu.with_memory_space_constraint(got, pltpu.VMEM))
-    low, high = lax.all_gather(low, plane), lax.all_gather(high, plane)
-    sum_second, sum_first = call(
-        finish_body, (), (low, high),
-        [pl.BlockSpec((4, 8, 16, 128), lambda i: (i, 0, 0, 0)), pl.BlockSpec((4, 9, 16, 128), lambda i: (i, 0, 0, 0))],
-        [pl.BlockSpec((128, HALF), lambda i: (i, 0)), pl.BlockSpec((8, CH), lambda i: (i, 0))],
-        [struct((CH, HALF), F32), struct((32, CH), F32)], grid=(4,),
-    )
+    main, first = near_call(depth_sum_body, (got,), [(8, 2, 16, 128), (16, 128)])
+    main = lax.all_to_all(main, "z", 0, 0, tiled=False)
+    whole_sums, = near_call(join_body, (main, first), [(16, 17, 16, 128)])
+    got = lax.all_to_all(whole_sums, plane, 0, 0, tiled=False)
+    sum_second, sum_first = pl.pallas_call(
+        finish_body, in_specs=[near], out_specs=[anywhere, anywhere],
+        out_shape=[struct((CH, HALF), F32), struct((32, CH), F32)],
+        scratch_shapes=[pltpu.VMEM((CH, HALF), F32), pltpu.VMEM((32, CH), F32), pltpu.SemaphoreType.DMA((5,))],
+        compiler_params=pltpu.CompilerParams(vmem_limit_bytes=VMEM),
+    )(place_near(got))
 
     parts = 2
     width = HALF // parts

time: 125 us -> 85.4 us (0.68)
  blocking collectives: 77.1 us -> 26.4 us
  waiting for transfers between devices: 10.9 us -> 20.5 us
  starting transfers between devices: 9.36 us -> 13.1 us
  Pallas kernels: 24.5 us -> 22.6 us
    all_gather x3 -> x0, blocking collectives: 77.1 us -> none  [the longest x2 49 us: local(): low, high = (lax.all_gather(low, plane), lax.all_gather(high, plane))]
    all_to_all x0 -> x2, blocking collectives: none -> 26.4 us  [the longest x1 15.6 us: local(): got = lax.all_to_all(part, 'z', 0, 0, tiled=False)]
    all_to_all x0 -> x1, waiting for transfers between devices: none -> 11.2 us  [local(): got = lax.all_to_all(whole_sums, plane, 0, 0, tiled=False)]
    pallas_call x4 -> x3, Pallas kernels: 24.4 us -> 19.9 us  [call(): pl.pallas_call(body, grid_spec=pltpu.PrefetchScalarGridSpec(num_scalar_pr...]
    all_to_all x0 -> x1, starting transfers between devices: none -> 3.7 us  [local(): got = lax.all_to_all(whole_sums, plane, 0, 0, tiled=False)]
    pallas_call x1 -> x4, Pallas kernels: 0.08 us -> 2.7 us  [the longest x1 1.4 us: local(): pl.pallas_call(finish_body, in_specs=[near], out_specs=[anywhere, anywher...]
    ppermute x9, waiting for transfers between devices: 4.79 us -> 2.39 us  [swapped(): return lax.ppermute(value, 'ctx', swap)]
  transfers between devices with their start and end apart: 10 -> 11, of which waited for: 2 -> 3; matrix products, arithmetic and copies ran while one was open for 0% -> 0% of each run, Pallas kernels for 13% -> 24%
where the time goes in v3:
time: 85.4 us; the launch traced here: 84.3 us
  blocking collectives  26.4 us (31%)
  Pallas kernels  22.6 us (26%)
  waiting for transfers between devices  20.5 us (24%)
  starting transfers between devices  13.1 us (15%)
  local copies, waits for them, and re-layouts  0.96 us (1%)
    pallas_call x3, Pallas kernels, call(): pl.pallas_call(body, grid_spec=pltpu.PrefetchScalarGridSpec(num_scalar_pr...  19.9 us
    all_to_all x1, blocking collectives, local(): got = lax.all_to_all(part, 'z', 0, 0, tiled=False)  15.6 us
    all_to_all x1, waiting for transfers between devices, local(): got = lax.all_to_all(whole_sums, plane, 0, 0, tiled=False)  11.2 us
    all_to_all x1, blocking collectives, local(): main = lax.all_to_all(main, 'z', 0, 0, tiled=False)  10.8 us
    all_to_all x1, starting transfers between devices, local(): got = lax.all_to_all(payload, plane, 0, 0, tiled=False)  7.05 us
    all_to_all x1, waiting for transfers between devices, local(): got = lax.all_to_all(payload, plane, 0, 0, tiled=False)  6.93 us
    all_to_all x1, starting transfers between devices, local(): got = lax.all_to_all(whole_sums, plane, 0, 0, tiled=False)  3.7 us
    ppermute x9, waiting for transfers between devices, swapped(): return lax.ppermute(value, 'ctx', swap)  2.39 us
  transfers between devices with their start and end apart: 11, of which 3 were waited for; matrix products, arithmetic and copies ran while one was open for 0% of the time, Pallas kernels for 24%

profile of v3, /device:TPU:32, one launch (start us, length us, event | category | flops | bytes accessed | tf_op | source)
XLA Modules:
  0.0 84.3 jit_solution(10132808921756250674)
XLA Ops:
  0.6 0.1 collective-permute-start.1
  0.7 0.5 collective-permute-start
  1.2 2.4 %collective-permute-done.lat_oth = bf16[32,128]{1,0:T(8,128)(2,1)S(1)} collective-permute-done((bf16[32,128]{1,0:T(8,128)(2,1)}, bf16[32,128]{1,0:T(8,128)(2,1)S(1)}, u32[]{:S(2)}, u32[]{:S(2)}) %collective-permute-start) | collective-permute-done | bytes 8224 | tf_op jit(solution)/shard_map/ppermute | solution.py:262
  3.6 0.0 collective-permute-done.1.g_oth
  3.6 0.2 collective-permute-start.2
  3.8 0.4 collective-permute-start.3
  4.2 0.1 collective-permute-start.4
  4.3 5.3 %shard_map.136 = bf16[16,17,16,128]{3,2,1,0:T(8,128)(2,1)} custom-call(s32[1]{0:T(128)} %bitcast.ctx_ref, s32[2]{0:T(128)} %bitcast.31, bf16[32,128]{1,0:T(8,128)(2,1)} %bitcast.28, bf16[32,128]{1,0:T(8,128)(2,1)S(1)} %collective-permute-done.lat_oth, bf16[32,512]{1,0:T(8,128)(2,1)} %w1.5, bf16[512,2048]{1,0:T(8,128)(2,1)} %w2.3, ...), custom_call_target="tpu_custom_call" | custom-call | tf_op jit(solution)/shard_map/pallas_call | solution.py:35
  9.7 7.0 %all-to-all-start = ((bf16[16,17,16,128]{3,2,1,0:T(8,128)(2,1)}), bf16[16,17,16,128]{3,2,1,0:T(8,128)(2,1)S(1)}, u32[]{:S(2)}, u32[]{:S(2)}) async-start(bf16[16,17,16,128]{3,2,1,0:T(8,128)(2,1)} %shard_map.136), calls=%async_computation | async-start | bytes 2228224 | tf_op jit(solution)/shard_map/all_to_all | solution.py:292
  16.8 0.9 %copy-done.2 = bf16[256,2048]{1,0:T(8,128)(2,1)} copy-done((bf16[256,2048]{1,0:T(8,128)(2,1)}, bf16[256,2048]{1,0:T(8,128)(2,1)S(1)}, u32[]{:S(2)}) %copy-start.2) | copy-done | bytes 1048600
  17.7 10.4 %shard_map.138 = (bf16[256,2048]{1,0:T(8,128)(2,1)}, bf16[256,2048]{1,0:T(8,128)(2,1)}, bf16[256,2048]{1,0:T(8,128)(2,1)}, bf16[256,2048]{1,0:T(8,128)(2,1)}, bf...) custom-call(s32[1]{0:T(128)} %bitcast.ctx_ref, ...), custom_call_target="tpu_custom_call" | custom-call | tf_op jit(solution)/shard_map/pallas_call | solution.py:35
  28.1 0.2 collective-permute-start.5
  28.4 0.4 collective-permute-start.6
  28.7 0.1 collective-permute-start.7
  28.9 0.4 collective-permute-start.8
  29.2 6.9 %all-to-all-done.got = bf16[16,17,16,128]{3,2,1,0:T(8,128)(2,1)S(1)} async-done(((bf16[16,17,16,128]{3,2,1,0:T(8,128)(2,1)}), bf16[16,17,16,128]{3,2,1,0:T(8,128)(2,1)S(1)}, u32[]{:S(2)}, u32[]{:S(2)}) %all-to-all-start) | async-done | bytes 1114144 | tf_op jit(solution)/shard_map/all_to_all | solution.py:292
  36.2 0.1 shard_map.137
  36.3 15.6 %all_to_all.20.got = bf16[8,3,16,128]{3,2,1,0:T(8,128)(2,1)S(1)} all-to-all(bf16[8,3,16,128]{3,2,1,0:T(8,128)(2,1)S(1)} %shard_map.137), channel_id=1, replica_groups=mesh['z'=8,'y'=4,'x'=4,'ctx'=2] {'z'}, dimensions={0} | all-to-all | bytes 196608 | tf_op jit(solution)/shard_map/all_to_all | solution.py:314
  52.0 10.8 %all_to_all.21.main = bf16[8,2,16,128]{3,2,1,0:T(8,128)(2,1)S(1)} all-to-all(bf16[8,2,16,128]{3,2,1,0:T(8,128)(2,1)S(1)} %get-tuple-element.54), channel_id=1, replica_groups=mesh['z'=8,'y'=4,'x'=4,'ctx'=2] {'z'}, dimensions={0} | all-to-all | bytes 131072 | tf_op jit(solution)/shard_map/all_to_all | solution.py:317
  62.8 1.1 %shard_map.141 = bf16[16,17,16,128]{3,2,1,0:T(8,128)(2,1)} custom-call(bf16[8,2,16,128]{3,2,1,0:T(8,128)(2,1)S(1)} %all_to_all.21.main, bf16[16,128]{1,0:T(8,128)(2,1)S(1)} %get-tuple-element.55.first), custom_call_target="tpu_custom_call" | custom-call | tf_op jit(solution)/shard_map/pallas_call | solution.py:279
  63.9 3.7 %all-to-all-start.3 = ((bf16[16,17,16,128]{3,2,1,0:T(8,128)(2,1)}), bf16[16,17,16,128]{3,2,1,0:T(8,128)(2,1)S(1)}, u32[]{:S(2)}, u32[]{:S(2)}) async-start(bf16[16,17,16,128]{3,2,1,0:T(8,128)(2,1)} %shard_map.141), calls=%async_computation.3 | async-start | bytes 2228224 | tf_op jit(solution)/shard_map/all_to_all | solution.py:319
  67.6 4.1 %shard_map.139 = (bf16[256,2048]{1,0:T(8,128)(2,1)}, bf16[256,2048]{1,0:T(8,128)(2,1)}, bf16[256,2048]{1,0:T(8,128)(2,1)}, bf16[256,2048]{1,0:T(8,128)(2,1)}) custom-call(s32[1]{0:T(128)} %bitcast.ctx_ref, s32[2]{0:T(128)} %bitcast.33, bf16[256,2048]{1,0:T(8,128)(2,1)} %bitcast.13, ...), custom_call_target="tpu_custom_call", output_to_operand_aliasing={{0}: (11, {}), {1}: (12, {}), {2}: (13, {}), {3}: (14, {})} | custom-call | tf_op jit(solution)/shard_map/pallas_call | solution.py:35
  71.7 11.2 %all-to-all-done.3.got = bf16[16,17,16,128]{3,2,1,0:T(8,128)(2,1)S(1)} async-done(((bf16[16,17,16,128]{3,2,1,0:T(8,128)(2,1)}), bf16[16,17,16,128]{3,2,1,0:T(8,128)(2,1)S(1)}, u32[]{:S(2)}, u32[]{:S(2)}) %all-to-all-start.3) | async-done | bytes 1114144 | tf_op jit(solution)/shard_map/all_to_all | solution.py:319
  82.9 1.4 %shard_map.142 = (f32[512,1024]{1,0:T(8,128)}, f32[32,512]{1,0:T(8,128)}) custom-call(bf16[16,17,16,128]{3,2,1,0:T(8,128)(2,1)S(1)} %all-to-all-done.3.got), custom_call_target="tpu_custom_call" | custom-call | tf_op jit(solution)/shard_map/pallas_call | solution.py:320
  (19 shorter events, 0.1 us)
Async XLA Ops:
  0.6 3.0 %collective-permute-start.1 = (bf16[256,2048]{1,0:T(8,128)(2,1)}, bf16[256,2048]{1,0:T(8,128)(2,1)S(1)}, u32[]{:S(2)}, u32[]{:S(2)}) collective-permute-start(bf16[256,2048]{1,0:T(8,128)(2,1)} %bitcast.14), channel_id=1, source_target_pairs={{0,1},{1,0},{2,3},{3,2},{4,5},{5,4},{6,7},{7,6},{8,9},{9,8},{10,11... | collective-permute-start | bytes 3145736 | tf_op jit(solution)/shard_map/ppermute | solution.py:262
  0.7 2.9 %collective-permute-start = (bf16[32,128]{1,0:T(8,128)(2,1)}, bf16[32,128]{1,0:T(8,128)(2,1)S(1)}, u32[]{:S(2)}, u32[]{:S(2)}) collective-permute-start(bf16[32,128]{1,0:T(8,128)(2,1)} %bitcast.27), channel_id=1, source_target_pairs={{0,1},{1,0},{2,3},{3,2},{4,5},{5,4},{6,7},{7,6},{8,9},{9,8},{10,11... | collective-permute-start | bytes 24584 | tf_op jit(solution)/shard_map/ppermute | solution.py:262
  3.6 6.1 %copy-start.1 = (bf16[32,128]{1,0:T(8,128)(2,1)}, bf16[32,128]{1,0:T(8,128)(2,1)S(1)}, u32[]{:S(2)}) copy-start(bf16[32,128]{1,0:T(8,128)(2,1)S(1)} %collective-permute-done.lat_oth) | copy-start | bytes 24580
  3.6 6.1 %copy-start = (bf16[256,2048]{1,0:T(8,128)(2,1)}, bf16[256,2048]{1,0:T(8,128)(2,1)S(1)}, u32[]{:S(2)}) copy-start(bf16[256,2048]{1,0:T(8,128)(2,1)S(1)} %collective-permute-done.1.g_oth) | copy-start | bytes 3145732
  3.6 13.1 %collective-permute-start.2 = (bf16[256,2048]{1,0:T(8,128)(2,1)}, bf16[256,2048]{1,0:T(8,128)(2,1)S(1)}, u32[]{:S(2)}, u32[]{:S(2)}) collective-permute-start(bf16[256,2048]{1,0:T(8,128)(2,1)} %bitcast.17), channel_id=1, source_target_pairs={{0,1},{1,0},{2,3},{3,2},{4,5},{5,4},{6,7},{7,6},{8,9},{9,8},{10,11... | collective-permute-start | bytes 3145736 | tf_op jit(solution)/shard_map/ppermute | solution.py:262
  3.8 13.0 %collective-permute-start.3 = (bf16[256,2048]{1,0:T(8,128)(2,1)}, bf16[256,2048]{1,0:T(8,128)(2,1)}, u32[]{:S(2)}, u32[]{:S(2)}) collective-permute-start(bf16[256,2048]{1,0:T(8,128)(2,1)} %bitcast.19), channel_id=1, source_target_pairs={{0,1},{1,0},{2,3},{3,2},{4,5},{5,4},{6,7},{7,6},{8,9},{9,8},{10,11... | collective-permute-start | bytes 3145736 | tf_op jit(solution)/shard_map/ppermute | solution.py:262
  4.2 12.6 %collective-permute-start.4 = (bf16[256,2048]{1,0:T(8,128)(2,1)}, bf16[256,2048]{1,0:T(8,128)(2,1)}, u32[]{:S(2)}, u32[]{:S(2)}) collective-permute-start(bf16[256,2048]{1,0:T(8,128)(2,1)} %bitcast.21), channel_id=1, source_target_pairs={{0,1},{1,0},{2,3},{3,2},{4,5},{5,4},{6,7},{7,6},{8,9},{9,8},{10,11... | collective-permute-start | bytes 3145736 | tf_op jit(solution)/shard_map/ppermute | solution.py:262
  9.7 26.5 %all-to-all-start = ((bf16[16,17,16,128]{3,2,1,0:T(8,128)(2,1)}), bf16[16,17,16,128]{3,2,1,0:T(8,128)(2,1)S(1)}, u32[]{:S(2)}, u32[]{:S(2)}) async-start(bf16[16,17,16,128]{3,2,1,0:T(8,128)(2,1)} %shard_map.136), calls=%async_computation | async-start | bytes 2228224 | tf_op jit(solution)/shard_map/all_to_all | solution.py:292
  16.7 1.0 %copy-start.2 = (bf16[256,2048]{1,0:T(8,128)(2,1)}, bf16[256,2048]{1,0:T(8,128)(2,1)S(1)}, u32[]{:S(2)}) copy-start(bf16[256,2048]{1,0:T(8,128)(2,1)S(1)} %collective-permute-done.2.q_oth) | copy-start | bytes 3145732
  28.1 23.8 %collective-permute-start.5 = (bf16[256,1024]{1,0:T(8,128)(2,1)}, bf16[256,1024]{1,0:T(8,128)(2,1)S(1)}, u32[]{:S(2)}, u32[]{:S(2)}) collective-permute-start(bf16[256,1024]{1,0:T(8,128)(2,1)} %get-tuple-element.37), channel_id=1, source_target_pairs={{0,1},{1,0},{2,3},{3,2},{4,5},{5,4},{6,7},{7,6},{8,9},{9,8},{10,11... | collective-permute-start | bytes 1572872 | tf_op jit(solution)/shard_map/ppermute | solution.py:262
  28.4 23.6 %collective-permute-start.6 = (bf16[256,1024]{1,0:T(8,128)(2,1)}, bf16[256,1024]{1,0:T(8,128)(2,1)S(1)}, u32[]{:S(2)}, u32[]{:S(2)}) collective-permute-start(bf16[256,1024]{1,0:T(8,128)(2,1)} %get-tuple-element.38), channel_id=1, source_target_pairs={{0,1},{1,0},{2,3},{3,2},{4,5},{5,4},{6,7},{7,6},{8,9},{9,8},{10,11... | collective-permute-start | bytes 1572872 | tf_op jit(solution)/shard_map/ppermute | solution.py:262
  28.7 23.3 %collective-permute-start.7 = (bf16[256,1024]{1,0:T(8,128)(2,1)}, bf16[256,1024]{1,0:T(8,128)(2,1)S(1)}, u32[]{:S(2)}, u32[]{:S(2)}) collective-permute-start(bf16[256,1024]{1,0:T(8,128)(2,1)} %get-tuple-element.39), channel_id=1, source_target_pairs={{0,1},{1,0},{2,3},{3,2},{4,5},{5,4},{6,7},{7,6},{8,9},{9,8},{10,11... | collective-permute-start | bytes 1572872 | tf_op jit(solution)/shard_map/ppermute | solution.py:262
  28.9 23.1 %collective-permute-start.8 = (bf16[256,1024]{1,0:T(8,128)(2,1)}, bf16[256,1024]{1,0:T(8,128)(2,1)}, u32[]{:S(2)}, u32[]{:S(2)}) collective-permute-start(bf16[256,1024]{1,0:T(8,128)(2,1)} %get-tuple-element.40), channel_id=1, source_target_pairs={{0,1},{1,0},{2,3},{3,2},{4,5},{5,4},{6,7},{7,6},{8,9},{9,8},{10,11... | collective-permute-start | bytes 1572872 | tf_op jit(solution)/shard_map/ppermute | solution.py:262
  52.0 12.0 %copy-start.3 = (bf16[256,1024]{1,0:T(8,128)(2,1)}, bf16[256,1024]{1,0:T(8,128)(2,1)S(1)}, u32[]{:S(2)}) copy-start(bf16[256,1024]{1,0:T(8,128)(2,1)S(1)} %collective-permute-done.5.att) | copy-start | bytes 1572868
  52.0 12.0 %copy-start.4 = (bf16[256,1024]{1,0:T(8,128)(2,1)}, bf16[256,1024]{1,0:T(8,128)(2,1)S(1)}, u32[]{:S(2)}) copy-start(bf16[256,1024]{1,0:T(8,128)(2,1)S(1)} %collective-permute-done.6.dq) | copy-start | bytes 1572868
  52.0 10.8 %copy-start.5 = (bf16[256,1024]{1,0:T(8,128)(2,1)}, bf16[256,1024]{1,0:T(8,128)(2,1)S(1)}, u32[]{:S(2)}) copy-start(bf16[256,1024]{1,0:T(8,128)(2,1)S(1)} %collective-permute-done.7.dk) | copy-start | bytes 1572868
  63.9 19.0 %all-to-all-start.3 = ((bf16[16,17,16,128]{3,2,1,0:T(8,128)(2,1)}), bf16[16,17,16,128]{3,2,1,0:T(8,128)(2,1)S(1)}, u32[]{:S(2)}, u32[]{:S(2)}) async-start(bf16[16,17,16,128]{3,2,1,0:T(8,128)(2,1)} %shard_map.141), calls=%async_computation.3 | async-start | bytes 2228224 | tf_op jit(solution)/shard_map/all_to_all | solution.py:319

commit v4 on v3

--- a/solution.py
+++ b/solution.py
@@ -63,22 +63,25 @@
     return jnp.where(in_order, one, two).astype(BF16), jnp.where(in_order, two, one).astype(BF16)
 
 
-def weight_body(ctx_ref, starts, lat_own, lat_oth, w1, w2_hbm, g_own, g_oth, out, w2, grads, sems):
+def weight_body(ctx_ref, starts, lat_hbm, lat_oth, w1_hbm, w2_hbm, g_own, g_oth, out, lat_own, w1, w2, grads, sems):
     ctx = ctx_ref[0]
     own_rows = pl.ds(pl.multiple_of(ctx * SPAN, SPAN), SPAN)
     oth_rows = pl.ds(pl.multiple_of(SPAN - ctx * SPAN, SPAN), SPAN)
     copies = [
-        pltpu.make_async_copy(g_own.at[own_rows, :], grads.at[0:SPAN, :], sems.at[0]),
-        pltpu.make_async_copy(w2_hbm, w2, sems.at[1]),
+        pltpu.make_async_copy(source, target, sems.at[i])
+        for i, (source, target) in enumerate((
+            (lat_hbm, lat_own), (w1_hbm, w1), (g_own.at[own_rows, :], grads.at[0:SPAN, :]), (w2_hbm, w2)))
     ]
     for copy in copies:
         copy.start()
     grads[SPAN:ROWS, :] = g_oth[oth_rows, :]
+    copies[0].wait()
+    copies[1].wait()
     patches = jnp.concatenate(pick(starts, lat_own, lat_oth), axis=1)
     pre = dot(w1[...], patches, 0, 0)
     sig = sigmoid(pre)
     hid_t = (pre * sig).astype(BF16)
-    copies[0].wait()
+    copies[2].wait()
     for n in range(4):
         half = grads[:, pl.ds(pl.multiple_of(ctx * HALF, HALF) + 256 * n, 256)]
         strip = dot(hid_t, half, 1, 0).astype(BF16)
@@ -86,7 +89,7 @@
             for i in range(4):
                 rows = 32 * j + 16 * (i // 2)
                 out[j, 8 * (i // 2) + 2 * n + i % 2] = strip[rows : rows + 16, 128 * (i % 2) : 128 * (i % 2) + 128]
-    copies[1].wait()
+    copies[3].wait()
     back = dot(w2[...], grads[...], 1, 1)
     grad_pre = (back * sig * (1.0 + pre * (1.0 - sig))).astype(BF16)
     first = dot(patches, grad_pre, 1, 1)
@@ -241,16 +244,23 @@
     lay_out[text_rows, :] = (text.astype(F32) + lay_out[text_rows, :].astype(F32)).astype(BF16)
 
 
-def merge_body(ctx_ref, starts, text, lat_own, lat_oth, w1, w2, att, dq, dk, dv, lay_in, dq_in, dk_in, dv_in,
-               lay_out, dq_out, dk_out, dv_out, hid):
+def place_body(ctx_ref, *refs):
+    count = (len(refs) - 1) // 3
+    got, out, sems = refs[:count], refs[2 * count : 3 * count], refs[-1]
+    cols = pl.ds(pl.multiple_of(HALF - ctx_ref[0] * HALF, HALF), HALF)
+    copies = [pltpu.make_async_copy(got[i], out[i].at[:, cols], sems.at[i]) for i in range(count)]
+    for copy in copies:
+        copy.start()
+    for copy in copies:
+        copy.wait()
+
+
+def merge_body(ctx_ref, starts, text, lat_own, lat_oth, w1, w2, att, lay_in, lay_out, hid):
     @pl.when(pl.program_id(0) == 0)
     def _():
         hid[...] = hidden_of(pick(starts, lat_own, lat_oth)[0], w1[...])
 
     add_residual(ctx_ref[0], lay_out, att[...], hid[...], w2[...], text[...])
-    dq_out[...] = dq[...]
-    dk_out[...] = dk[...]
-    dv_out[...] = dv[...]
 
 
 def local(queries, keys, values, residual, grad_out, latents, image_starts, w_first, w_second):
@@ -284,9 +294,9 @@
     lat_spec = whole((32, SPAN))
     payload, = call(
         weight_body, scalars, (lat_own, place_near(lat_oth), w_first, w_second, g_rows, place_near(g_oth)),
-        [lat_spec, near, whole((32, CH)), anywhere, anywhere, near],
-        [near], [pltpu.VMEM((16, 17, 16, 128), BF16)],
-        scratch=[pltpu.VMEM((CH, WIDTH), BF16), pltpu.VMEM((ROWS, WIDTH), BF16), pltpu.SemaphoreType.DMA((2,))],
+        [anywhere, near, anywhere, anywhere, anywhere, near], [near], [pltpu.VMEM((16, 17, 16, 128), BF16)],
+        scratch=[pltpu.VMEM((32, SPAN), BF16), pltpu.VMEM((32, CH), BF16), pltpu.VMEM((CH, WIDTH), BF16),
+                 pltpu.VMEM((ROWS, WIDTH), BF16), pltpu.SemaphoreType.DMA((4,))],
     )
     plane = ("y", "x")
     got = lax.all_to_all(payload, plane, 0, 0, tiled=False)
@@ -308,14 +318,28 @@
         grid=(steps,),
         scratch=[pltpu.VMEM((SEQ, cols), BF16)] * 8 + [pltpu.VMEM((SPAN, CH), BF16)],
     )
-    sent = [swapped(value) for value in result[4:]]
+    lay, dq, dk, dv = result[:4]
+    sent_att, sent_dq, sent_dk, sent_dv = [swapped(value) for value in result[4:]]
+
+    def placed(got, into):
+        count = len(got)
+        return call(
+            place_body, scalars[:1], (*got, *into), [anywhere] * (2 * count), [anywhere] * count, [big] * count,
+            scratch=[pltpu.SemaphoreType.DMA((count,))], aliases={1 + count + i: i for i in range(count)},
+        )
 
     part, = near_call(plane_sum_body, (got,), [(8, 3, 16, 128)])
+    part, sent_dq, sent_dk = lax.optimization_barrier((part, sent_dq, sent_dk))
     got = lax.all_to_all(part, "z", 0, 0, tiled=False)
-    got, *sent = lax.optimization_barrier((got, *sent))
+    dq, dk = placed((sent_dq, sent_dk), (dq, dk))
+    got, dq, dk = lax.optimization_barrier((got, dq, dk))
     main, first = near_call(depth_sum_body, (got,), [(8, 2, 16, 128), (16, 128)])
+    main, sent_dv = lax.optimization_barrier((main, sent_dv))
     main = lax.all_to_all(main, "z", 0, 0, tiled=False)
+    dv, = placed((sent_dv,), (dv,))
+    main, dv = lax.optimization_barrier((main, dv))
     whole_sums, = near_call(join_body, (main, first), [(16, 17, 16, 128)])
+    whole_sums, sent_att = lax.optimization_barrier((whole_sums, sent_att))
     got = lax.all_to_all(whole_sums, plane, 0, 0, tiled=False)
     sum_second, sum_first = pl.pallas_call(
         finish_body, in_specs=[near], out_specs=[anywhere, anywhere],
@@ -327,14 +351,14 @@
     parts = 2
     width = HALF // parts
     half_spec = pl.BlockSpec((ROWS, width), lambda i, c, s: (0, (1 - c[0]) * parts + i))
-    outs = call(
-        merge_body, scalars, (r_rows, lat_own, lat_oth, w_first, w_second, *sent, *result[:4]),
+    lay = call(
+        merge_body, scalars, (r_rows, lat_own, lat_oth, w_first, w_second, sent_att, lay),
         [pl.BlockSpec((SPAN, width), lambda i, c, s: (1 - c[0], (1 - c[0]) * parts + i)), lat_spec, lat_spec,
-         whole((32, CH)), pl.BlockSpec((CH, width), lambda i, c, s: (0, (1 - c[0]) * parts + i))]
-        + [pl.BlockSpec((ROWS, width), lambda i, c, s: (0, i))] * 4 + [anywhere] * 4,
-        [half_spec] * 4, [big] * 4, grid=(parts,), scratch=[pltpu.VMEM((SPAN, CH), BF16)],
-        aliases={11 + i: i for i in range(4)},
+         whole((32, CH)), pl.BlockSpec((CH, width), lambda i, c, s: (0, (1 - c[0]) * parts + i)),
+         pl.BlockSpec((ROWS, width), lambda i, c, s: (0, i)), anywhere],
+        half_spec, big, grid=(parts,), scratch=[pltpu.VMEM((SPAN, CH), BF16)], aliases={8: 0},
     )
+    outs = (lay, dq, dk, dv)
     return (*[value[None] for value in outs], sum_first, sum_second)
 
 

time: 85.4 us -> 127 us (1.49)
  Pallas kernels: 22.6 us -> 72.5 us
  blocking collectives: 26.4 us -> 0 us
  starting transfers between devices: 13.1 us -> 28.9 us
  waiting for transfers between devices: 20.5 us -> 22.5 us
    pallas_call x3 -> x5, Pallas kernels: 19.9 us -> 68.5 us  [call(): pl.pallas_call(body, grid_spec=pltpu.PrefetchScalarGridSpec(num_scalar_pr...]
    all_to_all x2 -> x0, blocking collectives: 26.4 us -> none  [the longest x1 15.6 us: local(): got = lax.all_to_all(part, 'z', 0, 0, tiled=False)]
    all_to_all x0 -> x2, starting transfers between devices: none -> 15.8 us  [the longest x1 8.58 us: local(): got = lax.all_to_all(part, 'z', 0, 0, tiled=False)]
    all_to_all x1, waiting for transfers between devices: 11.2 us -> 13.1 us  [local(): got = lax.all_to_all(whole_sums, plane, 0, 0, tiled=False)]
    pallas_call x3, Pallas kernels: 1.31 us -> 2.58 us  [near_call(): pl.pallas_call(body, in_specs=[near] * len(args), out_specs=[near] * len(...]
  transfers between devices with their start and end apart: 11 -> 13, of which waited for: 3 -> 3; matrix products, arithmetic and copies ran while one was open for 0% -> 0% of each run, Pallas kernels for 24% -> 56%
where the time goes in v4:
time: 127 us; the launch traced here: 126 us
  Pallas kernels  72.5 us (57%)
  starting transfers between devices  28.9 us (23%)
  waiting for transfers between devices  22.5 us (18%)
  local copies, waits for them, and re-layouts  1.74 us (1%)
    pallas_call x5, Pallas kernels, call(): pl.pallas_call(body, grid_spec=pltpu.PrefetchScalarGridSpec(num_scalar_pr...  68.5 us
    all_to_all x1, waiting for transfers between devices, local(): got = lax.all_to_all(whole_sums, plane, 0, 0, tiled=False)  13.1 us
    all_to_all x1, starting transfers between devices, local(): got = lax.all_to_all(part, 'z', 0, 0, tiled=False)  8.58 us
    all_to_all x1, starting transfers between devices, local(): main = lax.all_to_all(main, 'z', 0, 0, tiled=False)  7.21 us
    all_to_all x1, starting transfers between devices, local(): got = lax.all_to_all(payload, plane, 0, 0, tiled=False)  7.05 us
    all_to_all x1, waiting for transfers between devices, local(): got = lax.all_to_all(payload, plane, 0, 0, tiled=False)  6.95 us
    all_to_all x1, starting transfers between devices, local(): got = lax.all_to_all(whole_sums, plane, 0, 0, tiled=False)  3.7 us
    pallas_call x3, Pallas kernels, near_call(): pl.pallas_call(body, in_specs=[near] * len(args), out_specs=[near] * len(...  2.58 us
  transfers between devices with their start and end apart: 13, of which 3 were waited for; matrix products, arithmetic and copies ran while one was open for 0% of the time, Pallas kernels for 56%

profile of v4, /device:TPU:32, one launch (start us, length us, event | category | flops | bytes accessed | tf_op | source)
XLA Modules:
  0.0 126.4 jit_solution(13177717870110755585)
XLA Ops:
  0.7 0.5 collective-permute-start
  1.2 2.4 %collective-permute-done.lat_oth = bf16[32,128]{1,0:T(8,128)(2,1)S(1)} collective-permute-done((bf16[32,128]{1,0:T(8,128)(2,1)}, bf16[32,128]{1,0:T(8,128)(2,1)S(1)}, u32[]{:S(2)}, u32[]{:S(2)}) %collective-permute-start) | collective-permute-done | bytes 8224 | tf_op jit(solution)/shard_map/ppermute | solution.py:272
  3.6 0.2 collective-permute-start.2
  3.8 0.4 collective-permute-start.3
  4.3 4.6 %shard_map.136 = bf16[16,17,16,128]{3,2,1,0:T(8,128)(2,1)} custom-call(s32[1]{0:T(128)} %bitcast.ctx_ref, s32[2]{0:T(128)} %bitcast.31, bf16[32,128]{1,0:T(8,128)(2,1)} %bitcast.28, bf16[32,128]{1,0:T(8,128)(2,1)S(1)} %collective-permute-done.lat_oth, bf16[32,512]{1,0:T(8,128)(2,1)} %w1.3, bf16[512,2048]{1,0:T(8,128)(2,1)} %w2.3, ...), custom_call_target="tpu_custom_call" | custom-call | tf_op jit(solution)/shard_map/pallas_call | solution.py:35
  8.9 7.0 %all-to-all-start = ((bf16[16,17,16,128]{3,2,1,0:T(8,128)(2,1)}), bf16[16,17,16,128]{3,2,1,0:T(8,128)(2,1)S(1)}, u32[]{:S(2)}, u32[]{:S(2)}) async-start(bf16[16,17,16,128]{3,2,1,0:T(8,128)(2,1)} %shard_map.136), calls=%async_computation | async-start | bytes 2228224 | tf_op jit(solution)/shard_map/all_to_all | solution.py:302
  16.0 0.9 copy-done.2
  17.0 10.4 %shard_map.138 = (bf16[256,2048]{1,0:T(8,128)(2,1)}, bf16[256,2048]{1,0:T(8,128)(2,1)}, bf16[256,2048]{1,0:T(8,128)(2,1)}, bf16[256,2048]{1,0:T(8,128)(2,1)}, bf...) custom-call(s32[1]{0:T(128)} %bitcast.ctx_ref, ...), custom_call_target="tpu_custom_call" | custom-call | tf_op jit(solution)/shard_map/pallas_call | solution.py:35
  27.4 0.2 collective-permute-start.5
  27.6 0.4 collective-permute-start.6
  28.1 0.4 collective-permute-start.8
  28.5 7.0 %all-to-all-done.got = bf16[16,17,16,128]{3,2,1,0:T(8,128)(2,1)S(1)} async-done(((bf16[16,17,16,128]{3,2,1,0:T(8,128)(2,1)}), bf16[16,17,16,128]{3,2,1,0:T(8,128)(2,1)S(1)}, u32[]{:S(2)}, u32[]{:S(2)}) %all-to-all-start) | async-done | bytes 1114144 | tf_op jit(solution)/shard_map/all_to_all | solution.py:302
  35.4 0.8 shard_map.137
  36.2 8.6 %all-to-all-start.1 = ((bf16[8,3,16,128]{3,2,1,0:T(8,128)(2,1)}), bf16[8,3,16,128]{3,2,1,0:T(8,128)(2,1)S(1)}, u32[]{:S(2)}, u32[]{:S(2)}) async-start(bf16[8,3,16,128]{3,2,1,0:T(8,128)(2,1)} %shard_map.137), calls=%async_computation.1 | async-start | bytes 196608 | tf_op jit(solution)/shard_map/all_to_all | solution.py:333
  44.8 32.9 %shard_map.139 = (bf16[256,2048]{1,0:T(8,128)(2,1)}, bf16[256,2048]{1,0:T(8,128)(2,1)}) custom-call(s32[1]{0:T(128)} %bitcast.ctx_ref, bf16[256,1024]{1,0:T(8,128)(2,1)} %copy-done.5, bf16[256,1024]{1,0:T(8,128)(2,1)} %collective-permute-done.6.refs_1_, bf16[256,2048]{1,0:T(8,128)(2,1)} %get-tuple-element.47.refs_2_, ...), custom_call_target="tpu_custom_call", output_to_operand_aliasing={{0}: (3, {}), {1}: (4, {})} | custom-call | tf_op jit(solution)/shard_map/pallas_call | solution.py:35
  77.7 0.6 shard_map.140
  78.4 7.2 %all-to-all-start.2 = ((bf16[8,2,16,128]{3,2,1,0:T(8,128)(2,1)}), bf16[8,2,16,128]{3,2,1,0:T(8,128)(2,1)S(1)}, u32[]{:S(2)}, u32[]{:S(2)}) async-start(bf16[8,2,16,128]{3,2,1,0:T(8,128)(2,1)} %get-tuple-element.54), calls=%async_computation.2 | async-start | bytes 131072 | tf_op jit(solution)/shard_map/all_to_all | solution.py:338
  85.6 17.0 %shard_map.141 = bf16[256,2048]{1,0:T(8,128)(2,1)} custom-call(s32[1]{0:T(128)} %bitcast.ctx_ref, bf16[256,1024]{1,0:T(8,128)(2,1)} %copy-done.4, bf16[256,2048]{1,0:T(8,128)(2,1)} %get-tuple-element.56.refs_1_), custom_call_target="tpu_custom_call", output_to_operand_aliasing={{}: (2, {})} | custom-call | tf_op jit(solution)/shard_map/pallas_call | solution.py:35
  102.6 1.1 shard_map.142
  103.7 0.8 copy-done.3
  104.5 3.7 %all-to-all-start.3 = ((bf16[16,17,16,128]{3,2,1,0:T(8,128)(2,1)}), bf16[16,17,16,128]{3,2,1,0:T(8,128)(2,1)S(1)}, u32[]{:S(2)}, u32[]{:S(2)}) async-start(bf16[16,17,16,128]{3,2,1,0:T(8,128)(2,1)} %shard_map.142), calls=%async_computation.3 | async-start | bytes 2228224 | tf_op jit(solution)/shard_map/all_to_all | solution.py:343
  108.2 3.6 %shard_map.143 = bf16[256,2048]{1,0:T(8,128)(2,1)} custom-call(s32[1]{0:T(128)} %bitcast.ctx_ref, s32[2]{0:T(128)} %bitcast.33, bf16[256,2048]{1,0:T(8,128)(2,1)} %bitcast.13, bf16[32,128]{1,0:T(8,128)(2,1)} %bitcast.30, bf16[32,128]{1,0:T(8,128)(2,1)} %copy-done.1, bf16[32,512]{1,0:T(8,128)(2,1)} %w1.3, ...), custom_call_target="tpu_custom_call", output_to_operand_aliasing={{}: (8, {})} | custom-call | tf_op jit(solution)/shard_map/pallas_call | solution.py:35
  111.9 13.1 %all-to-all-done.3.got = bf16[16,17,16,128]{3,2,1,0:T(8,128)(2,1)S(1)} async-done(((bf16[16,17,16,128]{3,2,1,0:T(8,128)(2,1)}), bf16[16,17,16,128]{3,2,1,0:T(8,128)(2,1)S(1)}, u32[]{:S(2)}, u32[]{:S(2)}) %all-to-all-start.3) | async-done | bytes 1114144 | tf_op jit(solution)/shard_map/all_to_all | solution.py:343
  125.0 1.4 %shard_map.144 = (f32[512,1024]{1,0:T(8,128)}, f32[32,512]{1,0:T(8,128)}) custom-call(bf16[16,17,16,128]{3,2,1,0:T(8,128)(2,1)S(1)} %all-to-all-done.3.got), custom_call_target="tpu_custom_call" | custom-call | tf_op jit(solution)/shard_map/pallas_call | solution.py:344
  (23 shorter events, 0.4 us)
Async XLA Ops:
  0.6 3.0 %collective-permute-start.1 = (bf16[256,2048]{1,0:T(8,128)(2,1)}, bf16[256,2048]{1,0:T(8,128)(2,1)S(1)}, u32[]{:S(2)}, u32[]{:S(2)}) collective-permute-start(bf16[256,2048]{1,0:T(8,128)(2,1)} %bitcast.14), channel_id=1, source_target_pairs={{0,1},{1,0},{2,3},{3,2},{4,5},{5,4},{6,7},{7,6},{8,9},{9,8},{10,11... | collective-permute-start | bytes 3145736 | tf_op jit(solution)/shard_map/ppermute | solution.py:272
  0.7 2.9 %collective-permute-start = (bf16[32,128]{1,0:T(8,128)(2,1)}, bf16[32,128]{1,0:T(8,128)(2,1)S(1)}, u32[]{:S(2)}, u32[]{:S(2)}) collective-permute-start(bf16[32,128]{1,0:T(8,128)(2,1)} %bitcast.27), channel_id=1, source_target_pairs={{0,1},{1,0},{2,3},{3,2},{4,5},{5,4},{6,7},{7,6},{8,9},{9,8},{10,11... | collective-permute-start | bytes 24584 | tf_op jit(solution)/shard_map/ppermute | solution.py:272
  3.6 5.3 %copy-start.1 = (bf16[32,128]{1,0:T(8,128)(2,1)}, bf16[32,128]{1,0:T(8,128)(2,1)S(1)}, u32[]{:S(2)}) copy-start(bf16[32,128]{1,0:T(8,128)(2,1)S(1)} %collective-permute-done.lat_oth) | copy-start | bytes 24580
  3.6 5.3 %copy-start = (bf16[256,2048]{1,0:T(8,128)(2,1)}, bf16[256,2048]{1,0:T(8,128)(2,1)S(1)}, u32[]{:S(2)}) copy-start(bf16[256,2048]{1,0:T(8,128)(2,1)S(1)} %collective-permute-done.1.g_oth) | copy-start | bytes 3145732
  3.6 12.4 %collective-permute-start.2 = (bf16[256,2048]{1,0:T(8,128)(2,1)}, bf16[256,2048]{1,0:T(8,128)(2,1)S(1)}, u32[]{:S(2)}, u32[]{:S(2)}) collective-permute-start(bf16[256,2048]{1,0:T(8,128)(2,1)} %bitcast.17), channel_id=1, source_target_pairs={{0,1},{1,0},{2,3},{3,2},{4,5},{5,4},{6,7},{7,6},{8,9},{9,8},{10,11... | collective-permute-start | bytes 3145736 | tf_op jit(solution)/shard_map/ppermute | solution.py:272
  3.8 12.3 %collective-permute-start.3 = (bf16[256,2048]{1,0:T(8,128)(2,1)}, bf16[256,2048]{1,0:T(8,128)(2,1)}, u32[]{:S(2)}, u32[]{:S(2)}) collective-permute-start(bf16[256,2048]{1,0:T(8,128)(2,1)} %bitcast.19), channel_id=1, source_target_pairs={{0,1},{1,0},{2,3},{3,2},{4,5},{5,4},{6,7},{7,6},{8,9},{9,8},{10,11... | collective-permute-start | bytes 3145736 | tf_op jit(solution)/shard_map/ppermute | solution.py:272
  4.2 11.8 %collective-permute-start.4 = (bf16[256,2048]{1,0:T(8,128)(2,1)}, bf16[256,2048]{1,0:T(8,128)(2,1)}, u32[]{:S(2)}, u32[]{:S(2)}) collective-permute-start(bf16[256,2048]{1,0:T(8,128)(2,1)} %bitcast.21), channel_id=1, source_target_pairs={{0,1},{1,0},{2,3},{3,2},{4,5},{5,4},{6,7},{7,6},{8,9},{9,8},{10,11... | collective-permute-start | bytes 3145736 | tf_op jit(solution)/shard_map/ppermute | solution.py:272
  8.9 26.5 %all-to-all-start = ((bf16[16,17,16,128]{3,2,1,0:T(8,128)(2,1)}), bf16[16,17,16,128]{3,2,1,0:T(8,128)(2,1)S(1)}, u32[]{:S(2)}, u32[]{:S(2)}) async-start(bf16[16,17,16,128]{3,2,1,0:T(8,128)(2,1)} %shard_map.136), calls=%async_computation | async-start | bytes 2228224 | tf_op jit(solution)/shard_map/all_to_all | solution.py:302
  16.0 1.0 copy-start.2
  27.4 8.9 %collective-permute-start.5 = (bf16[256,1024]{1,0:T(8,128)(2,1)}, bf16[256,1024]{1,0:T(8,128)(2,1)S(1)}, u32[]{:S(2)}, u32[]{:S(2)}) collective-permute-start(bf16[256,1024]{1,0:T(8,128)(2,1)} %get-tuple-element.42), channel_id=1, source_target_pairs={{0,1},{1,0},{2,3},{3,2},{4,5},{5,4},{6,7},{7,6},{8,9},{9,8},{10,11... | collective-permute-start | bytes 1572872 | tf_op jit(solution)/shard_map/ppermute | solution.py:272
  27.6 8.6 %collective-permute-start.6 = (bf16[256,1024]{1,0:T(8,128)(2,1)}, bf16[256,1024]{1,0:T(8,128)(2,1)}, u32[]{:S(2)}, u32[]{:S(2)}) collective-permute-start(bf16[256,1024]{1,0:T(8,128)(2,1)} %get-tuple-element.43), channel_id=1, source_target_pairs={{0,1},{1,0},{2,3},{3,2},{4,5},{5,4},{6,7},{7,6},{8,9},{9,8},{10,11... | collective-permute-start | bytes 1572872 | tf_op jit(solution)/shard_map/ppermute | solution.py:272
  28.0 50.4 %collective-permute-start.7 = (bf16[256,1024]{1,0:T(8,128)(2,1)}, bf16[256,1024]{1,0:T(8,128)(2,1)S(1)}, u32[]{:S(2)}, u32[]{:S(2)}) collective-permute-start(bf16[256,1024]{1,0:T(8,128)(2,1)} %get-tuple-element.53), channel_id=1, source_target_pairs={{0,1},{1,0},{2,3},{3,2},{4,5},{5,4},{6,7},{7,6},{8,9},{9,8},{10,11... | collective-permute-start | bytes 1572872 | tf_op jit(solution)/shard_map/ppermute | solution.py:272
  28.1 75.6 %collective-permute-start.8 = (bf16[256,1024]{1,0:T(8,128)(2,1)}, bf16[256,1024]{1,0:T(8,128)(2,1)S(1)}, u32[]{:S(2)}, u32[]{:S(2)}) collective-permute-start(bf16[256,1024]{1,0:T(8,128)(2,1)} %get-tuple-element.59), channel_id=1, source_target_pairs={{0,1},{1,0},{2,3},{3,2},{4,5},{5,4},{6,7},{7,6},{8,9},{9,8},{10,11... | collective-permute-start | bytes 1572872 | tf_op jit(solution)/shard_map/ppermute | solution.py:272
  36.2 8.6 %copy-start.5 = (bf16[256,1024]{1,0:T(8,128)(2,1)}, bf16[256,1024]{1,0:T(8,128)(2,1)S(1)}, u32[]{:S(2)}) copy-start(bf16[256,1024]{1,0:T(8,128)(2,1)S(1)} %collective-permute-done.5.refs_0_) | copy-start | bytes 1572868
  36.2 41.5 %all-to-all-start.1 = ((bf16[8,3,16,128]{3,2,1,0:T(8,128)(2,1)}), bf16[8,3,16,128]{3,2,1,0:T(8,128)(2,1)S(1)}, u32[]{:S(2)}, u32[]{:S(2)}) async-start(bf16[8,3,16,128]{3,2,1,0:T(8,128)(2,1)} %shard_map.137), calls=%async_computation.1 | async-start | bytes 196608 | tf_op jit(solution)/shard_map/all_to_all | solution.py:333
  78.4 7.2 %copy-start.4 = (bf16[256,1024]{1,0:T(8,128)(2,1)}, bf16[256,1024]{1,0:T(8,128)(2,1)S(1)}, u32[]{:S(2)}) copy-start(bf16[256,1024]{1,0:T(8,128)(2,1)S(1)} %collective-permute-done.7.refs_0_) | copy-start | bytes 1572868
  78.4 24.2 %all-to-all-start.2 = ((bf16[8,2,16,128]{3,2,1,0:T(8,128)(2,1)}), bf16[8,2,16,128]{3,2,1,0:T(8,128)(2,1)S(1)}, u32[]{:S(2)}, u32[]{:S(2)}) async-start(bf16[8,2,16,128]{3,2,1,0:T(8,128)(2,1)} %get-tuple-element.54), calls=%async_computation.2 | async-start | bytes 131072 | tf_op jit(solution)/shard_map/all_to_all | solution.py:338
  103.7 0.8 copy-start.3
  104.5 20.5 %all-to-all-start.3 = ((bf16[16,17,16,128]{3,2,1,0:T(8,128)(2,1)}), bf16[16,17,16,128]{3,2,1,0:T(8,128)(2,1)S(1)}, u32[]{:S(2)}, u32[]{:S(2)}) async-start(bf16[16,17,16,128]{3,2,1,0:T(8,128)(2,1)} %shard_map.142), calls=%async_computation.3 | async-start | bytes 2228224 | tf_op jit(solution)/shard_map/all_to_all | solution.py:343

commit v5 on v4

--- a/solution.py
+++ b/solution.py
@@ -17,6 +17,7 @@
 CH = 512
 HEADS = 8
 GROUP = 4
+GROUPS = 32
 VMEM = 56 * 1024 * 1024
 
 F32 = jnp.float32
@@ -85,60 +86,48 @@
     for n in range(4):
         half = grads[:, pl.ds(pl.multiple_of(ctx * HALF, HALF) + 256 * n, 256)]
         strip = dot(hid_t, half, 1, 0).astype(BF16)
-        for j in range(16):
-            for i in range(4):
-                rows = 32 * j + 16 * (i // 2)
-                out[j, 8 * (i // 2) + 2 * n + i % 2] = strip[rows : rows + 16, 128 * (i % 2) : 128 * (i % 2) + 128]
+        for j in range(GROUPS):
+            for i in range(2):
+                out[j, 2 * n + i] = strip[16 * j : 16 * j + 16, 128 * i : 128 * i + 128]
     copies[3].wait()
     back = dot(w2[...], grads[...], 1, 1)
     grad_pre = (back * sig * (1.0 + pre * (1.0 - sig))).astype(BF16)
     first = dot(patches, grad_pre, 1, 1)
-    zeros = jnp.zeros((8, 128), F32)
-    for j in range(16):
-        tile = first[8 * (j // 4) : 8 * (j // 4) + 8, 128 * (j % 4) : 128 * (j % 4) + 128]
-        out[j, 16] = jnp.concatenate([tile, zeros], axis=0).astype(BF16)
-
-
-def plane_sum_body(got, out):
+    first = first.astype(BF16)
+    for j in range(GROUPS):
+        m = j // 4
+        out[j, 8] = first[16 * (m // 4) : 16 * (m // 4) + 16, 128 * (m % 4) : 128 * (m % 4) + 128]
+
+
+def group_sum_body(got, out):
     total = got[0].astype(F32)
-    for j in range(1, 16):
+    for j in range(1, GROUPS):
         total = total + got[j].astype(F32)
-    total = total.astype(BF16)
-    for z in range(8):
-        out[z, 0:2] = total[2 * z : 2 * z + 2]
-        out[z, 2] = total[16]
-
-
-def depth_sum_body(got, main, first):
-    total = got[0].astype(F32)
-    for z in range(1, 8):
-        total = total + got[z].astype(F32)
-    total = total.astype(BF16)
-    for z in range(8):
-        main[z] = total[0:2]
-    first[...] = total[2]
-
-
-def join_body(main, first, out):
-    for j in range(16):
-        for z in range(8):
-            out[j, 2 * z : 2 * z + 2] = main[z]
-        out[j, 16] = first[...]
+    out[...] = total.astype(BF16)
+
+
+def pair_sum_body(one, two, out):
+    out[...] = (one[...].astype(F32) + two[...].astype(F32)).astype(BF16)
+
+
+def spread_sum_body(one, two, out):
+    total = (one[...].astype(F32) + two[...].astype(F32)).astype(BF16)
+    for j in range(GROUPS):
+        out[j] = total
 
 
 def finish_body(got, second, first, second_near, first_near, sems):
     copies = []
     for n in range(4):
-        for j in range(4 * n, 4 * n + 4):
-            for t in range(16):
-                rows = 32 * j + 16 * (t // 8)
-                cols = 128 * (t % 8)
-                second_near[rows : rows + 16, cols : cols + 128] = got[j, t].astype(F32) * (1.0 / 128.0)
-            cols = 128 * (j % 4)
-            first_near[8 * n : 8 * n + 8, cols : cols + 128] = got[j, 16].astype(F32)[0:8] * (1.0 / 128.0)
+        for j in range(8 * n, 8 * n + 8):
+            for t in range(8):
+                second_near[16 * j : 16 * j + 16, 128 * t : 128 * t + 128] = got[j, t].astype(F32) * (1.0 / 128.0)
         part = pl.ds(128 * n, 128)
         copies.append(pltpu.make_async_copy(second_near.at[part, :], second.at[part, :], sems.at[n]))
         copies[-1].start()
+    for m in range(8):
+        rows, cols = 16 * (m // 4), 128 * (m % 4)
+        first_near[rows : rows + 16, cols : cols + 128] = got[4 * m, 8].astype(F32) * (1.0 / 128.0)
     copies.append(pltpu.make_async_copy(first_near, first, sems.at[4]))
     copies[-1].start()
     for copy in copies:
@@ -211,9 +200,11 @@
     def _():
         hid[...] = hidden_of(pick(starts, lat_own, lat_oth)[0], w1[...])
 
+    step = pl.program_id(0)
+    there = pl.ds(pl.multiple_of(ctx * HALF + step * GROUP * HEAD, GROUP * HEAD), GROUP * HEAD)
     for full, a, b in ((q, q_own, q_oth), (k, k_own, k_oth), (v, v_own, v_oth), (g, g_own, g_oth)):
         full[pl.ds(own, ROWS), :] = a[...]
-        full[pl.ds(oth, ROWS), :] = b[...]
+        full[pl.ds(oth, ROWS), :] = b[:, there]
     unit = eye(HEAD)
     waiting = []
     for h in range(GROUP):
@@ -245,14 +236,11 @@
 
 
 def place_body(ctx_ref, *refs):
-    count = (len(refs) - 1) // 3
-    got, out, sems = refs[:count], refs[2 * count : 3 * count], refs[-1]
-    cols = pl.ds(pl.multiple_of(HALF - ctx_ref[0] * HALF, HALF), HALF)
-    copies = [pltpu.make_async_copy(got[i], out[i].at[:, cols], sems.at[i]) for i in range(count)]
-    for copy in copies:
-        copy.start()
-    for copy in copies:
-        copy.wait()
+    count = len(refs) // 3
+    width = refs[-1].shape[1]
+    cols = pl.ds(pl.multiple_of(pl.program_id(0) * width, width), width)
+    for i in range(count):
+        refs[2 * count + i][...] = refs[i][:, cols]
 
 
 def merge_body(ctx_ref, starts, text, lat_own, lat_oth, w1, w2, att, lay_in, lay_out, hid):
@@ -260,7 +248,9 @@
     def _():
         hid[...] = hidden_of(pick(starts, lat_own, lat_oth)[0], w1[...])
 
-    add_residual(ctx_ref[0], lay_out, att[...], hid[...], w2[...], text[...])
+    width = lay_out.shape[1]
+    cols = pl.ds(pl.multiple_of(pl.program_id(0) * width, width), width)
+    add_residual(ctx_ref[0], lay_out, att[:, cols], hid[...], w2[...], text[...])
 
 
 def local(queries, keys, values, residual, grad_out, latents, image_starts, w_first, w_second):
@@ -294,12 +284,14 @@
     lat_spec = whole((32, SPAN))
     payload, = call(
         weight_body, scalars, (lat_own, place_near(lat_oth), w_first, w_second, g_rows, place_near(g_oth)),
-        [anywhere, near, anywhere, anywhere, anywhere, near], [near], [pltpu.VMEM((16, 17, 16, 128), BF16)],
+        [anywhere, near, anywhere, anywhere, anywhere, near], [near], [pltpu.VMEM((GROUPS, 9, 16, 128), BF16)],
         scratch=[pltpu.VMEM((32, SPAN), BF16), pltpu.VMEM((32, CH), BF16), pltpu.VMEM((CH, WIDTH), BF16),
                  pltpu.VMEM((ROWS, WIDTH), BF16), pltpu.SemaphoreType.DMA((4,))],
     )
-    plane = ("y", "x")
-    got = lax.all_to_all(payload, plane, 0, 0, tiled=False)
+    block = ("zl", "y", "x")
+    payload, v_oth = lax.optimization_barrier((payload, v_oth))
+    q_oth, k_oth, v_oth, g_oth = [place_near(value) for value in (q_oth, k_oth, v_oth, g_oth)]
+    got = lax.all_to_all(payload, block, 0, 0, tiled=False)
 
     cols = GROUP * HEAD
     steps = HEADS // GROUP
@@ -310,7 +302,7 @@
     result = call(
         attention_body, scalars,
         (q_rows, q_oth, k_rows, k_oth, v_rows, v_oth, g_rows, g_oth, r_rows, lat_own, lat_oth, w_first, w_second),
-        [own_spec] * 8
+        [own_spec, near] * 4
         + [pl.BlockSpec((SPAN, cols), lambda i, c, s: (1 - c[0], c[0] * steps + i)),
            lat_spec, lat_spec, whole((32, CH)), pl.BlockSpec((CH, cols), lambda i, c, s: (0, c[0] * steps + i))],
         [own_spec] * 4 + [send_spec] * 4,
@@ -321,26 +313,38 @@
     lay, dq, dk, dv = result[:4]
     sent_att, sent_dq, sent_dk, sent_dv = [swapped(value) for value in result[4:]]
 
+    parts = 2
+    width = HALF // parts
+    half_spec = pl.BlockSpec((ROWS, width), lambda i, c, *_: (0, (1 - c[0]) * parts + i))
+
     def placed(got, into):
         count = len(got)
         return call(
-            place_body, scalars[:1], (*got, *into), [anywhere] * (2 * count), [anywhere] * count, [big] * count,
-            scratch=[pltpu.SemaphoreType.DMA((count,))], aliases={1 + count + i: i for i in range(count)},
+            place_body, scalars[:1], (*map(place_near, got), *into), [near] * count + [anywhere] * count, [half_spec] * count,
+            [big] * count, grid=(parts,), aliases={1 + count + i: i for i in range(count)},
         )
 
-    part, = near_call(plane_sum_body, (got,), [(8, 3, 16, 128)])
-    part, sent_dq, sent_dk = lax.optimization_barrier((part, sent_dq, sent_dk))
-    got = lax.all_to_all(part, "z", 0, 0, tiled=False)
+    def exchanged(value, turn):
+        pairs = []
+        for z in range(4):
+            for core in range(2):
+                other = (z + 2) % 4 if core == turn else z ^ 1
+                pairs.append((2 * z + core, 2 * other + core))
+        return lax.ppermute(value, ("zh", "ctx"), pairs)
+
+    one, = near_call(group_sum_body, (got,), [(9, 16, 128)])
+    one, sent_dq, sent_dk = lax.optimization_barrier((one, sent_dq, sent_dk))
+    two = exchanged(one, 0)
     dq, dk = placed((sent_dq, sent_dk), (dq, dk))
-    got, dq, dk = lax.optimization_barrier((got, dq, dk))
-    main, first = near_call(depth_sum_body, (got,), [(8, 2, 16, 128), (16, 128)])
-    main, sent_dv = lax.optimization_barrier((main, sent_dv))
-    main = lax.all_to_all(main, "z", 0, 0, tiled=False)
+    two, dq, dk = lax.optimization_barrier((two, dq, dk))
+    one, = near_call(pair_sum_body, (one, two), [(9, 16, 128)])
+    one, sent_dv = lax.optimization_barrier((one, sent_dv))
+    two = exchanged(one, 1)
     dv, = placed((sent_dv,), (dv,))
-    main, dv = lax.optimization_barrier((main, dv))
-    whole_sums, = near_call(join_body, (main, first), [(16, 17, 16, 128)])
-    whole_sums, sent_att = lax.optimization_barrier((whole_sums, sent_att))
-    got = lax.all_to_all(whole_sums, plane, 0, 0, tiled=False)
+    two, dv = lax.optimization_barrier((two, dv))
+    sums, = near_call(spread_sum_body, (one, two), [(GROUPS, 9, 16, 128)])
+    sums, sent_att = lax.optimization_barrier((sums, sent_att))
+    got = lax.all_to_all(sums, block, 0, 0, tiled=False)
     sum_second, sum_first = pl.pallas_call(
         finish_body, in_specs=[near], out_specs=[anywhere, anywhere],
         out_shape=[struct((CH, HALF), F32), struct((32, CH), F32)],
@@ -348,14 +352,11 @@
         compiler_params=pltpu.CompilerParams(vmem_limit_bytes=VMEM),
     )(place_near(got))
 
-    parts = 2
-    width = HALF // parts
-    half_spec = pl.BlockSpec((ROWS, width), lambda i, c, s: (0, (1 - c[0]) * parts + i))
     lay = call(
-        merge_body, scalars, (r_rows, lat_own, lat_oth, w_first, w_second, sent_att, lay),
+        merge_body, scalars, (r_rows, lat_own, lat_oth, w_first, w_second, place_near(sent_att), lay),
         [pl.BlockSpec((SPAN, width), lambda i, c, s: (1 - c[0], (1 - c[0]) * parts + i)), lat_spec, lat_spec,
          whole((32, CH)), pl.BlockSpec((CH, width), lambda i, c, s: (0, (1 - c[0]) * parts + i)),
-         pl.BlockSpec((ROWS, width), lambda i, c, s: (0, i)), anywhere],
+         near, anywhere],
         half_spec, big, grid=(parts,), scratch=[pltpu.VMEM((SPAN, CH), BF16)], aliases={8: 0},
     )
     outs = (lay, dq, dk, dv)
@@ -363,8 +364,8 @@
 
 
 def solution(mesh):
-    axes = Mesh(mesh.devices.reshape(8, 4, 4, 2), ("z", "y", "x", "ctx"))
-    dp = ("z", "y", "x")
+    axes = Mesh(mesh.devices.reshape(4, 2, 4, 4, 2), ("zh", "zl", "y", "x", "ctx"))
+    dp = ("zh", "zl", "y", "x")
     rows = P(dp, "ctx", None)
     return jax.shard_map(
         local,

time: 127 us -> 75.2 us (0.59)
  Pallas kernels: 72.5 us -> 22.5 us
  local copies, waits for them, and re-layouts: 1.74 us -> 0.01 us
    pallas_call x5, Pallas kernels: 68.5 us -> 19.9 us  [call(): pl.pallas_call(body, grid_spec=pltpu.PrefetchScalarGridSpec(num_scalar_pr...]
    all_to_all x4 -> x2, starting transfers between devices: 26.5 us -> 16.1 us  [the longest x1 8.58 us: local(): got = lax.all_to_all(payload, block, 0, 0, tiled=False)]
    ppermute x0 -> x2, starting transfers between devices: none -> 9.47 us  [exchanged(): return lax.ppermute(value, ('zh', 'ctx'), pairs)]
    all_to_all x4 -> x2, waiting for transfers between devices: 20.1 us -> 14.8 us  [the longest x1 12.3 us: local(): got = lax.all_to_all(sums, block, 0, 0, tiled=False)]
    ppermute x9, waiting for transfers between devices: 2.39 us -> 6.25 us  [swapped(): return lax.ppermute(value, 'ctx', swap)]
    ppermute x0 -> x2, waiting for transfers between devices: none -> 2.07 us  [exchanged(): return lax.ppermute(value, ('zh', 'ctx'), pairs)]
    unnamed x12 -> x2, local copies, waits for them, and re-layouts: 1.74 us -> 0.01 us
    pallas_call x3, Pallas kernels: 2.58 us -> 1.27 us  [near_call(): pl.pallas_call(body, in_specs=[near] * len(args), out_specs=[near] * len(...]
  transfers between devices with their start and end apart: 13 -> 13, of which waited for: 3 -> 7; matrix products, arithmetic and copies ran while one was open for 0% -> 0% of each run, Pallas kernels for 56% -> 28%
where the time goes in v5:
time: 75.2 us; the launch traced here: 74.4 us
  starting transfers between devices  28 us (37%)
  waiting for transfers between devices  23.1 us (31%)
  Pallas kernels  22.5 us (30%)
    pallas_call x5, Pallas kernels, call(): pl.pallas_call(body, grid_spec=pltpu.PrefetchScalarGridSpec(num_scalar_pr...  19.9 us
    all_to_all x1, waiting for transfers between devices, local(): got = lax.all_to_all(sums, block, 0, 0, tiled=False)  12.3 us
    ppermute x2, starting transfers between devices, exchanged(): return lax.ppermute(value, ('zh', 'ctx'), pairs)  9.47 us
    all_to_all x1, starting transfers between devices, local(): got = lax.all_to_all(payload, block, 0, 0, tiled=False)  8.58 us
    all_to_all x1, starting transfers between devices, local(): got = lax.all_to_all(sums, block, 0, 0, tiled=False)  7.49 us
    ppermute x9, waiting for transfers between devices, swapped(): return lax.ppermute(value, 'ctx', swap)  6.25 us
    all_to_all x1, waiting for transfers between devices, local(): got = lax.all_to_all(payload, block, 0, 0, tiled=False)  2.54 us
    ppermute x9, starting transfers between devices, swapped(): return lax.ppermute(value, 'ctx', swap)  2.42 us
  transfers between devices with their start and end apart: 13, of which 7 were waited for; matrix products, arithmetic and copies ran while one was open for 0% of the time, Pallas kernels for 28%

profile of v5, /device:TPU:32, one launch (start us, length us, event | category | flops | bytes accessed | tf_op | source)
XLA Modules:
  0.0 74.4 jit_solution(14881805498313045590)
XLA Ops:
  0.7 0.5 collective-permute-start
  1.2 2.4 %collective-permute-done.lat_oth = bf16[32,128]{1,0:T(8,128)(2,1)S(1)} collective-permute-done((bf16[32,128]{1,0:T(8,128)(2,1)}, bf16[32,128]{1,0:T(8,128)(2,1)S(1)}, u32[]{:S(2)}, u32[]{:S(2)}) %collective-permute-start) | collective-permute-done | bytes 8224 | tf_op jit(solution)/shard_map/ppermute | solution.py:262
  3.7 4.6 %shard_map.136 = bf16[32,9,16,128]{3,2,1,0:T(8,128)(2,1)} custom-call(s32[1]{0:T(128)} %bitcast.ctx_ref, s32[2]{0:T(128)} %bitcast.31, bf16[32,128]{1,0:T(8,128)(2,1)} %bitcast.28, bf16[32,128]{1,0:T(8,128)(2,1)S(1)} %collective-permute-done.lat_oth, bf16[32,512]{1,0:T(8,128)(2,1)} %w1.3, bf16[512,2048]{1,0:T(8,128)(2,1)} %w2.3, bf16[256,2048]{1,0:T(8,128)(2,1)} %bitcast.15, ...), custom_call_target="tpu_custom_call" | custom-call | tf_op jit(solution)/shard_map/pallas_call | solution.py:36
  8.4 8.6 %all-to-all-start = ((bf16[32,9,16,128]{3,2,1,0:T(8,128)(2,1)}), bf16[32,9,16,128]{3,2,1,0:T(8,128)(2,1)S(1)}, u32[]{:S(2)}, u32[]{:S(2)}) async-start(bf16[32,9,16,128]{3,2,1,0:T(8,128)(2,1)} %shard_map.136), calls=%async_computation | async-start | bytes 2359296 | tf_op jit(solution)/shard_map/all_to_all | solution.py:294
  17.1 0.5 collective-permute-start.4
  17.6 2.4 %collective-permute-done.3.q_oth = bf16[256,2048]{1,0:T(8,128)(2,1)S(1)} collective-permute-done((bf16[256,2048]{1,0:T(8,128)(2,1)}, bf16[256,2048]{1,0:T(8,128)(2,1)S(1)}, u32[]{:S(2)}, u32[]{:S(2)}) %collective-permute-start.3) | collective-permute-done | bytes 1048608 | tf_op jit(solution)/shard_map/ppermute | solution.py:262
  19.9 1.5 %collective-permute-done.4.k_oth = bf16[256,2048]{1,0:T(8,128)(2,1)S(1)} collective-permute-done((bf16[256,2048]{1,0:T(8,128)(2,1)}, bf16[256,2048]{1,0:T(8,128)(2,1)S(1)}, u32[]{:S(2)}, u32[]{:S(2)}) %collective-permute-start.4) | collective-permute-done | bytes 1048608 | tf_op jit(solution)/shard_map/ppermute | solution.py:262
  21.4 10.1 %shard_map.138 = (bf16[256,2048]{1,0:T(8,128)(2,1)}, bf16[256,2048]{1,0:T(8,128)(2,1)}, bf16[256,2048]{1,0:T(8,128)(2,1)}, bf16[256,2048]{1,0:T(8,128)(2,1)}, bf...) custom-call(s32[1]{0:T(128)} %bitcast.ctx_ref, ...), custom_call_target="tpu_custom_call" | custom-call | tf_op jit(solution)/shard_map/pallas_call | solution.py:36
  31.5 0.2 collective-permute-start.5
  31.7 0.4 collective-permute-start.6
  32.2 0.4 collective-permute-start.10
  32.6 2.5 %all-to-all-done.got = bf16[32,9,16,128]{3,2,1,0:T(8,128)(2,1)S(1)} async-done(((bf16[32,9,16,128]{3,2,1,0:T(8,128)(2,1)}), bf16[32,9,16,128]{3,2,1,0:T(8,128)(2,1)S(1)}, u32[]{:S(2)}, u32[]{:S(2)}) %all-to-all-start) | async-done | bytes 1179680 | tf_op jit(solution)/shard_map/all_to_all | solution.py:294
  35.2 0.2 shard_map.137.one
  35.3 6.4 %collective-permute-start.7 = (bf16[9,16,128]{2,1,0:T(8,128)(2,1)S(1)}, bf16[9,16,128]{2,1,0:T(8,128)(2,1)S(1)}, u32[]{:S(2)}, u32[]{:S(2)}) collective-permute-start(bf16[9,16,128]{2,1,0:T(8,128)(2,1)S(1)} %shard_map.137.one), channel_id=1, source_target_pairs={{0,128},{1,65},{64,192},{65,1},{128,0},{129,193},{192,64},{193,129... | collective-permute-start | bytes 110600 | tf_op jit(solution)/shard_map/ppermute | solution.py:333
  41.7 1.0 %shard_map.139 = (bf16[256,2048]{1,0:T(8,128)(2,1)}, bf16[256,2048]{1,0:T(8,128)(2,1)}) custom-call(s32[1]{0:T(128)} %bitcast.ctx_ref, bf16[256,1024]{1,0:T(8,128)(2,1)S(1)} %collective-permute-done.5.refs_0_, bf16[256,1024]{1,0:T(8,128)(2,1)S(1)} %collective-permute-done.6.refs_1_, ...), custom_call_target="tpu_custom_call", output_to_operand_aliasing={{0}: (3, {}), {1}: (4, {})} | custom-call | tf_op jit(solution)/shard_map/pallas_call | solution.py:36
  42.7 0.9 %collective-permute-done.7.two = bf16[9,16,128]{2,1,0:T(8,128)(2,1)S(1)} collective-permute-done((bf16[9,16,128]{2,1,0:T(8,128)(2,1)S(1)}, bf16[9,16,128]{2,1,0:T(8,128)(2,1)S(1)}, u32[]{:S(2)}, u32[]{:S(2)}) %collective-permute-start.7) | collective-permute-done | bytes 36896 | tf_op jit(solution)/shard_map/ppermute | solution.py:333
  43.7 3.1 %collective-permute-start.9 = (bf16[9,16,128]{2,1,0:T(8,128)(2,1)S(1)}, bf16[9,16,128]{2,1,0:T(8,128)(2,1)S(1)}, u32[]{:S(2)}, u32[]{:S(2)}) collective-permute-start(bf16[9,16,128]{2,1,0:T(8,128)(2,1)S(1)} %shard_map.140.one), channel_id=1, source_target_pairs={{0,64},{1,129},{64,0},{65,193},{128,192},{129,1},{192,128},{193,65... | collective-permute-start | bytes 110600 | tf_op jit(solution)/shard_map/ppermute | solution.py:333
  46.8 0.8 %shard_map.141 = bf16[256,2048]{1,0:T(8,128)(2,1)} custom-call(s32[1]{0:T(128)} %bitcast.ctx_ref, bf16[256,1024]{1,0:T(8,128)(2,1)S(1)} %collective-permute-done.8.refs_0_, bf16[256,2048]{1,0:T(8,128)(2,1)} %get-tuple-element.57.refs_1_), custom_call_target="tpu_custom_call", output_to_operand_aliasing={{}: (2, {})} | custom-call | tf_op jit(solution)/shard_map/pallas_call | solution.py:36
  47.6 1.1 %collective-permute-done.9.two = bf16[9,16,128]{2,1,0:T(8,128)(2,1)S(1)} collective-permute-done((bf16[9,16,128]{2,1,0:T(8,128)(2,1)S(1)}, bf16[9,16,128]{2,1,0:T(8,128)(2,1)S(1)}, u32[]{:S(2)}, u32[]{:S(2)}) %collective-permute-start.9) | collective-permute-done | bytes 36896 | tf_op jit(solution)/shard_map/ppermute | solution.py:333
  48.7 1.1 %shard_map.142 = bf16[32,9,16,128]{3,2,1,0:T(8,128)(2,1)} custom-call(bf16[9,16,128]{2,1,0:T(8,128)(2,1)S(1)} %shard_map.140.one, bf16[9,16,128]{2,1,0:T(8,128)(2,1)S(1)} %collective-permute-done.9.two), custom_call_target="tpu_custom_call" | custom-call | tf_op jit(solution)/shard_map/pallas_call | solution.py:279
  49.8 7.5 %all-to-all-start.1 = ((bf16[32,9,16,128]{3,2,1,0:T(8,128)(2,1)}), bf16[32,9,16,128]{3,2,1,0:T(8,128)(2,1)S(1)}, u32[]{:S(2)}, u32[]{:S(2)}) async-start(bf16[32,9,16,128]{3,2,1,0:T(8,128)(2,1)} %shard_map.142), calls=%async_computation.1 | async-start | bytes 2359296 | tf_op jit(solution)/shard_map/all_to_all | solution.py:347
  57.3 3.4 %shard_map.143 = bf16[256,2048]{1,0:T(8,128)(2,1)} custom-call(s32[1]{0:T(128)} %bitcast.ctx_ref, s32[2]{0:T(128)} %bitcast.33, bf16[256,2048]{1,0:T(8,128)(2,1)} %bitcast.13, bf16[32,128]{1,0:T(8,128)(2,1)} %bitcast.30, bf16[32,128]{1,0:T(8,128)(2,1)} %copy-done, bf16[32,512]{1,0:T(8,128)(2,1)} %w1.3, ...), custom_call_target="tpu_custom_call", output_to_operand_aliasing={{}: (8, {})} | custom-call | tf_op jit(solution)/shard_map/pallas_call | solution.py:36
  60.7 12.3 %all-to-all-done.1.got = bf16[32,9,16,128]{3,2,1,0:T(8,128)(2,1)S(1)} async-done(((bf16[32,9,16,128]{3,2,1,0:T(8,128)(2,1)}), bf16[32,9,16,128]{3,2,1,0:T(8,128)(2,1)S(1)}, u32[]{:S(2)}, u32[]{:S(2)}) %all-to-all-start.1) | async-done | bytes 1179680 | tf_op jit(solution)/shard_map/all_to_all | solution.py:347
  73.0 1.4 %shard_map.144 = (f32[512,1024]{1,0:T(8,128)}, f32[32,512]{1,0:T(8,128)}) custom-call(bf16[32,9,16,128]{3,2,1,0:T(8,128)(2,1)S(1)} %all-to-all-done.1.got), custom_call_target="tpu_custom_call" | custom-call | tf_op jit(solution)/shard_map/pallas_call | solution.py:348
  (13 shorter events, 0.5 us)
Async XLA Ops:
  0.6 3.0 %collective-permute-start.1 = (bf16[256,2048]{1,0:T(8,128)(2,1)}, bf16[256,2048]{1,0:T(8,128)(2,1)S(1)}, u32[]{:S(2)}, u32[]{:S(2)}) collective-permute-start(bf16[256,2048]{1,0:T(8,128)(2,1)} %bitcast.14), channel_id=1, source_target_pairs={{0,1},{1,0},{2,3},{3,2},{4,5},{5,4},{6,7},{7,6},{8,9},{9,8},{10,11... | collective-permute-start | bytes 3145736 | tf_op jit(solution)/shard_map/ppermute | solution.py:262
  0.7 2.9 %collective-permute-start = (bf16[32,128]{1,0:T(8,128)(2,1)}, bf16[32,128]{1,0:T(8,128)(2,1)S(1)}, u32[]{:S(2)}, u32[]{:S(2)}) collective-permute-start(bf16[32,128]{1,0:T(8,128)(2,1)} %bitcast.27), channel_id=1, source_target_pairs={{0,1},{1,0},{2,3},{3,2},{4,5},{5,4},{6,7},{7,6},{8,9},{9,8},{10,11... | collective-permute-start | bytes 24584 | tf_op jit(solution)/shard_map/ppermute | solution.py:262
  3.6 4.8 %copy-start = (bf16[32,128]{1,0:T(8,128)(2,1)}, bf16[32,128]{1,0:T(8,128)(2,1)S(1)}, u32[]{:S(2)}) copy-start(bf16[32,128]{1,0:T(8,128)(2,1)S(1)} %collective-permute-done.lat_oth) | copy-start | bytes 24580
  3.6 4.8 %collective-permute-start.2 = (bf16[256,2048]{1,0:T(8,128)(2,1)}, bf16[256,2048]{1,0:T(8,128)(2,1)S(1)}, u32[]{:S(2)}, u32[]{:S(2)}) collective-permute-start(bf16[256,2048]{1,0:T(8,128)(2,1)} %bitcast.21), channel_id=1, source_target_pairs={{0,1},{1,0},{2,3},{3,2},{4,5},{5,4},{6,7},{7,6},{8,9},{9,8},{10,11... | collective-permute-start | bytes 3145736 | tf_op jit(solution)/shard_map/ppermute | solution.py:262
  8.4 26.8 %all-to-all-start = ((bf16[32,9,16,128]{3,2,1,0:T(8,128)(2,1)}), bf16[32,9,16,128]{3,2,1,0:T(8,128)(2,1)S(1)}, u32[]{:S(2)}, u32[]{:S(2)}) async-start(bf16[32,9,16,128]{3,2,1,0:T(8,128)(2,1)} %shard_map.136), calls=%async_computation | async-start | bytes 2359296 | tf_op jit(solution)/shard_map/all_to_all | solution.py:294
  17.0 3.0 %collective-permute-start.3 = (bf16[256,2048]{1,0:T(8,128)(2,1)}, bf16[256,2048]{1,0:T(8,128)(2,1)S(1)}, u32[]{:S(2)}, u32[]{:S(2)}) collective-permute-start(bf16[256,2048]{1,0:T(8,128)(2,1)} %bitcast.17), channel_id=1, source_target_pairs={{0,1},{1,0},{2,3},{3,2},{4,5},{5,4},{6,7},{7,6},{8,9},{9,8},{10,11... | collective-permute-start | bytes 3145736 | tf_op jit(solution)/shard_map/ppermute | solution.py:262
  17.1 4.4 %collective-permute-start.4 = (bf16[256,2048]{1,0:T(8,128)(2,1)}, bf16[256,2048]{1,0:T(8,128)(2,1)S(1)}, u32[]{:S(2)}, u32[]{:S(2)}) collective-permute-start(bf16[256,2048]{1,0:T(8,128)(2,1)} %bitcast.19), channel_id=1, source_target_pairs={{0,1},{1,0},{2,3},{3,2},{4,5},{5,4},{6,7},{7,6},{8,9},{9,8},{10,11... | collective-permute-start | bytes 3145736 | tf_op jit(solution)/shard_map/ppermute | solution.py:262
  31.5 3.8 %collective-permute-start.5 = (bf16[256,1024]{1,0:T(8,128)(2,1)}, bf16[256,1024]{1,0:T(8,128)(2,1)S(1)}, u32[]{:S(2)}, u32[]{:S(2)}) collective-permute-start(bf16[256,1024]{1,0:T(8,128)(2,1)} %get-tuple-element.44), channel_id=1, source_target_pairs={{0,1},{1,0},{2,3},{3,2},{4,5},{5,4},{6,7},{7,6},{8,9},{9,8},{10,11... | collective-permute-start | bytes 1572872 | tf_op jit(solution)/shard_map/ppermute | solution.py:262
  31.7 3.6 %collective-permute-start.6 = (bf16[256,1024]{1,0:T(8,128)(2,1)}, bf16[256,1024]{1,0:T(8,128)(2,1)S(1)}, u32[]{:S(2)}, u32[]{:S(2)}) collective-permute-start(bf16[256,1024]{1,0:T(8,128)(2,1)} %get-tuple-element.45), channel_id=1, source_target_pairs={{0,1},{1,0},{2,3},{3,2},{4,5},{5,4},{6,7},{7,6},{8,9},{9,8},{10,11... | collective-permute-start | bytes 1572872 | tf_op jit(solution)/shard_map/ppermute | solution.py:262
  32.1 11.6 %collective-permute-start.8 = (bf16[256,1024]{1,0:T(8,128)(2,1)}, bf16[256,1024]{1,0:T(8,128)(2,1)S(1)}, u32[]{:S(2)}, u32[]{:S(2)}) collective-permute-start(bf16[256,1024]{1,0:T(8,128)(2,1)} %get-tuple-element.54), channel_id=1, source_target_pairs={{0,1},{1,0},{2,3},{3,2},{4,5},{5,4},{6,7},{7,6},{8,9},{9,8},{10,11... | collective-permute-start | bytes 1572872 | tf_op jit(solution)/shard_map/ppermute | solution.py:262
  32.2 17.6 %collective-permute-start.10 = (bf16[256,1024]{1,0:T(8,128)(2,1)}, bf16[256,1024]{1,0:T(8,128)(2,1)S(1)}, u32[]{:S(2)}, u32[]{:S(2)}) collective-permute-start(bf16[256,1024]{1,0:T(8,128)(2,1)} %get-tuple-element.59), channel_id=1, source_target_pairs={{0,1},{1,0},{2,3},{3,2},{4,5},{5,4},{6,7},{7,6},{8,9},{9,8},{10,11... | collective-permute-start | bytes 1572872 | tf_op jit(solution)/shard_map/ppermute | solution.py:262
  35.3 8.3 %collective-permute-start.7 = (bf16[9,16,128]{2,1,0:T(8,128)(2,1)S(1)}, bf16[9,16,128]{2,1,0:T(8,128)(2,1)S(1)}, u32[]{:S(2)}, u32[]{:S(2)}) collective-permute-start(bf16[9,16,128]{2,1,0:T(8,128)(2,1)S(1)} %shard_map.137.one), channel_id=1, source_target_pairs={{0,128},{1,65},{64,192},{65,1},{128,0},{129,193},{192,64},{193,129... | collective-permute-start | bytes 110600 | tf_op jit(solution)/shard_map/ppermute | solution.py:333
  43.7 5.0 %collective-permute-start.9 = (bf16[9,16,128]{2,1,0:T(8,128)(2,1)S(1)}, bf16[9,16,128]{2,1,0:T(8,128)(2,1)S(1)}, u32[]{:S(2)}, u32[]{:S(2)}) collective-permute-start(bf16[9,16,128]{2,1,0:T(8,128)(2,1)S(1)} %shard_map.140.one), channel_id=1, source_target_pairs={{0,64},{1,129},{64,0},{65,193},{128,192},{129,1},{192,128},{193,65... | collective-permute-start | bytes 110600 | tf_op jit(solution)/shard_map/ppermute | solution.py:333
  49.8 23.2 %all-to-all-start.1 = ((bf16[32,9,16,128]{3,2,1,0:T(8,128)(2,1)}), bf16[32,9,16,128]{3,2,1,0:T(8,128)(2,1)S(1)}, u32[]{:S(2)}, u32[]{:S(2)}) async-start(bf16[32,9,16,128]{3,2,1,0:T(8,128)(2,1)} %shard_map.142), calls=%async_computation.1 | async-start | bytes 2359296 | tf_op jit(solution)/shard_map/all_to_all | solution.py:347

commit v6 on v5

--- a/solution.py
+++ b/solution.py
@@ -88,7 +88,7 @@
         strip = dot(hid_t, half, 1, 0).astype(BF16)
         for j in range(GROUPS):
             for i in range(2):
-                out[j, 2 * n + i] = strip[16 * j : 16 * j + 16, 128 * i : 128 * i + 128]
+                out[j // 8, j % 8, 2 * n + i] = strip[16 * j : 16 * j + 16, 128 * i : 128 * i + 128]
     copies[3].wait()
     back = dot(w2[...], grads[...], 1, 1)
     grad_pre = (back * sig * (1.0 + pre * (1.0 - sig))).astype(BF16)
@@ -96,12 +96,12 @@
     first = first.astype(BF16)
     for j in range(GROUPS):
         m = j // 4
-        out[j, 8] = first[16 * (m // 4) : 16 * (m // 4) + 16, 128 * (m % 4) : 128 * (m % 4) + 128]
+        out[j // 8, j % 8, 8] = first[16 * (m // 4) : 16 * (m // 4) + 16, 128 * (m % 4) : 128 * (m % 4) + 128]
 
 
 def group_sum_body(got, out):
     total = got[0].astype(F32)
-    for j in range(1, GROUPS):
+    for j in range(1, got.shape[0]):
         total = total + got[j].astype(F32)
     out[...] = total.astype(BF16)
 
@@ -112,8 +112,13 @@
 
 def spread_sum_body(one, two, out):
     total = (one[...].astype(F32) + two[...].astype(F32)).astype(BF16)
-    for j in range(GROUPS):
+    for j in range(out.shape[0]):
         out[j] = total
+
+
+def spread_body(part, out):
+    for j in range(out.shape[0]):
+        out[j] = part[...]
 
 
 def finish_body(got, second, first, second_near, first_near, sems):
@@ -121,13 +126,13 @@
     for n in range(4):
         for j in range(8 * n, 8 * n + 8):
             for t in range(8):
-                second_near[16 * j : 16 * j + 16, 128 * t : 128 * t + 128] = got[j, t].astype(F32) * (1.0 / 128.0)
+                second_near[16 * j : 16 * j + 16, 128 * t : 128 * t + 128] = got[j // 8, j % 8, t].astype(F32) * (1.0 / 128.0)
         part = pl.ds(128 * n, 128)
         copies.append(pltpu.make_async_copy(second_near.at[part, :], second.at[part, :], sems.at[n]))
         copies[-1].start()
     for m in range(8):
         rows, cols = 16 * (m // 4), 128 * (m % 4)
-        first_near[rows : rows + 16, cols : cols + 128] = got[4 * m, 8].astype(F32) * (1.0 / 128.0)
+        first_near[rows : rows + 16, cols : cols + 128] = got[m // 2, 4 * (m % 2), 8].astype(F32) * (1.0 / 128.0)
     copies.append(pltpu.make_async_copy(first_near, first, sems.at[4]))
     copies[-1].start()
     for copy in copies:
@@ -182,6 +187,20 @@
         new_v = new_v + shared["dv"]
     dk[rows, cols] = (new_k[seen - ROWS : seen] * scale).astype(BF16)
     dv[rows, cols] = new_v[seen - ROWS : seen].astype(BF16)
+
+
+def near_groups():
+    def chip(half, place):
+        return place if half == 0 else 3 - place
+
+    def device(zl, halves, places, core):
+        return ((zl * 4 + chip(halves // 2, places // 2)) * 4 + chip(halves % 2, places % 2)) * 2 + core
+
+    four = [[device(zl, h, p, 0) for p in range(4)] for zl in range(2) for h in range(4)]
+    four += [[device(zl, h, p, 1) for h in range(4)] for zl in range(2) for p in range(4)]
+    eight = [[device(zl, h, p, 0) for zl in range(2) for h in range(4)] for p in range(4)]
+    eight += [[device(zl, h, p, 1) for zl in range(2) for p in range(4)] for h in range(4)]
+    return four, eight
 
 
 def hidden_of(lat, w1):
@@ -284,14 +303,17 @@
     lat_spec = whole((32, SPAN))
     payload, = call(
         weight_body, scalars, (lat_own, place_near(lat_oth), w_first, w_second, g_rows, place_near(g_oth)),
-        [anywhere, near, anywhere, anywhere, anywhere, near], [near], [pltpu.VMEM((GROUPS, 9, 16, 128), BF16)],
+        [anywhere, near, anywhere, anywhere, anywhere, near], [near], [pltpu.VMEM((4, 8, 9, 16, 128), BF16)],
         scratch=[pltpu.VMEM((32, SPAN), BF16), pltpu.VMEM((32, CH), BF16), pltpu.VMEM((CH, WIDTH), BF16),
                  pltpu.VMEM((ROWS, WIDTH), BF16), pltpu.SemaphoreType.DMA((4,))],
     )
-    block = ("zl", "y", "x")
-    payload, v_oth = lax.optimization_barrier((payload, v_oth))
+    four, eight = near_groups()
+
+    def traded(value, groups):
+        return lax.all_to_all(value, ("zl", "y", "x", "ctx"), 0, 0, axis_index_groups=groups, tiled=False)
+
     q_oth, k_oth, v_oth, g_oth = [place_near(value) for value in (q_oth, k_oth, v_oth, g_oth)]
-    got = lax.all_to_all(payload, block, 0, 0, tiled=False)
+    got = traded(payload, four)
 
     cols = GROUP * HEAD
     steps = HEADS // GROUP
@@ -310,6 +332,7 @@
         grid=(steps,),
         scratch=[pltpu.VMEM((SEQ, cols), BF16)] * 8 + [pltpu.VMEM((SPAN, CH), BF16)],
     )
+    got, *result = lax.optimization_barrier((got, *result))
     lay, dq, dk, dv = result[:4]
     sent_att, sent_dq, sent_dk, sent_dv = [swapped(value) for value in result[4:]]
 
@@ -317,11 +340,11 @@
     width = HALF // parts
     half_spec = pl.BlockSpec((ROWS, width), lambda i, c, *_: (0, (1 - c[0]) * parts + i))
 
-    def placed(got, into):
+    def placed(after, got, into):
         count = len(got)
         return call(
-            place_body, scalars[:1], (*map(place_near, got), *into), [near] * count + [anywhere] * count, [half_spec] * count,
-            [big] * count, grid=(parts,), aliases={1 + count + i: i for i in range(count)},
+            place_body, (after,), (*map(place_near, got), *into), [near] * count + [anywhere] * count,
+            [half_spec] * count, [big] * count, grid=(parts,), aliases={1 + count + i: i for i in range(count)},
         )
 
     def exchanged(value, turn):
@@ -332,19 +355,22 @@
                 pairs.append((2 * z + core, 2 * other + core))
         return lax.ppermute(value, ("zh", "ctx"), pairs)
 
-    one, = near_call(group_sum_body, (got,), [(9, 16, 128)])
-    one, sent_dq, sent_dk = lax.optimization_barrier((one, sent_dq, sent_dk))
+    part, = near_call(group_sum_body, (got,), [(8, 9, 16, 128)])
+    one, = near_call(group_sum_body, (traded(part, eight),), [(9, 16, 128)])
+    one, after = lax.optimization_barrier((one, scalars[0]))
     two = exchanged(one, 0)
-    dq, dk = placed((sent_dq, sent_dk), (dq, dk))
+    dq, dk = placed(after, (sent_dq, sent_dk), (dq, dk))
     two, dq, dk = lax.optimization_barrier((two, dq, dk))
     one, = near_call(pair_sum_body, (one, two), [(9, 16, 128)])
-    one, sent_dv = lax.optimization_barrier((one, sent_dv))
     two = exchanged(one, 1)
-    dv, = placed((sent_dv,), (dv,))
-    two, dv = lax.optimization_barrier((two, dv))
-    sums, = near_call(spread_sum_body, (one, two), [(GROUPS, 9, 16, 128)])
-    sums, sent_att = lax.optimization_barrier((sums, sent_att))
-    got = lax.all_to_all(sums, block, 0, 0, tiled=False)
+    part, = near_call(spread_sum_body, (one, two), [(8, 9, 16, 128)])
+    part, after = lax.optimization_barrier((part, after))
+    part = traded(part, eight)
+    dv, = placed(after, (sent_dv,), (dv,))
+    part, dv = lax.optimization_barrier((part, dv))
+    sums, = near_call(spread_body, (part,), [(4, 8, 9, 16, 128)])
+    sums, after = lax.optimization_barrier((sums, after))
+    got = traded(sums, four)
     sum_second, sum_first = pl.pallas_call(
         finish_body, in_specs=[near], out_specs=[anywhere, anywhere],
         out_shape=[struct((CH, HALF), F32), struct((32, CH), F32)],
@@ -353,7 +379,7 @@
     )(place_near(got))
 
     lay = call(
-        merge_body, scalars, (r_rows, lat_own, lat_oth, w_first, w_second, place_near(sent_att), lay),
+        merge_body, (after, scalars[1]), (r_rows, lat_own, lat_oth, w_first, w_second, place_near(sent_att), lay),
         [pl.BlockSpec((SPAN, width), lambda i, c, s: (1 - c[0], (1 - c[0]) * parts + i)), lat_spec, lat_spec,
          whole((32, CH)), pl.BlockSpec((CH, width), lambda i, c, s: (0, (1 - c[0]) * parts + i)),
          near, anywhere],

time: 75.2 us -> 85.7 us (1.14)
  waiting for transfers between devices: 23.1 us -> 27.2 us
  starting transfers between devices: 28 us -> 31.1 us
  Pallas kernels: 22.5 us -> 25.3 us
    all_to_all x2 -> x4, waiting for transfers between devices: 14.8 us -> 19.6 us  [traded(): lax.all_to_all(value, ('zl', 'y', 'x', 'ctx'), 0, 0, axis_index_groups=gr...]
    all_to_all x2 -> x4, starting transfers between devices: 16.1 us -> 20 us  [traded(): lax.all_to_all(value, ('zl', 'y', 'x', 'ctx'), 0, 0, axis_index_groups=gr...]
    ppermute x9, waiting for transfers between devices: 6.25 us -> 4.29 us  [swapped(): return lax.ppermute(value, 'ctx', swap)]
    pallas_call x3 -> x5, Pallas kernels: 1.27 us -> 2.82 us  [near_call(): pl.pallas_call(body, in_specs=[near] * len(args), out_specs=[near] * len(...]
    ppermute x2, waiting for transfers between devices: 2.07 us -> 3.28 us  [exchanged(): return lax.ppermute(value, ('zh', 'ctx'), pairs)]
    pallas_call x5, Pallas kernels: 19.9 us -> 21.1 us  [call(): pl.pallas_call(body, grid_spec=pltpu.PrefetchScalarGridSpec(num_scalar_pr...]
  transfers between devices with their start and end apart: 13 -> 15, of which waited for: 7 -> 7; matrix products, arithmetic and copies ran while one was open for 0% -> 0% of each run, Pallas kernels for 28% -> 26%
where the time goes in v6:
time: 85.7 us; the launch traced here: 84.3 us
  starting transfers between devices  31.1 us (36%)
  waiting for transfers between devices  27.2 us (32%)
  Pallas kernels  25.3 us (30%)
    pallas_call x5, Pallas kernels, call(): pl.pallas_call(body, grid_spec=pltpu.PrefetchScalarGridSpec(num_scalar_pr...  21.1 us
    all_to_all x4, starting transfers between devices, traded(): lax.all_to_all(value, ('zl', 'y', 'x', 'ctx'), 0, 0, axis_index_groups=gr...  20 us
    all_to_all x4, waiting for transfers between devices, traded(): lax.all_to_all(value, ('zl', 'y', 'x', 'ctx'), 0, 0, axis_index_groups=gr...  19.6 us
    ppermute x2, starting transfers between devices, exchanged(): return lax.ppermute(value, ('zh', 'ctx'), pairs)  9.21 us
    ppermute x9, waiting for transfers between devices, swapped(): return lax.ppermute(value, 'ctx', swap)  4.29 us
    ppermute x2, waiting for transfers between devices, exchanged(): return lax.ppermute(value, ('zh', 'ctx'), pairs)  3.28 us
    pallas_call x5, Pallas kernels, near_call(): pl.pallas_call(body, in_specs=[near] * len(args), out_specs=[near] * len(...  2.82 us
    ppermute x9, starting transfers between devices, swapped(): return lax.ppermute(value, 'ctx', swap)  1.83 us
  transfers between devices with their start and end apart: 15, of which 7 were waited for; matrix products, arithmetic and copies ran while one was open for 0% of the time, Pallas kernels for 26%

profile of v6, /device:TPU:32, one launch (start us, length us, event | category | flops | bytes accessed | tf_op | source)
XLA Modules:
  0.0 84.3 jit_solution(15635607079531673420)
XLA Ops:
  0.7 0.5 collective-permute-start
  1.2 2.4 %collective-permute-done.lat_oth = bf16[32,128]{1,0:T(8,128)(2,1)S(1)} collective-permute-done((bf16[32,128]{1,0:T(8,128)(2,1)}, bf16[32,128]{1,0:T(8,128)(2,1)S(1)}, u32[]{:S(2)}, u32[]{:S(2)}) %collective-permute-start) | collective-permute-done | bytes 8224 | tf_op jit(solution)/shard_map/ppermute | solution.py:281
  4.3 4.6 %shard_map.136 = bf16[4,8,9,16,128]{4,3,2,1,0:T(8,128)(2,1)} custom-call(s32[1]{0:T(128)} %bitcast.ctx_ref, s32[2]{0:T(128)} %bitcast.31, bf16[32,128]{1,0:T(8,128)(2,1)} %bitcast.28, bf16[32,128]{1,0:T(8,128)(2,1)S(1)} %collective-permute-done.lat_oth, bf16[32,512]{1,0:T(8,128)(2,1)} %w1.3, bf16[512,2048]{1,0:T(8,128)(2,1)} %w2.3, ...), custom_call_target="tpu_custom_call" | custom-call | tf_op jit(solution)/shard_map/pallas_call | solution.py:36
  8.9 3.8 %all-to-all-start = ((bf16[4,8,9,16,128]{4,3,2,1,0:T(8,128)(2,1)}), bf16[4,8,9,16,128]{4,3,2,1,0:T(8,128)(2,1)S(1)}, u32[]{:S(2)}, u32[]{:S(2)}) async-start(bf16[4,8,9,16,128]{4,3,2,1,0:T(8,128)(2,1)} %shard_map.136), calls=%async_computation | async-start | bytes 2359296 | tf_op jit(solution)/shard_map/all_to_all | solution.py:313
  12.7 11.2 %shard_map.137 = (bf16[256,2048]{1,0:T(8,128)(2,1)}, bf16[256,2048]{1,0:T(8,128)(2,1)}, bf16[256,2048]{1,0:T(8,128)(2,1)}, bf16[256,2048]{1,0:T(8,128)(2,1)}, bf...) custom-call(s32[1]{0:T(128)} %bitcast.ctx_ref, ...), custom_call_target="tpu_custom_call" | custom-call | tf_op jit(solution)/shard_map/pallas_call | solution.py:36
  24.0 0.9 %shard_map.138 = bf16[8,9,16,128]{3,2,1,0:T(8,128)(2,1)} custom-call(bf16[4,8,9,16,128]{4,3,2,1,0:T(8,128)(2,1)S(1)} %all-to-all-done.got), custom_call_target="tpu_custom_call" | custom-call | tf_op jit(solution)/shard_map/pallas_call | solution.py:298
  24.8 7.7 %all-to-all-start.1 = ((bf16[8,9,16,128]{3,2,1,0:T(8,128)(2,1)}), bf16[8,9,16,128]{3,2,1,0:T(8,128)(2,1)S(1)}, u32[]{:S(2)}, u32[]{:S(2)}) async-start(bf16[8,9,16,128]{3,2,1,0:T(8,128)(2,1)} %shard_map.138), calls=%async_computation.1 | async-start | bytes 589824 | tf_op jit(solution)/shard_map/all_to_all | solution.py:313
  32.6 0.5 collective-permute-start.7
  33.1 7.6 %all-to-all-done.1.got = bf16[8,9,16,128]{3,2,1,0:T(8,128)(2,1)S(1)} async-done(((bf16[8,9,16,128]{3,2,1,0:T(8,128)(2,1)}), bf16[8,9,16,128]{3,2,1,0:T(8,128)(2,1)S(1)}, u32[]{:S(2)}, u32[]{:S(2)}) %all-to-all-start.1) | async-done | bytes 294944 | tf_op jit(solution)/shard_map/all_to_all | solution.py:313
  40.7 6.4 %collective-permute-start.5 = (bf16[9,16,128]{2,1,0:T(8,128)(2,1)S(1)}, bf16[9,16,128]{2,1,0:T(8,128)(2,1)S(1)}, u32[]{:S(2)}, u32[]{:S(2)}) collective-permute-start(bf16[9,16,128]{2,1,0:T(8,128)(2,1)S(1)} %shard_map.139.one), channel_id=1, source_target_pairs={{0,128},{1,65},{64,192},{65,1},{128,0},{129,193},{192,64},{193,129... | collective-permute-start | bytes 110600 | tf_op jit(solution)/shard_map/ppermute | solution.py:356
  47.1 1.0 %shard_map.140 = (bf16[256,2048]{1,0:T(8,128)(2,1)}, bf16[256,2048]{1,0:T(8,128)(2,1)}) custom-call(s32[1]{0:T(128)} %bitcast.ctx_ref, bf16[256,1024]{1,0:T(8,128)(2,1)S(1)} %collective-permute-done.6.refs_0_, bf16[256,1024]{1,0:T(8,128)(2,1)S(1)} %collective-permute-done.7.refs_1_, ...), custom_call_target="tpu_custom_call", output_to_operand_aliasing={{0}: (3, {}), {1}: (4, {})} | custom-call | tf_op jit(solution)/shard_map/pallas_call | solution.py:36
  48.1 1.1 %collective-permute-done.5.two = bf16[9,16,128]{2,1,0:T(8,128)(2,1)S(1)} collective-permute-done((bf16[9,16,128]{2,1,0:T(8,128)(2,1)S(1)}, bf16[9,16,128]{2,1,0:T(8,128)(2,1)S(1)}, u32[]{:S(2)}, u32[]{:S(2)}) %collective-permute-start.5) | collective-permute-done | bytes 36896 | tf_op jit(solution)/shard_map/ppermute | solution.py:356
  49.2 2.8 %collective-permute-start.8 = (bf16[9,16,128]{2,1,0:T(8,128)(2,1)S(1)}, bf16[9,16,128]{2,1,0:T(8,128)(2,1)S(1)}, u32[]{:S(2)}, u32[]{:S(2)}) collective-permute-start(bf16[9,16,128]{2,1,0:T(8,128)(2,1)S(1)} %shard_map.141.one), channel_id=1, source_target_pairs={{0,64},{1,129},{64,0},{65,193},{128,192},{129,1},{192,128},{193,65... | collective-permute-start | bytes 110600 | tf_op jit(solution)/shard_map/ppermute | solution.py:356
  52.0 2.2 %collective-permute-done.8.two = bf16[9,16,128]{2,1,0:T(8,128)(2,1)S(1)} collective-permute-done((bf16[9,16,128]{2,1,0:T(8,128)(2,1)S(1)}, bf16[9,16,128]{2,1,0:T(8,128)(2,1)S(1)}, u32[]{:S(2)}, u32[]{:S(2)}) %collective-permute-start.8) | collective-permute-done | bytes 36896 | tf_op jit(solution)/shard_map/ppermute | solution.py:356
  54.3 0.7 shard_map.142
  55.0 4.9 %all-to-all-start.2 = ((bf16[8,9,16,128]{3,2,1,0:T(8,128)(2,1)}), bf16[8,9,16,128]{3,2,1,0:T(8,128)(2,1)S(1)}, u32[]{:S(2)}, u32[]{:S(2)}) async-start(bf16[8,9,16,128]{3,2,1,0:T(8,128)(2,1)} %shard_map.142), calls=%async_computation.2 | async-start | bytes 589824 | tf_op jit(solution)/shard_map/all_to_all | solution.py:313
  59.9 0.8 shard_map.143
  60.7 7.3 %all-to-all-done.2.part = bf16[8,9,16,128]{3,2,1,0:T(8,128)(2,1)S(1)} async-done(((bf16[8,9,16,128]{3,2,1,0:T(8,128)(2,1)}), bf16[8,9,16,128]{3,2,1,0:T(8,128)(2,1)S(1)}, u32[]{:S(2)}, u32[]{:S(2)}) %all-to-all-start.2) | async-done | bytes 294944 | tf_op jit(solution)/shard_map/all_to_all | solution.py:313
  68.0 1.2 %shard_map.144 = bf16[4,8,9,16,128]{4,3,2,1,0:T(8,128)(2,1)} custom-call(bf16[8,9,16,128]{3,2,1,0:T(8,128)(2,1)S(1)} %all-to-all-done.2.part), custom_call_target="tpu_custom_call" | custom-call | tf_op jit(solution)/shard_map/pallas_call | solution.py:298
  69.1 3.7 %all-to-all-start.3 = ((bf16[4,8,9,16,128]{4,3,2,1,0:T(8,128)(2,1)}), bf16[4,8,9,16,128]{4,3,2,1,0:T(8,128)(2,1)S(1)}, u32[]{:S(2)}, u32[]{:S(2)}) async-start(bf16[4,8,9,16,128]{4,3,2,1,0:T(8,128)(2,1)} %shard_map.144), calls=%async_computation.3 | async-start | bytes 2359296 | tf_op jit(solution)/shard_map/all_to_all | solution.py:313
  72.9 1.9 %collective-permute-done.10.att = bf16[256,1024]{1,0:T(8,128)(2,1)S(1)} collective-permute-done((bf16[256,1024]{1,0:T(8,128)(2,1)S(1)}, bf16[256,1024]{1,0:T(8,128)(2,1)S(1)}, u32[]{:S(2)}, u32[]{:S(2)}) %collective-permute-start.10) | collective-permute-done | bytes 524320 | tf_op jit(solution)/shard_map/ppermute | solution.py:281
  74.8 3.4 %shard_map.145 = bf16[256,2048]{1,0:T(8,128)(2,1)} custom-call(s32[1]{0:T(128)} %bitcast.ctx_ref, s32[2]{0:T(128)} %bitcast.33, bf16[256,2048]{1,0:T(8,128)(2,1)} %bitcast.13, bf16[32,128]{1,0:T(8,128)(2,1)} %bitcast.30, bf16[32,128]{1,0:T(8,128)(2,1)} %copy-done, bf16[32,512]{1,0:T(8,128)(2,1)} %w1.3, ...), custom_call_target="tpu_custom_call", output_to_operand_aliasing={{}: (8, {})} | custom-call | tf_op jit(solution)/shard_map/pallas_call | solution.py:36
  78.2 4.7 %all-to-all-done.3.got = bf16[4,8,9,16,128]{4,3,2,1,0:T(8,128)(2,1)S(1)} async-done(((bf16[4,8,9,16,128]{4,3,2,1,0:T(8,128)(2,1)}), bf16[4,8,9,16,128]{4,3,2,1,0:T(8,128)(2,1)S(1)}, u32[]{:S(2)}, u32[]{:S(2)}) %all-to-all-start.3) | async-done | bytes 1179680 | tf_op jit(solution)/shard_map/all_to_all | solution.py:313
  82.9 1.4 %shard_map.146 = (f32[512,1024]{1,0:T(8,128)}, f32[32,512]{1,0:T(8,128)}) custom-call(bf16[4,8,9,16,128]{4,3,2,1,0:T(8,128)(2,1)S(1)} %all-to-all-done.3.got), custom_call_target="tpu_custom_call" | custom-call | tf_op jit(solution)/shard_map/pallas_call | solution.py:374
  (27 shorter events, 0.9 us)
Async XLA Ops:
  0.6 3.0 %collective-permute-start.1 = (bf16[256,2048]{1,0:T(8,128)(2,1)}, bf16[256,2048]{1,0:T(8,128)(2,1)S(1)}, u32[]{:S(2)}, u32[]{:S(2)}) collective-permute-start(bf16[256,2048]{1,0:T(8,128)(2,1)} %bitcast.14), channel_id=1, source_target_pairs={{0,1},{1,0},{2,3},{3,2},{4,5},{5,4},{6,7},{7,6},{8,9},{9,8},{10,11... | collective-permute-start | bytes 3145736 | tf_op jit(solution)/shard_map/ppermute | solution.py:281
  0.7 2.9 %collective-permute-start = (bf16[32,128]{1,0:T(8,128)(2,1)}, bf16[32,128]{1,0:T(8,128)(2,1)S(1)}, u32[]{:S(2)}, u32[]{:S(2)}) collective-permute-start(bf16[32,128]{1,0:T(8,128)(2,1)} %bitcast.27), channel_id=1, source_target_pairs={{0,1},{1,0},{2,3},{3,2},{4,5},{5,4},{6,7},{7,6},{8,9},{9,8},{10,11... | collective-permute-start | bytes 24584 | tf_op jit(solution)/shard_map/ppermute | solution.py:281
  3.6 5.3 %copy-start = (bf16[32,128]{1,0:T(8,128)(2,1)}, bf16[32,128]{1,0:T(8,128)(2,1)S(1)}, u32[]{:S(2)}) copy-start(bf16[32,128]{1,0:T(8,128)(2,1)S(1)} %collective-permute-done.lat_oth) | copy-start | bytes 24580
  3.6 9.1 %collective-permute-start.2 = (bf16[256,2048]{1,0:T(8,128)(2,1)}, bf16[256,2048]{1,0:T(8,128)(2,1)}, u32[]{:S(2)}, u32[]{:S(2)}) collective-permute-start(bf16[256,2048]{1,0:T(8,128)(2,1)} %bitcast.17), channel_id=1, source_target_pairs={{0,1},{1,0},{2,3},{3,2},{4,5},{5,4},{6,7},{7,6},{8,9},{9,8},{10,11... | collective-permute-start | bytes 3145736 | tf_op jit(solution)/shard_map/ppermute | solution.py:281
  3.7 8.9 %collective-permute-start.3 = (bf16[256,2048]{1,0:T(8,128)(2,1)}, bf16[256,2048]{1,0:T(8,128)(2,1)}, u32[]{:S(2)}, u32[]{:S(2)}) collective-permute-start(bf16[256,2048]{1,0:T(8,128)(2,1)} %bitcast.19), channel_id=1, source_target_pairs={{0,1},{1,0},{2,3},{3,2},{4,5},{5,4},{6,7},{7,6},{8,9},{9,8},{10,11... | collective-permute-start | bytes 3145736 | tf_op jit(solution)/shard_map/ppermute | solution.py:281
  4.1 8.6 %collective-permute-start.4 = (bf16[256,2048]{1,0:T(8,128)(2,1)}, bf16[256,2048]{1,0:T(8,128)(2,1)}, u32[]{:S(2)}, u32[]{:S(2)}) collective-permute-start(bf16[256,2048]{1,0:T(8,128)(2,1)} %bitcast.21), channel_id=1, source_target_pairs={{0,1},{1,0},{2,3},{3,2},{4,5},{5,4},{6,7},{7,6},{8,9},{9,8},{10,11... | collective-permute-start | bytes 3145736 | tf_op jit(solution)/shard_map/ppermute | solution.py:281
  8.9 15.1 %all-to-all-start = ((bf16[4,8,9,16,128]{4,3,2,1,0:T(8,128)(2,1)}), bf16[4,8,9,16,128]{4,3,2,1,0:T(8,128)(2,1)S(1)}, u32[]{:S(2)}, u32[]{:S(2)}) async-start(bf16[4,8,9,16,128]{4,3,2,1,0:T(8,128)(2,1)} %shard_map.136), calls=%async_computation | async-start | bytes 2359296 | tf_op jit(solution)/shard_map/all_to_all | solution.py:313
  23.9 8.6 %copy-start.4 = (bf16[256,1024]{1,0:T(8,128)(2,1)S(1)}, bf16[256,1024]{1,0:T(8,128)(2,1)}, u32[]{:S(2)}) copy-start(bf16[256,1024]{1,0:T(8,128)(2,1)} %get-tuple-element.59) | copy-start | bytes 1572868
  23.9 8.6 %copy-start.3 = (bf16[256,1024]{1,0:T(8,128)(2,1)S(1)}, bf16[256,1024]{1,0:T(8,128)(2,1)}, u32[]{:S(2)}) copy-start(bf16[256,1024]{1,0:T(8,128)(2,1)} %get-tuple-element.60) | copy-start | bytes 1572868
  24.8 15.8 %all-to-all-start.1 = ((bf16[8,9,16,128]{3,2,1,0:T(8,128)(2,1)}), bf16[8,9,16,128]{3,2,1,0:T(8,128)(2,1)S(1)}, u32[]{:S(2)}, u32[]{:S(2)}) async-start(bf16[8,9,16,128]{3,2,1,0:T(8,128)(2,1)} %shard_map.138), calls=%async_computation.1 | async-start | bytes 589824 | tf_op jit(solution)/shard_map/all_to_all | solution.py:313
  32.5 14.5 %collective-permute-start.6 = (bf16[256,1024]{1,0:T(8,128)(2,1)S(1)}, bf16[256,1024]{1,0:T(8,128)(2,1)S(1)}, u32[]{:S(2)}, u32[]{:S(2)}) collective-permute-start(bf16[256,1024]{1,0:T(8,128)(2,1)S(1)} %copy-done.4), channel_id=1, source_target_pairs={{0,1},{1,0},{2,3},{3,2},{4,5},{5,4},{6,7},{7,6},{8,9},{9,8},{10,11... | collective-permute-start | bytes 1572872 | tf_op jit(solution)/shard_map/ppermute | solution.py:281
  32.6 14.5 %collective-permute-start.7 = (bf16[256,1024]{1,0:T(8,128)(2,1)S(1)}, bf16[256,1024]{1,0:T(8,128)(2,1)S(1)}, u32[]{:S(2)}, u32[]{:S(2)}) collective-permute-start(bf16[256,1024]{1,0:T(8,128)(2,1)S(1)} %copy-done.3), channel_id=1, source_target_pairs={{0,1},{1,0},{2,3},{3,2},{4,5},{5,4},{6,7},{7,6},{8,9},{9,8},{10,11... | collective-permute-start | bytes 1572872 | tf_op jit(solution)/shard_map/ppermute | solution.py:281
  40.7 11.3 %copy-start.2 = (bf16[256,1024]{1,0:T(8,128)(2,1)S(1)}, bf16[256,1024]{1,0:T(8,128)(2,1)}, u32[]{:S(2)}) copy-start(bf16[256,1024]{1,0:T(8,128)(2,1)} %get-tuple-element.68) | copy-start | bytes 1572868
  40.7 8.5 %collective-permute-start.5 = (bf16[9,16,128]{2,1,0:T(8,128)(2,1)S(1)}, bf16[9,16,128]{2,1,0:T(8,128)(2,1)S(1)}, u32[]{:S(2)}, u32[]{:S(2)}) collective-permute-start(bf16[9,16,128]{2,1,0:T(8,128)(2,1)S(1)} %shard_map.139.one), channel_id=1, source_target_pairs={{0,128},{1,65},{64,192},{65,1},{128,0},{129,193},{192,64},{193,129... | collective-permute-start | bytes 110600 | tf_op jit(solution)/shard_map/ppermute | solution.py:356
  49.2 5.0 %collective-permute-start.8 = (bf16[9,16,128]{2,1,0:T(8,128)(2,1)S(1)}, bf16[9,16,128]{2,1,0:T(8,128)(2,1)S(1)}, u32[]{:S(2)}, u32[]{:S(2)}) collective-permute-start(bf16[9,16,128]{2,1,0:T(8,128)(2,1)S(1)} %shard_map.141.one), channel_id=1, source_target_pairs={{0,64},{1,129},{64,0},{65,193},{128,192},{129,1},{192,128},{193,65... | collective-permute-start | bytes 110600 | tf_op jit(solution)/shard_map/ppermute | solution.py:356
  52.0 7.8 %collective-permute-start.9 = (bf16[256,1024]{1,0:T(8,128)(2,1)S(1)}, bf16[256,1024]{1,0:T(8,128)(2,1)S(1)}, u32[]{:S(2)}, u32[]{:S(2)}) collective-permute-start(bf16[256,1024]{1,0:T(8,128)(2,1)S(1)} %copy-done.2), channel_id=1, source_target_pairs={{0,1},{1,0},{2,3},{3,2},{4,5},{5,4},{6,7},{7,6},{8,9},{9,8},{10,11... | collective-permute-start | bytes 1572872 | tf_op jit(solution)/shard_map/ppermute | solution.py:281
  55.0 13.0 %all-to-all-start.2 = ((bf16[8,9,16,128]{3,2,1,0:T(8,128)(2,1)}), bf16[8,9,16,128]{3,2,1,0:T(8,128)(2,1)S(1)}, u32[]{:S(2)}, u32[]{:S(2)}) async-start(bf16[8,9,16,128]{3,2,1,0:T(8,128)(2,1)} %shard_map.142), calls=%async_computation.2 | async-start | bytes 589824 | tf_op jit(solution)/shard_map/all_to_all | solution.py:313
  69.1 3.7 %copy-start.1 = (bf16[256,1024]{1,0:T(8,128)(2,1)S(1)}, bf16[256,1024]{1,0:T(8,128)(2,1)}, u32[]{:S(2)}) copy-start(bf16[256,1024]{1,0:T(8,128)(2,1)} %get-tuple-element.72) | copy-start | bytes 1572868
  69.1 13.8 %all-to-all-start.3 = ((bf16[4,8,9,16,128]{4,3,2,1,0:T(8,128)(2,1)}), bf16[4,8,9,16,128]{4,3,2,1,0:T(8,128)(2,1)S(1)}, u32[]{:S(2)}, u32[]{:S(2)}) async-start(bf16[4,8,9,16,128]{4,3,2,1,0:T(8,128)(2,1)} %shard_map.144), calls=%async_computation.3 | async-start | bytes 2359296 | tf_op jit(solution)/shard_map/all_to_all | solution.py:313
  72.8 2.0 %collective-permute-start.10 = (bf16[256,1024]{1,0:T(8,128)(2,1)S(1)}, bf16[256,1024]{1,0:T(8,128)(2,1)S(1)}, u32[]{:S(2)}, u32[]{:S(2)}) collective-permute-start(bf16[256,1024]{1,0:T(8,128)(2,1)S(1)} %copy-done.1), channel_id=1, source_target_pairs={{0,1},{1,0},{2,3},{3,2},{4,5},{5,4},{6,7},{7,6},{8,9},{9,8},{10,11... | collective-permute-start | bytes 1572872 | tf_op jit(solution)/shard_map/ppermute | solution.py:281

commit v7 on v5

--- a/solution.py
+++ b/solution.py
@@ -32,7 +32,7 @@
     return pl.BlockSpec(shape, lambda *_: (0,) * len(shape))
 
 
-def call(body, scalars, args, in_specs, out_specs, out_shape, grid=(1,), scratch=(), aliases=None):
+def call(body, scalars, args, in_specs, out_specs, out_shape, grid=(1,), scratch=(), aliases=None, cost=None):
     return pl.pallas_call(
         body,
         grid_spec=pltpu.PrefetchScalarGridSpec(
@@ -44,6 +44,7 @@
         ),
         out_shape=out_shape,
         input_output_aliases=aliases or {},
+        cost_estimate=cost,
         compiler_params=pltpu.CompilerParams(vmem_limit_bytes=VMEM),
     )(*scalars, *args)
 
@@ -289,7 +290,6 @@
                  pltpu.VMEM((ROWS, WIDTH), BF16), pltpu.SemaphoreType.DMA((4,))],
     )
     block = ("zl", "y", "x")
-    payload, v_oth = lax.optimization_barrier((payload, v_oth))
     q_oth, k_oth, v_oth, g_oth = [place_near(value) for value in (q_oth, k_oth, v_oth, g_oth)]
     got = lax.all_to_all(payload, block, 0, 0, tiled=False)
 
@@ -309,6 +309,7 @@
         [big] * 4 + [small] * 4,
         grid=(steps,),
         scratch=[pltpu.VMEM((SEQ, cols), BF16)] * 8 + [pltpu.VMEM((SPAN, CH), BF16)],
+        cost=pl.CostEstimate(flops=40_000_000_000, bytes_accessed=100_000_000, transcendentals=4_000_000),
     )
     lay, dq, dk, dv = result[:4]
     sent_att, sent_dq, sent_dk, sent_dv = [swapped(value) for value in result[4:]]
@@ -333,15 +334,12 @@
         return lax.ppermute(value, ("zh", "ctx"), pairs)
 
     one, = near_call(group_sum_body, (got,), [(9, 16, 128)])
-    one, sent_dq, sent_dk = lax.optimization_barrier((one, sent_dq, sent_dk))
     two = exchanged(one, 0)
-    dq, dk = placed((sent_dq, sent_dk), (dq, dk))
-    two, dq, dk = lax.optimization_barrier((two, dq, dk))
     one, = near_call(pair_sum_body, (one, two), [(9, 16, 128)])
-    one, sent_dv = lax.optimization_barrier((one, sent_dv))
+    one, sent_dq, sent_dk, sent_dv = lax.optimization_barrier((one, sent_dq, sent_dk, sent_dv))
     two = exchanged(one, 1)
-    dv, = placed((sent_dv,), (dv,))
-    two, dv = lax.optimization_barrier((two, dv))
+    dq, dk, dv = placed((sent_dq, sent_dk, sent_dv), (dq, dk, dv))
+    two, dq, dk, dv = lax.optimization_barrier((two, dq, dk, dv))
     sums, = near_call(spread_sum_body, (one, two), [(GROUPS, 9, 16, 128)])
     sums, sent_att = lax.optimization_barrier((sums, sent_att))
     got = lax.all_to_all(sums, block, 0, 0, tiled=False)

time: 75.2 us -> 72.8 us (0.968)
  starting transfers between devices: 28 us -> 25.5 us
    ppermute x9, waiting for transfers between devices: 6.25 us -> 2.39 us  [swapped(): return lax.ppermute(value, 'ctx', swap)]
    all_to_all x1, waiting for transfers between devices: 2.54 us -> 6.12 us  [local(): got = lax.all_to_all(payload, block, 0, 0, tiled=False)]
    all_to_all x1, starting transfers between devices: 7.49 us -> 5.19 us  [local(): got = lax.all_to_all(sums, block, 0, 0, tiled=False)]
    pallas_call x5 -> x4, Pallas kernels: 19.9 us -> 20.1 us  [call(): pl.pallas_call(body, grid_spec=pltpu.PrefetchScalarGridSpec(num_scalar_pr...]
  transfers between devices with their start and end apart: 13 -> 13, of which waited for: 7 -> 5; matrix products, arithmetic and copies ran while one was open for 0% -> 0% of each run, Pallas kernels for 28% -> 30%
where the time goes in v7:
time: 72.8 us; the launch traced here: 72.2 us
  starting transfers between devices  25.5 us (35%)
  waiting for transfers between devices  23.2 us (32%)
  Pallas kernels  22.8 us (31%)
  between operations  0.74 us (1%)
    pallas_call x4, Pallas kernels, call(): pl.pallas_call(body, grid_spec=pltpu.PrefetchScalarGridSpec(num_scalar_pr...  20.1 us
    all_to_all x1, waiting for transfers between devices, local(): got = lax.all_to_all(sums, block, 0, 0, tiled=False)  12 us
    ppermute x2, starting transfers between devices, exchanged(): return lax.ppermute(value, ('zh', 'ctx'), pairs)  9.37 us
    all_to_all x1, starting transfers between devices, local(): got = lax.all_to_all(payload, block, 0, 0, tiled=False)  8.58 us
    all_to_all x1, waiting for transfers between devices, local(): got = lax.all_to_all(payload, block, 0, 0, tiled=False)  6.12 us
    all_to_all x1, starting transfers between devices, local(): got = lax.all_to_all(sums, block, 0, 0, tiled=False)  5.19 us
    ppermute x2, waiting for transfers between devices, exchanged(): return lax.ppermute(value, ('zh', 'ctx'), pairs)  2.7 us
    ppermute x9, waiting for transfers between devices, swapped(): return lax.ppermute(value, 'ctx', swap)  2.39 us
  transfers between devices with their start and end apart: 13, of which 5 were waited for; matrix products, arithmetic and copies ran while one was open for 0% of the time, Pallas kernels for 30%

profile of v7, /device:TPU:32, one launch (start us, length us, event | category | flops | bytes accessed | tf_op | source)
XLA Modules:
  0.0 72.2 jit_solution(16387222686130249301)
XLA Ops:
  0.6 0.1 collective-permute-start.1
  0.7 0.5 collective-permute-start
  1.2 2.4 %collective-permute-done.lat_oth = bf16[32,128]{1,0:T(8,128)(2,1)S(1)} collective-permute-done((bf16[32,128]{1,0:T(8,128)(2,1)}, bf16[32,128]{1,0:T(8,128)(2,1)S(1)}, u32[]{:S(2)}, u32[]{:S(2)}) %collective-permute-start) | collective-permute-done | bytes 8224 | tf_op jit(solution)/shard_map/ppermute | solution.py:263
  3.6 0.1 collective-permute-start.3
  3.7 0.4 collective-permute-start.4
  4.1 0.1 collective-permute-start.5
  4.3 4.6 %shard_map.136 = bf16[32,9,16,128]{3,2,1,0:T(8,128)(2,1)} custom-call(s32[1]{0:T(128)} %bitcast.ctx_ref, s32[2]{0:T(128)} %bitcast.25, bf16[32,128]{1,0:T(8,128)(2,1)} %bitcast.22, bf16[32,128]{1,0:T(8,128)(2,1)S(1)} %collective-permute-done.lat_oth, bf16[32,512]{1,0:T(8,128)(2,1)} %w1.3, bf16[512,2048]{1,0:T(8,128)(2,1)} %w2.3, bf16[256,2048]{1,0:T(8,128)(2,1)} %bitcast.19, ...), custom_call_target="tpu_custom_call" | custom-call | tf_op jit(solution)/shard_map/pallas_call | solution.py:36
  8.9 8.6 %all-to-all-start = ((bf16[32,9,16,128]{3,2,1,0:T(8,128)(2,1)}), bf16[32,9,16,128]{3,2,1,0:T(8,128)(2,1)S(1)}, u32[]{:S(2)}, u32[]{:S(2)}) async-start(bf16[32,9,16,128]{3,2,1,0:T(8,128)(2,1)} %shard_map.136), calls=%async_computation | async-start | bytes 2359296 | tf_op jit(solution)/shard_map/all_to_all | solution.py:294
  17.5 10.9 %shard_map.139 = (bf16[256,2048]{1,0:T(8,128)(2,1)}, bf16[256,2048]{1,0:T(8,128)(2,1)}, bf16[256,2048]{1,0:T(8,128)(2,1)}, bf16[256,2048]{1,0:T(8,128)(2,1)}, bf...) custom-call(s32[1]{0:T(128)} %bitcast.ctx_ref, ...), custom_call_target="tpu_custom_call" | custom-call | flops 40000000000 | bytes 100000000 | tf_op jit(solution)/shard_map/pallas_call | solution.py:36
  28.5 0.5 collective-permute-start.7
  29.0 0.1 collective-permute-start.8
  29.1 0.4 collective-permute-start.10
  29.5 6.1 %all-to-all-done.got = bf16[32,9,16,128]{3,2,1,0:T(8,128)(2,1)S(1)} async-done(((bf16[32,9,16,128]{3,2,1,0:T(8,128)(2,1)}), bf16[32,9,16,128]{3,2,1,0:T(8,128)(2,1)S(1)}, u32[]{:S(2)}, u32[]{:S(2)}) %all-to-all-start) | async-done | bytes 1179680 | tf_op jit(solution)/shard_map/all_to_all | solution.py:294
  35.7 0.2 shard_map.137.one
  35.8 6.4 %collective-permute-start.2 = (bf16[9,16,128]{2,1,0:T(8,128)(2,1)S(1)}, bf16[9,16,128]{2,1,0:T(8,128)(2,1)S(1)}, u32[]{:S(2)}, u32[]{:S(2)}) collective-permute-start(bf16[9,16,128]{2,1,0:T(8,128)(2,1)S(1)} %shard_map.137.one), channel_id=1, source_target_pairs={{0,128},{1,65},{64,192},{65,1},{128,0},{129,193},{192,64},{193,129... | collective-permute-start | bytes 110600 | tf_op jit(solution)/shard_map/ppermute | solution.py:334
  42.2 1.9 %collective-permute-done.2.two = bf16[9,16,128]{2,1,0:T(8,128)(2,1)S(1)} collective-permute-done((bf16[9,16,128]{2,1,0:T(8,128)(2,1)S(1)}, bf16[9,16,128]{2,1,0:T(8,128)(2,1)S(1)}, u32[]{:S(2)}, u32[]{:S(2)}) %collective-permute-start.2) | collective-permute-done | bytes 36896 | tf_op jit(solution)/shard_map/ppermute | solution.py:334
  44.2 3.0 %collective-permute-start.9 = (bf16[9,16,128]{2,1,0:T(8,128)(2,1)S(1)}, bf16[9,16,128]{2,1,0:T(8,128)(2,1)S(1)}, u32[]{:S(2)}, u32[]{:S(2)}) collective-permute-start(bf16[9,16,128]{2,1,0:T(8,128)(2,1)S(1)} %shard_map.138.one), channel_id=1, source_target_pairs={{0,64},{1,129},{64,0},{65,193},{128,192},{129,1},{192,128},{193,65... | collective-permute-start | bytes 110600 | tf_op jit(solution)/shard_map/ppermute | solution.py:334
  47.2 1.2 %shard_map.140 = (bf16[256,2048]{1,0:T(8,128)(2,1)}, bf16[256,2048]{1,0:T(8,128)(2,1)}, bf16[256,2048]{1,0:T(8,128)(2,1)}) custom-call(s32[1]{0:T(128)} %bitcast.ctx_ref, bf16[256,1024]{1,0:T(8,128)(2,1)S(1)} %collective-permute-done.6.refs_0_, ...), custom_call_target="tpu_custom_call", output_to_operand_aliasing={{0}: (4, {}), {1}: (5, {}), {2}: (6, {})} | custom-call | tf_op jit(solution)/shard_map/pallas_call | solution.py:36
  48.4 0.8 %collective-permute-done.9.two = bf16[9,16,128]{2,1,0:T(8,128)(2,1)S(1)} collective-permute-done((bf16[9,16,128]{2,1,0:T(8,128)(2,1)S(1)}, bf16[9,16,128]{2,1,0:T(8,128)(2,1)S(1)}, u32[]{:S(2)}, u32[]{:S(2)}) %collective-permute-start.9) | collective-permute-done | bytes 36896 | tf_op jit(solution)/shard_map/ppermute | solution.py:334
  49.1 1.1 %shard_map.141 = bf16[32,9,16,128]{3,2,1,0:T(8,128)(2,1)} custom-call(bf16[9,16,128]{2,1,0:T(8,128)(2,1)S(1)} %shard_map.138.one, bf16[9,16,128]{2,1,0:T(8,128)(2,1)S(1)} %collective-permute-done.9.two), custom_call_target="tpu_custom_call" | custom-call | tf_op jit(solution)/shard_map/pallas_call | solution.py:280
  50.2 5.2 %all-to-all-start.1 = ((bf16[32,9,16,128]{3,2,1,0:T(8,128)(2,1)}), bf16[32,9,16,128]{3,2,1,0:T(8,128)(2,1)S(1)}, u32[]{:S(2)}, u32[]{:S(2)}) async-start(bf16[32,9,16,128]{3,2,1,0:T(8,128)(2,1)} %shard_map.141), calls=%async_computation.1 | async-start | bytes 2359296 | tf_op jit(solution)/shard_map/all_to_all | solution.py:345
  55.4 3.4 %shard_map.142 = bf16[256,2048]{1,0:T(8,128)(2,1)} custom-call(s32[1]{0:T(128)} %bitcast.ctx_ref, s32[2]{0:T(128)} %bitcast.27, bf16[256,2048]{1,0:T(8,128)(2,1)} %bitcast.13, bf16[32,128]{1,0:T(8,128)(2,1)} %bitcast.24, bf16[32,128]{1,0:T(8,128)(2,1)} %copy-done, bf16[32,512]{1,0:T(8,128)(2,1)} %w1.3, ...), custom_call_target="tpu_custom_call", output_to_operand_aliasing={{}: (8, {})} | custom-call | tf_op jit(solution)/shard_map/pallas_call | solution.py:36
  58.8 12.0 %all-to-all-done.1.got = bf16[32,9,16,128]{3,2,1,0:T(8,128)(2,1)S(1)} async-done(((bf16[32,9,16,128]{3,2,1,0:T(8,128)(2,1)}), bf16[32,9,16,128]{3,2,1,0:T(8,128)(2,1)S(1)}, u32[]{:S(2)}, u32[]{:S(2)}) %all-to-all-start.1) | async-done | bytes 1179680 | tf_op jit(solution)/shard_map/all_to_all | solution.py:345
  70.8 1.4 %shard_map.143 = (f32[512,1024]{1,0:T(8,128)}, f32[32,512]{1,0:T(8,128)}) custom-call(bf16[32,9,16,128]{3,2,1,0:T(8,128)(2,1)S(1)} %all-to-all-done.1.got), custom_call_target="tpu_custom_call" | custom-call | tf_op jit(solution)/shard_map/pallas_call | solution.py:346
  (12 shorter events, 0.1 us)
Async XLA Ops:
  0.6 3.0 %collective-permute-start.1 = (bf16[256,2048]{1,0:T(8,128)(2,1)}, bf16[256,2048]{1,0:T(8,128)(2,1)S(1)}, u32[]{:S(2)}, u32[]{:S(2)}) collective-permute-start(bf16[256,2048]{1,0:T(8,128)(2,1)} %bitcast.18), channel_id=1, source_target_pairs={{0,1},{1,0},{2,3},{3,2},{4,5},{5,4},{6,7},{7,6},{8,9},{9,8},{10,11... | collective-permute-start | bytes 3145736 | tf_op jit(solution)/shard_map/ppermute | solution.py:263
  0.7 2.9 %collective-permute-start = (bf16[32,128]{1,0:T(8,128)(2,1)}, bf16[32,128]{1,0:T(8,128)(2,1)S(1)}, u32[]{:S(2)}, u32[]{:S(2)}) collective-permute-start(bf16[32,128]{1,0:T(8,128)(2,1)} %bitcast.21), channel_id=1, source_target_pairs={{0,1},{1,0},{2,3},{3,2},{4,5},{5,4},{6,7},{7,6},{8,9},{9,8},{10,11... | collective-permute-start | bytes 24584 | tf_op jit(solution)/shard_map/ppermute | solution.py:263
  3.6 5.3 %copy-start = (bf16[32,128]{1,0:T(8,128)(2,1)}, bf16[32,128]{1,0:T(8,128)(2,1)S(1)}, u32[]{:S(2)}) copy-start(bf16[32,128]{1,0:T(8,128)(2,1)S(1)} %collective-permute-done.lat_oth) | copy-start | bytes 24580
  3.6 13.9 %collective-permute-start.3 = (bf16[256,2048]{1,0:T(8,128)(2,1)}, bf16[256,2048]{1,0:T(8,128)(2,1)S(1)}, u32[]{:S(2)}, u32[]{:S(2)}) collective-permute-start(bf16[256,2048]{1,0:T(8,128)(2,1)} %bitcast.28), channel_id=1, source_target_pairs={{0,1},{1,0},{2,3},{3,2},{4,5},{5,4},{6,7},{7,6},{8,9},{9,8},{10,11... | collective-permute-start | bytes 3145736 | tf_op jit(solution)/shard_map/ppermute | solution.py:263
  3.7 13.8 %collective-permute-start.4 = (bf16[256,2048]{1,0:T(8,128)(2,1)}, bf16[256,2048]{1,0:T(8,128)(2,1)}, u32[]{:S(2)}, u32[]{:S(2)}) collective-permute-start(bf16[256,2048]{1,0:T(8,128)(2,1)} %bitcast.30), channel_id=1, source_target_pairs={{0,1},{1,0},{2,3},{3,2},{4,5},{5,4},{6,7},{7,6},{8,9},{9,8},{10,11... | collective-permute-start | bytes 3145736 | tf_op jit(solution)/shard_map/ppermute | solution.py:263
  4.1 13.4 %collective-permute-start.5 = (bf16[256,2048]{1,0:T(8,128)(2,1)}, bf16[256,2048]{1,0:T(8,128)(2,1)}, u32[]{:S(2)}, u32[]{:S(2)}) collective-permute-start(bf16[256,2048]{1,0:T(8,128)(2,1)} %bitcast.32), channel_id=1, source_target_pairs={{0,1},{1,0},{2,3},{3,2},{4,5},{5,4},{6,7},{7,6},{8,9},{9,8},{10,11... | collective-permute-start | bytes 3145736 | tf_op jit(solution)/shard_map/ppermute | solution.py:263
  8.9 26.8 %all-to-all-start = ((bf16[32,9,16,128]{3,2,1,0:T(8,128)(2,1)}), bf16[32,9,16,128]{3,2,1,0:T(8,128)(2,1)S(1)}, u32[]{:S(2)}, u32[]{:S(2)}) async-start(bf16[32,9,16,128]{3,2,1,0:T(8,128)(2,1)} %shard_map.136), calls=%async_computation | async-start | bytes 2359296 | tf_op jit(solution)/shard_map/all_to_all | solution.py:294
  28.4 15.7 %collective-permute-start.6 = (bf16[256,1024]{1,0:T(8,128)(2,1)}, bf16[256,1024]{1,0:T(8,128)(2,1)S(1)}, u32[]{:S(2)}, u32[]{:S(2)}) collective-permute-start(bf16[256,1024]{1,0:T(8,128)(2,1)} %get-tuple-element.39), channel_id=1, source_target_pairs={{0,1},{1,0},{2,3},{3,2},{4,5},{5,4},{6,7},{7,6},{8,9},{9,8},{10,11... | collective-permute-start | bytes 1572872 | tf_op jit(solution)/shard_map/ppermute | solution.py:263
  28.5 15.6 %collective-permute-start.7 = (bf16[256,1024]{1,0:T(8,128)(2,1)}, bf16[256,1024]{1,0:T(8,128)(2,1)S(1)}, u32[]{:S(2)}, u32[]{:S(2)}) collective-permute-start(bf16[256,1024]{1,0:T(8,128)(2,1)} %get-tuple-element.40), channel_id=1, source_target_pairs={{0,1},{1,0},{2,3},{3,2},{4,5},{5,4},{6,7},{7,6},{8,9},{9,8},{10,11... | collective-permute-start | bytes 1572872 | tf_op jit(solution)/shard_map/ppermute | solution.py:263
  29.0 15.2 %collective-permute-start.8 = (bf16[256,1024]{1,0:T(8,128)(2,1)}, bf16[256,1024]{1,0:T(8,128)(2,1)S(1)}, u32[]{:S(2)}, u32[]{:S(2)}) collective-permute-start(bf16[256,1024]{1,0:T(8,128)(2,1)} %get-tuple-element.41), channel_id=1, source_target_pairs={{0,1},{1,0},{2,3},{3,2},{4,5},{5,4},{6,7},{7,6},{8,9},{9,8},{10,11... | collective-permute-start | bytes 1572872 | tf_op jit(solution)/shard_map/ppermute | solution.py:263
  29.1 21.1 %collective-permute-start.10 = (bf16[256,1024]{1,0:T(8,128)(2,1)}, bf16[256,1024]{1,0:T(8,128)(2,1)S(1)}, u32[]{:S(2)}, u32[]{:S(2)}) collective-permute-start(bf16[256,1024]{1,0:T(8,128)(2,1)} %get-tuple-element.53), channel_id=1, source_target_pairs={{0,1},{1,0},{2,3},{3,2},{4,5},{5,4},{6,7},{7,6},{8,9},{9,8},{10,11... | collective-permute-start | bytes 1572872 | tf_op jit(solution)/shard_map/ppermute | solution.py:263
  35.8 8.3 %collective-permute-start.2 = (bf16[9,16,128]{2,1,0:T(8,128)(2,1)S(1)}, bf16[9,16,128]{2,1,0:T(8,128)(2,1)S(1)}, u32[]{:S(2)}, u32[]{:S(2)}) collective-permute-start(bf16[9,16,128]{2,1,0:T(8,128)(2,1)S(1)} %shard_map.137.one), channel_id=1, source_target_pairs={{0,128},{1,65},{64,192},{65,1},{128,0},{129,193},{192,64},{193,129... | collective-permute-start | bytes 110600 | tf_op jit(solution)/shard_map/ppermute | solution.py:334
  44.2 4.9 %collective-permute-start.9 = (bf16[9,16,128]{2,1,0:T(8,128)(2,1)S(1)}, bf16[9,16,128]{2,1,0:T(8,128)(2,1)S(1)}, u32[]{:S(2)}, u32[]{:S(2)}) collective-permute-start(bf16[9,16,128]{2,1,0:T(8,128)(2,1)S(1)} %shard_map.138.one), channel_id=1, source_target_pairs={{0,64},{1,129},{64,0},{65,193},{128,192},{129,1},{192,128},{193,65... | collective-permute-start | bytes 110600 | tf_op jit(solution)/shard_map/ppermute | solution.py:334
  50.2 20.6 %all-to-all-start.1 = ((bf16[32,9,16,128]{3,2,1,0:T(8,128)(2,1)}), bf16[32,9,16,128]{3,2,1,0:T(8,128)(2,1)S(1)}, u32[]{:S(2)}, u32[]{:S(2)}) async-start(bf16[32,9,16,128]{3,2,1,0:T(8,128)(2,1)} %shard_map.141), calls=%async_computation.1 | async-start | bytes 2359296 | tf_op jit(solution)/shard_map/all_to_all | solution.py:345

commit v8 on v7

--- a/solution.py
+++ b/solution.py
@@ -65,39 +65,50 @@
     return jnp.where(in_order, one, two).astype(BF16), jnp.where(in_order, two, one).astype(BF16)
 
 
-def weight_body(ctx_ref, starts, lat_hbm, lat_oth, w1_hbm, w2_hbm, g_own, g_oth, out, lat_own, w1, w2, grads, sems):
-    ctx = ctx_ref[0]
-    own_rows = pl.ds(pl.multiple_of(ctx * SPAN, SPAN), SPAN)
-    oth_rows = pl.ds(pl.multiple_of(SPAN - ctx * SPAN, SPAN), SPAN)
+def hidden_body(ctx_ref, starts, lat_hbm, lat_oth, w1_hbm, w2_hbm, g_own, patches, hid_t, gate, w2, grads, lat_own, w1, sems):
+    own_rows = pl.ds(pl.multiple_of(ctx_ref[0] * SPAN, SPAN), SPAN)
     copies = [
         pltpu.make_async_copy(source, target, sems.at[i])
         for i, (source, target) in enumerate((
-            (lat_hbm, lat_own), (w1_hbm, w1), (g_own.at[own_rows, :], grads.at[0:SPAN, :]), (w2_hbm, w2)))
+            (lat_hbm, lat_own), (w1_hbm, w1), (g_own.at[own_rows, :], grads), (w2_hbm, w2)))
     ]
     for copy in copies:
         copy.start()
-    grads[SPAN:ROWS, :] = g_oth[oth_rows, :]
     copies[0].wait()
     copies[1].wait()
-    patches = jnp.concatenate(pick(starts, lat_own, lat_oth), axis=1)
-    pre = dot(w1[...], patches, 0, 0)
+    both = jnp.concatenate(pick(starts, lat_own, lat_oth), axis=1)
+    pre = dot(w1[...], both, 0, 0)
     sig = sigmoid(pre)
-    hid_t = (pre * sig).astype(BF16)
+    patches[...] = both
+    hid_t[...] = (pre * sig).astype(BF16)
+    gate[...] = sig * (1.0 + pre * (1.0 - sig))
     copies[2].wait()
+    copies[3].wait()
+
+
+def weight_body(ctx_ref, patches, hid_t, gate, w2, g_own, g_oth, out, grads, tiles, sems):
+    ctx = ctx_ref[0]
+    oth_rows = pl.ds(pl.multiple_of(SPAN - ctx * SPAN, SPAN), SPAN)
+    grads[0:SPAN, :] = g_own[...]
+    grads[SPAN:ROWS, :] = g_oth[oth_rows, :]
     for n in range(4):
         half = grads[:, pl.ds(pl.multiple_of(ctx * HALF, HALF) + 256 * n, 256)]
-        strip = dot(hid_t, half, 1, 0).astype(BF16)
+        strip = dot(hid_t[...], half, 1, 0).astype(BF16)
         for j in range(GROUPS):
             for i in range(2):
-                out[j, 2 * n + i] = strip[16 * j : 16 * j + 16, 128 * i : 128 * i + 128]
-    copies[3].wait()
+                tiles[j, 2 * n + i] = strip[16 * j : 16 * j + 16, 128 * i : 128 * i + 128]
+    main, rest = pl.ds(0, 8), pl.ds(8, 1)
+    copies = [pltpu.make_async_copy(tiles.at[:, part], out.at[:, part], sems.at[i]) for i, part in enumerate((main, rest))]
+    copies[0].start()
     back = dot(w2[...], grads[...], 1, 1)
-    grad_pre = (back * sig * (1.0 + pre * (1.0 - sig))).astype(BF16)
-    first = dot(patches, grad_pre, 1, 1)
-    first = first.astype(BF16)
+    grad_pre = (back * gate[...]).astype(BF16)
+    first = dot(patches[...], grad_pre, 1, 1).astype(BF16)
     for j in range(GROUPS):
         m = j // 4
-        out[j, 8] = first[16 * (m // 4) : 16 * (m // 4) + 16, 128 * (m % 4) : 128 * (m % 4) + 128]
+        tiles[j, 8] = first[16 * (m // 4) : 16 * (m // 4) + 16, 128 * (m % 4) : 128 * (m % 4) + 128]
+    copies[1].start()
+    copies[0].wait()
+    copies[1].wait()
 
 
 def group_sum_body(got, out):
@@ -107,12 +118,10 @@
     out[...] = total.astype(BF16)
 
 
-def pair_sum_body(one, two, out):
-    out[...] = (one[...].astype(F32) + two[...].astype(F32)).astype(BF16)
-
-
-def spread_sum_body(one, two, out):
-    total = (one[...].astype(F32) + two[...].astype(F32)).astype(BF16)
+def spread_sum_body(one, next1, next2, next3, out):
+    even = one[...].astype(F32) + next2[...].astype(F32)
+    odd = next1[...].astype(F32) + next3[...].astype(F32)
+    total = (even + odd).astype(BF16)
     for j in range(GROUPS):
         out[j] = total
 
@@ -265,9 +274,8 @@
     q_rows, k_rows, v_rows, g_rows, r_rows = queries[0], keys[0], values[0], grad_out[0], residual[0]
     lat_own = latents[0, 0]
     lat_oth = swapped(lat_own)
-    g_oth = swapped(g_rows)
-    lat_oth, g_oth, *rows = lax.optimization_barrier((lat_oth, g_oth, q_rows, k_rows, v_rows))
-    q_oth, k_oth, v_oth = [swapped(value) for value in rows]
+    lat_oth, g_send = lax.optimization_barrier((lat_oth, g_rows))
+    g_oth = swapped(g_send)
 
     struct = jax.ShapeDtypeStruct
     anywhere = pl.BlockSpec(memory_space=pl.ANY)
@@ -283,11 +291,21 @@
         )(*[place_near(value) for value in args])
 
     lat_spec = whole((32, SPAN))
-    payload, = call(
-        weight_body, scalars, (lat_own, place_near(lat_oth), w_first, w_second, g_rows, place_near(g_oth)),
-        [anywhere, near, anywhere, anywhere, anywhere, near], [near], [pltpu.VMEM((GROUPS, 9, 16, 128), BF16)],
-        scratch=[pltpu.VMEM((32, SPAN), BF16), pltpu.VMEM((32, CH), BF16), pltpu.VMEM((CH, WIDTH), BF16),
-                 pltpu.VMEM((ROWS, WIDTH), BF16), pltpu.SemaphoreType.DMA((4,))],
+    ready = call(
+        hidden_body, scalars, (lat_own, place_near(lat_oth), w_first, w_second, g_rows),
+        [anywhere, near, anywhere, anywhere, anywhere], [near] * 5,
+        [pltpu.VMEM((32, ROWS), BF16), pltpu.VMEM((CH, ROWS), BF16), pltpu.VMEM((CH, ROWS), F32),
+         pltpu.VMEM((CH, WIDTH), BF16), pltpu.VMEM((SPAN, WIDTH), BF16)],
+        scratch=[pltpu.VMEM((32, SPAN), BF16), pltpu.VMEM((32, CH), BF16), pltpu.SemaphoreType.DMA((4,))],
+        cost=pl.CostEstimate(flops=4_000_000_000, bytes_accessed=10_000_000, transcendentals=200_000),
+    )
+    g_oth, *rest = lax.optimization_barrier((g_oth, *ready, q_rows, k_rows, v_rows))
+    ready, rows = rest[:5], rest[5:]
+    q_oth, k_oth, v_oth = [swapped(value) for value in rows]
+    payload = call(
+        weight_body, scalars[:1], [place_near(value) for value in (*ready, g_oth)],
+        [near] * 6, anywhere, struct((GROUPS, 9, 16, 128), BF16),
+        scratch=[pltpu.VMEM((ROWS, WIDTH), BF16), pltpu.VMEM((GROUPS, 9, 16, 128), BF16), pltpu.SemaphoreType.DMA((2,))],
     )
     block = ("zl", "y", "x")
     q_oth, k_oth, v_oth, g_oth = [place_near(value) for value in (q_oth, k_oth, v_oth, g_oth)]
@@ -318,29 +336,19 @@
     width = HALF // parts
     half_spec = pl.BlockSpec((ROWS, width), lambda i, c, *_: (0, (1 - c[0]) * parts + i))
 
-    def placed(got, into):
+    def placed(after, got, into):
         count = len(got)
         return call(
-            place_body, scalars[:1], (*map(place_near, got), *into), [near] * count + [anywhere] * count, [half_spec] * count,
+            place_body, (after,), (*map(place_near, got), *into), [near] * count + [anywhere] * count, [half_spec] * count,
             [big] * count, grid=(parts,), aliases={1 + count + i: i for i in range(count)},
         )
 
-    def exchanged(value, turn):
-        pairs = []
-        for z in range(4):
-            for core in range(2):
-                other = (z + 2) % 4 if core == turn else z ^ 1
-                pairs.append((2 * z + core, 2 * other + core))
-        return lax.ppermute(value, ("zh", "ctx"), pairs)
-
     one, = near_call(group_sum_body, (got,), [(9, 16, 128)])
-    two = exchanged(one, 0)
-    one, = near_call(pair_sum_body, (one, two), [(9, 16, 128)])
-    one, sent_dq, sent_dk, sent_dv = lax.optimization_barrier((one, sent_dq, sent_dk, sent_dv))
-    two = exchanged(one, 1)
-    dq, dk, dv = placed((sent_dq, sent_dk, sent_dv), (dq, dk, dv))
-    two, dq, dk, dv = lax.optimization_barrier((two, dq, dk, dv))
-    sums, = near_call(spread_sum_body, (one, two), [(GROUPS, 9, 16, 128)])
+    one, after = lax.optimization_barrier((one, scalars[0]))
+    others = [lax.ppermute(one, "zh", [(z, (z + s) % 4) for z in range(4)]) for s in (1, 2, 3)]
+    dq, dk, dv = placed(after, (sent_dq, sent_dk, sent_dv), (dq, dk, dv))
+    *others, dq, dk, dv = lax.optimization_barrier((*others, dq, dk, dv))
+    sums, = near_call(spread_sum_body, (one, *others), [(GROUPS, 9, 16, 128)])
     sums, sent_att = lax.optimization_barrier((sums, sent_att))
     got = lax.all_to_all(sums, block, 0, 0, tiled=False)
     sum_second, sum_first = pl.pallas_call(

time: 72.8 us -> 72.1 us (level)
    ppermute x9, waiting for transfers between devices: 2.39 us -> 1.58 us  [swapped(): return lax.ppermute(value, 'ctx', swap)]
    ppermute x2 -> x3, waiting for transfers between devices: 2.7 us -> 3.13 us  [local(): lax.ppermute(one, 'zh', [(z, (z + s) % 4) for z in range(4)])]
    pallas_call x4 -> x5, Pallas kernels: 20.1 us -> 20.4 us  [call(): pl.pallas_call(body, grid_spec=pltpu.PrefetchScalarGridSpec(num_scalar_pr...]
    ppermute x2 -> x3, starting transfers between devices: 9.37 us -> 9.3 us  [local(): lax.ppermute(one, 'zh', [(z, (z + s) % 4) for z in range(4)])]
  transfers between devices with their start and end apart: 13 -> 14, of which waited for: 5 -> 6; matrix products, arithmetic and copies ran while one was open for 0% -> 0% of each run, Pallas kernels for 30% -> 30%
where the time goes in v8:
time: 72.1 us; the launch traced here: 71.8 us
  starting transfers between devices  25.2 us (35%)
  Pallas kernels  23.1 us (32%)
  waiting for transfers between devices  22.8 us (32%)
  between operations  0.73 us (1%)
    pallas_call x5, Pallas kernels, call(): pl.pallas_call(body, grid_spec=pltpu.PrefetchScalarGridSpec(num_scalar_pr...  20.4 us
    all_to_all x1, waiting for transfers between devices, local(): got = lax.all_to_all(sums, block, 0, 0, tiled=False)  12.4 us
    ppermute x3, starting transfers between devices, local(): lax.ppermute(one, 'zh', [(z, (z + s) % 4) for z in range(4)])  9.3 us
    all_to_all x1, starting transfers between devices, local(): got = lax.all_to_all(payload, block, 0, 0, tiled=False)  8.56 us
    all_to_all x1, waiting for transfers between devices, local(): got = lax.all_to_all(payload, block, 0, 0, tiled=False)  5.72 us
    all_to_all x1, starting transfers between devices, local(): got = lax.all_to_all(sums, block, 0, 0, tiled=False)  5.2 us
    ppermute x3, waiting for transfers between devices, local(): lax.ppermute(one, 'zh', [(z, (z + s) % 4) for z in range(4)])  3.13 us
    ppermute x9, starting transfers between devices, swapped(): return lax.ppermute(value, 'ctx', swap)  2.12 us
  transfers between devices with their start and end apart: 14, of which 6 were waited for; matrix products, arithmetic and copies ran while one was open for 0% of the time, Pallas kernels for 30%

profile of v8, /device:TPU:32, one launch (start us, length us, event | category | flops | bytes accessed | tf_op | source)
XLA Modules:
  0.0 71.8 jit_solution(7410807671893475712)
XLA Ops:
  0.7 1.4 %collective-permute-done.lat_oth = bf16[32,128]{1,0:T(8,128)(2,1)S(1)} collective-permute-done((bf16[32,128]{1,0:T(8,128)(2,1)}, bf16[32,128]{1,0:T(8,128)(2,1)S(1)}, u32[]{:S(2)}, u32[]{:S(2)}) %collective-permute-start) | collective-permute-done | bytes 8224 | tf_op jit(solution)/shard_map/ppermute | solution.py:272
  2.1 0.2 collective-permute-start.1
  2.3 2.5 %shard_map.136 = (bf16[32,256]{1,0:T(8,128)(2,1)S(1)}, bf16[512,256]{1,0:T(8,128)(2,1)S(1)}, f32[512,256]{1,0:T(8,128)S(1)}, bf16[512,2048]{1,0:T(8,128)(2,1)S(1)}, bf16[128,2048]{1,0:T(8,128)(2,1)S(1)}) custom-call(s32[1]{0:T(128)} %bitcast.ctx_ref, s32[2]{0:T(128)} %bitcast.22, bf16[32,128]{1,0:T(8,128)(2,1)} %bitcast.19, ...), custom_call_target="tpu_custom_call" | custom-call | flops 4000000000 | bytes 10000000 | tf_op jit(solution)/shard_map/pallas_call | solution.py:36
  4.8 0.2 collective-permute-done.1.g_oth
  5.0 0.2 collective-permute-start.5
  5.2 0.3 collective-permute-start.6
  5.5 0.2 collective-permute-start.7
  5.7 2.1 %shard_map.137 = bf16[32,9,16,128]{3,2,1,0:T(8,128)(2,1)} custom-call(s32[1]{0:T(128)} %bitcast.ctx_ref, bf16[32,256]{1,0:T(8,128)(2,1)S(1)} %get-tuple-element.52.patches, bf16[512,256]{1,0:T(8,128)(2,1)S(1)} %get-tuple-element.53.hid_t, f32[512,256]{1,0:T(8,128)S(1)} %get-tuple-element.54.gate, bf16[512,2048]{1,0:T(8,128)(2,1)S(1)} %get-tuple-element.55.w2, ...), custom_call_target="tpu_custom_call" | custom-call | tf_op jit(solution)/shard_map/pallas_call | solution.py:36
  7.9 8.6 %all-to-all-start = ((bf16[32,9,16,128]{3,2,1,0:T(8,128)(2,1)}), bf16[32,9,16,128]{3,2,1,0:T(8,128)(2,1)S(1)}, u32[]{:S(2)}, u32[]{:S(2)}) async-start(bf16[32,9,16,128]{3,2,1,0:T(8,128)(2,1)} %shard_map.137), calls=%async_computation | async-start | bytes 2359296 | tf_op jit(solution)/shard_map/all_to_all | solution.py:312
  16.5 11.2 %shard_map.139 = (bf16[256,2048]{1,0:T(8,128)(2,1)}, bf16[256,2048]{1,0:T(8,128)(2,1)}, bf16[256,2048]{1,0:T(8,128)(2,1)}, bf16[256,2048]{1,0:T(8,128)(2,1)}, bf...) custom-call(s32[1]{0:T(128)} %bitcast.ctx_ref, ...), custom_call_target="tpu_custom_call" | custom-call | flops 40000000000 | bytes 100000000 | tf_op jit(solution)/shard_map/pallas_call | solution.py:36
  27.8 0.5 collective-permute-start.9
  28.4 0.4 collective-permute-start.11
  28.8 5.7 %all-to-all-done.got = bf16[32,9,16,128]{3,2,1,0:T(8,128)(2,1)S(1)} async-done(((bf16[32,9,16,128]{3,2,1,0:T(8,128)(2,1)}), bf16[32,9,16,128]{3,2,1,0:T(8,128)(2,1)S(1)}, u32[]{:S(2)}, u32[]{:S(2)}) %all-to-all-start) | async-done | bytes 1179680 | tf_op jit(solution)/shard_map/all_to_all | solution.py:312
  34.7 5.5 %collective-permute-start.4 = (bf16[9,16,128]{2,1,0:T(8,128)(2,1)S(1)}, bf16[9,16,128]{2,1,0:T(8,128)(2,1)S(1)}, u32[]{:S(2)}, u32[]{:S(2)}) collective-permute-start(bf16[9,16,128]{2,1,0:T(8,128)(2,1)S(1)} %shard_map.138.one), channel_id=1, source_target_pairs={{0,192},{64,0},{128,64},{192,128},{1,193},{65,1},{129,65},{193,129... | collective-permute-start | bytes 110600 | tf_op jit(solution)/shard_map/ppermute | solution.py:348
  40.2 1.4 %collective-permute-start.3 = (bf16[9,16,128]{2,1,0:T(8,128)(2,1)S(1)}, bf16[9,16,128]{2,1,0:T(8,128)(2,1)S(1)}, u32[]{:S(2)}, u32[]{:S(2)}) collective-permute-start(bf16[9,16,128]{2,1,0:T(8,128)(2,1)S(1)} %shard_map.138.one), channel_id=1, source_target_pairs={{0,128},{64,192},{128,0},{192,64},{1,129},{65,193},{129,1},{193,65... | collective-permute-start | bytes 110600 | tf_op jit(solution)/shard_map/ppermute | solution.py:348
  41.6 2.4 %collective-permute-start.2 = (bf16[9,16,128]{2,1,0:T(8,128)(2,1)S(1)}, bf16[9,16,128]{2,1,0:T(8,128)(2,1)S(1)}, u32[]{:S(2)}, u32[]{:S(2)}) collective-permute-start(bf16[9,16,128]{2,1,0:T(8,128)(2,1)S(1)} %shard_map.138.one), channel_id=1, source_target_pairs={{0,64},{64,128},{128,192},{192,0},{1,65},{65,129},{129,193},{193,1... | collective-permute-start | bytes 110600 | tf_op jit(solution)/shard_map/ppermute | solution.py:348
  44.0 1.2 %shard_map.140 = (bf16[256,2048]{1,0:T(8,128)(2,1)}, bf16[256,2048]{1,0:T(8,128)(2,1)}, bf16[256,2048]{1,0:T(8,128)(2,1)}) custom-call(s32[1]{0:T(128)} %bitcast.ctx_ref, bf16[256,1024]{1,0:T(8,128)(2,1)S(1)} %collective-permute-done.8.refs_0_, ...), custom_call_target="tpu_custom_call", output_to_operand_aliasing={{0}: (4, {}), {1}: (5, {}), {2}: (6, {})} | custom-call | tf_op jit(solution)/shard_map/pallas_call | solution.py:36
  45.2 2.9 %collective-permute-done.3.next2 = bf16[9,16,128]{2,1,0:T(8,128)(2,1)S(1)} collective-permute-done((bf16[9,16,128]{2,1,0:T(8,128)(2,1)S(1)}, bf16[9,16,128]{2,1,0:T(8,128)(2,1)S(1)}, u32[]{:S(2)}, u32[]{:S(2)}) %collective-permute-start.3) | collective-permute-done | bytes 36896 | tf_op jit(solution)/shard_map/ppermute | solution.py:348
  48.0 0.3 collective-permute-done.2.next1
  48.3 1.1 %shard_map.141 = bf16[32,9,16,128]{3,2,1,0:T(8,128)(2,1)} custom-call(bf16[9,16,128]{2,1,0:T(8,128)(2,1)S(1)} %shard_map.138.one, bf16[9,16,128]{2,1,0:T(8,128)(2,1)S(1)} %collective-permute-done.2.next1, bf16[9,16,128]{2,1,0:T(8,128)(2,1)S(1)} %collective-permute-done.3.next2, bf16[9,16,128]{2,1,0:T(8,128)(2,1)S(1)} %collective-permute-done.4.next3), custom_call_target="tpu_custom_call" | custom-call | tf_op jit(solution)/shard_map/pallas_call | solution.py:288
  49.4 5.2 %all-to-all-start.1 = ((bf16[32,9,16,128]{3,2,1,0:T(8,128)(2,1)}), bf16[32,9,16,128]{3,2,1,0:T(8,128)(2,1)S(1)}, u32[]{:S(2)}, u32[]{:S(2)}) async-start(bf16[32,9,16,128]{3,2,1,0:T(8,128)(2,1)} %shard_map.141), calls=%async_computation.1 | async-start | bytes 2359296 | tf_op jit(solution)/shard_map/all_to_all | solution.py:353
  54.6 3.4 %shard_map.142 = bf16[256,2048]{1,0:T(8,128)(2,1)} custom-call(s32[1]{0:T(128)} %bitcast.ctx_ref, s32[2]{0:T(128)} %bitcast.24, bf16[256,2048]{1,0:T(8,128)(2,1)} %bitcast.13, bf16[32,128]{1,0:T(8,128)(2,1)} %bitcast.21, bf16[32,128]{1,0:T(8,128)(2,1)} %copy-done, bf16[32,512]{1,0:T(8,128)(2,1)} %w1.3, ...), custom_call_target="tpu_custom_call", output_to_operand_aliasing={{}: (8, {})} | custom-call | tf_op jit(solution)/shard_map/pallas_call | solution.py:36
  58.0 12.4 %all-to-all-done.1.got = bf16[32,9,16,128]{3,2,1,0:T(8,128)(2,1)S(1)} async-done(((bf16[32,9,16,128]{3,2,1,0:T(8,128)(2,1)}), bf16[32,9,16,128]{3,2,1,0:T(8,128)(2,1)S(1)}, u32[]{:S(2)}, u32[]{:S(2)}) %all-to-all-start.1) | async-done | bytes 1179680 | tf_op jit(solution)/shard_map/all_to_all | solution.py:353
  70.4 1.4 %shard_map.143 = (f32[512,1024]{1,0:T(8,128)}, f32[32,512]{1,0:T(8,128)}) custom-call(bf16[32,9,16,128]{3,2,1,0:T(8,128)(2,1)S(1)} %all-to-all-done.1.got), custom_call_target="tpu_custom_call" | custom-call | tf_op jit(solution)/shard_map/pallas_call | solution.py:354
  (14 shorter events, 0.5 us)
Async XLA Ops:
  0.6 1.5 %collective-permute-start = (bf16[32,128]{1,0:T(8,128)(2,1)}, bf16[32,128]{1,0:T(8,128)(2,1)S(1)}, u32[]{:S(2)}, u32[]{:S(2)}) collective-permute-start(bf16[32,128]{1,0:T(8,128)(2,1)} %bitcast.18), channel_id=1, source_target_pairs={{0,1},{1,0},{2,3},{3,2},{4,5},{5,4},{6,7},{7,6},{8,9},{9,8},{10,11... | collective-permute-start | bytes 24584 | tf_op jit(solution)/shard_map/ppermute | solution.py:272
  2.1 2.7 %copy-start = (bf16[32,128]{1,0:T(8,128)(2,1)}, bf16[32,128]{1,0:T(8,128)(2,1)S(1)}, u32[]{:S(2)}) copy-start(bf16[32,128]{1,0:T(8,128)(2,1)S(1)} %collective-permute-done.lat_oth) | copy-start | bytes 24580
  2.1 2.9 %collective-permute-start.1 = (bf16[256,2048]{1,0:T(8,128)(2,1)}, bf16[256,2048]{1,0:T(8,128)(2,1)S(1)}, u32[]{:S(2)}, u32[]{:S(2)}) collective-permute-start(bf16[256,2048]{1,0:T(8,128)(2,1)} %bitcast.25), channel_id=1, source_target_pairs={{0,1},{1,0},{2,3},{3,2},{4,5},{5,4},{6,7},{7,6},{8,9},{9,8},{10,11... | collective-permute-start | bytes 3145736 | tf_op jit(solution)/shard_map/ppermute | solution.py:272
  5.0 11.5 %collective-permute-start.5 = (bf16[256,2048]{1,0:T(8,128)(2,1)}, bf16[256,2048]{1,0:T(8,128)(2,1)}, u32[]{:S(2)}, u32[]{:S(2)}) collective-permute-start(bf16[256,2048]{1,0:T(8,128)(2,1)} %bitcast.5.q_own), channel_id=1, source_target_pairs={{0,1},{1,0},{2,3},{3,2},{4,5},{5,4},{6,7},{7,6},{8,9},{9,8},{10,11... | collective-permute-start | bytes 3145736 | tf_op jit(solution)/shard_map/ppermute | solution.py:272
  5.2 11.2 %collective-permute-start.6 = (bf16[256,2048]{1,0:T(8,128)(2,1)}, bf16[256,2048]{1,0:T(8,128)(2,1)}, u32[]{:S(2)}, u32[]{:S(2)}) collective-permute-start(bf16[256,2048]{1,0:T(8,128)(2,1)} %bitcast.6.k_own), channel_id=1, source_target_pairs={{0,1},{1,0},{2,3},{3,2},{4,5},{5,4},{6,7},{7,6},{8,9},{9,8},{10,11... | collective-permute-start | bytes 3145736 | tf_op jit(solution)/shard_map/ppermute | solution.py:272
  5.5 11.0 %collective-permute-start.7 = (bf16[256,2048]{1,0:T(8,128)(2,1)}, bf16[256,2048]{1,0:T(8,128)(2,1)}, u32[]{:S(2)}, u32[]{:S(2)}) collective-permute-start(bf16[256,2048]{1,0:T(8,128)(2,1)} %bitcast.7.v_own), channel_id=1, source_target_pairs={{0,1},{1,0},{2,3},{3,2},{4,5},{5,4},{6,7},{7,6},{8,9},{9,8},{10,11... | collective-permute-start | bytes 3145736 | tf_op jit(solution)/shard_map/ppermute | solution.py:272
  7.9 26.6 %all-to-all-start = ((bf16[32,9,16,128]{3,2,1,0:T(8,128)(2,1)}), bf16[32,9,16,128]{3,2,1,0:T(8,128)(2,1)S(1)}, u32[]{:S(2)}, u32[]{:S(2)}) async-start(bf16[32,9,16,128]{3,2,1,0:T(8,128)(2,1)} %shard_map.137), calls=%async_computation | async-start | bytes 2359296 | tf_op jit(solution)/shard_map/all_to_all | solution.py:312
  27.7 12.5 %collective-permute-start.8 = (bf16[256,1024]{1,0:T(8,128)(2,1)}, bf16[256,1024]{1,0:T(8,128)(2,1)S(1)}, u32[]{:S(2)}, u32[]{:S(2)}) collective-permute-start(bf16[256,1024]{1,0:T(8,128)(2,1)} %get-tuple-element.63), channel_id=1, source_target_pairs={{0,1},{1,0},{2,3},{3,2},{4,5},{5,4},{6,7},{7,6},{8,9},{9,8},{10,11... | collective-permute-start | bytes 1572872 | tf_op jit(solution)/shard_map/ppermute | solution.py:272
  27.8 13.8 %collective-permute-start.9 = (bf16[256,1024]{1,0:T(8,128)(2,1)}, bf16[256,1024]{1,0:T(8,128)(2,1)S(1)}, u32[]{:S(2)}, u32[]{:S(2)}) collective-permute-start(bf16[256,1024]{1,0:T(8,128)(2,1)} %get-tuple-element.64), channel_id=1, source_target_pairs={{0,1},{1,0},{2,3},{3,2},{4,5},{5,4},{6,7},{7,6},{8,9},{9,8},{10,11... | collective-permute-start | bytes 1572872 | tf_op jit(solution)/shard_map/ppermute | solution.py:272
  28.3 15.7 %collective-permute-start.10 = (bf16[256,1024]{1,0:T(8,128)(2,1)}, bf16[256,1024]{1,0:T(8,128)(2,1)S(1)}, u32[]{:S(2)}, u32[]{:S(2)}) collective-permute-start(bf16[256,1024]{1,0:T(8,128)(2,1)} %get-tuple-element.65), channel_id=1, source_target_pairs={{0,1},{1,0},{2,3},{3,2},{4,5},{5,4},{6,7},{7,6},{8,9},{9,8},{10,11... | collective-permute-start | bytes 1572872 | tf_op jit(solution)/shard_map/ppermute | solution.py:272
  28.4 21.0 %collective-permute-start.11 = (bf16[256,1024]{1,0:T(8,128)(2,1)}, bf16[256,1024]{1,0:T(8,128)(2,1)S(1)}, u32[]{:S(2)}, u32[]{:S(2)}) collective-permute-start(bf16[256,1024]{1,0:T(8,128)(2,1)} %get-tuple-element.75), channel_id=1, source_target_pairs={{0,1},{1,0},{2,3},{3,2},{4,5},{5,4},{6,7},{7,6},{8,9},{9,8},{10,11... | collective-permute-start | bytes 1572872 | tf_op jit(solution)/shard_map/ppermute | solution.py:272
  34.7 10.5 %collective-permute-start.4 = (bf16[9,16,128]{2,1,0:T(8,128)(2,1)S(1)}, bf16[9,16,128]{2,1,0:T(8,128)(2,1)S(1)}, u32[]{:S(2)}, u32[]{:S(2)}) collective-permute-start(bf16[9,16,128]{2,1,0:T(8,128)(2,1)S(1)} %shard_map.138.one), channel_id=1, source_target_pairs={{0,192},{64,0},{128,64},{192,128},{1,193},{65,1},{129,65},{193,129... | collective-permute-start | bytes 110600 | tf_op jit(solution)/shard_map/ppermute | solution.py:348
  40.2 7.9 %collective-permute-start.3 = (bf16[9,16,128]{2,1,0:T(8,128)(2,1)S(1)}, bf16[9,16,128]{2,1,0:T(8,128)(2,1)S(1)}, u32[]{:S(2)}, u32[]{:S(2)}) collective-permute-start(bf16[9,16,128]{2,1,0:T(8,128)(2,1)S(1)} %shard_map.138.one), channel_id=1, source_target_pairs={{0,128},{64,192},{128,0},{192,64},{1,129},{65,193},{129,1},{193,65... | collective-permute-start | bytes 110600 | tf_op jit(solution)/shard_map/ppermute | solution.py:348
  41.6 6.7 %collective-permute-start.2 = (bf16[9,16,128]{2,1,0:T(8,128)(2,1)S(1)}, bf16[9,16,128]{2,1,0:T(8,128)(2,1)S(1)}, u32[]{:S(2)}, u32[]{:S(2)}) collective-permute-start(bf16[9,16,128]{2,1,0:T(8,128)(2,1)S(1)} %shard_map.138.one), channel_id=1, source_target_pairs={{0,64},{64,128},{128,192},{192,0},{1,65},{65,129},{129,193},{193,1... | collective-permute-start | bytes 110600 | tf_op jit(solution)/shard_map/ppermute | solution.py:348
  49.4 20.9 %all-to-all-start.1 = ((bf16[32,9,16,128]{3,2,1,0:T(8,128)(2,1)}), bf16[32,9,16,128]{3,2,1,0:T(8,128)(2,1)S(1)}, u32[]{:S(2)}, u32[]{:S(2)}) async-start(bf16[32,9,16,128]{3,2,1,0:T(8,128)(2,1)} %shard_map.141), calls=%async_computation.1 | async-start | bytes 2359296 | tf_op jit(solution)/shard_map/all_to_all | solution.py:353

commit v9 on v8

--- a/solution.py
+++ b/solution.py
@@ -65,35 +65,41 @@
     return jnp.where(in_order, one, two).astype(BF16), jnp.where(in_order, two, one).astype(BF16)
 
 
-def hidden_body(ctx_ref, starts, lat_hbm, lat_oth, w1_hbm, w2_hbm, g_own, patches, hid_t, gate, w2, grads, lat_own, w1, sems):
+def hidden_and_gate(w1, lat):
+    pre = dot(w1, lat, 0, 0)
+    sig = sigmoid(pre)
+    return (pre * sig).astype(BF16), sig * (1.0 + pre * (1.0 - sig))
+
+
+def hidden_body(ctx_ref, lat_hbm, w1_hbm, w2_hbm, g_own, lat, w1, hid_t, gate, w2, grads, sems):
     own_rows = pl.ds(pl.multiple_of(ctx_ref[0] * SPAN, SPAN), SPAN)
     copies = [
         pltpu.make_async_copy(source, target, sems.at[i])
         for i, (source, target) in enumerate((
-            (lat_hbm, lat_own), (w1_hbm, w1), (g_own.at[own_rows, :], grads), (w2_hbm, w2)))
+            (lat_hbm, lat), (w1_hbm, w1), (g_own.at[own_rows, :], grads), (w2_hbm, w2)))
     ]
     for copy in copies:
         copy.start()
     copies[0].wait()
     copies[1].wait()
-    both = jnp.concatenate(pick(starts, lat_own, lat_oth), axis=1)
-    pre = dot(w1[...], both, 0, 0)
-    sig = sigmoid(pre)
-    patches[...] = both
-    hid_t[...] = (pre * sig).astype(BF16)
-    gate[...] = sig * (1.0 + pre * (1.0 - sig))
+    hid_t[...], gate[...] = hidden_and_gate(w1[...], lat[...])
     copies[2].wait()
     copies[3].wait()
 
 
-def weight_body(ctx_ref, patches, hid_t, gate, w2, g_own, g_oth, out, grads, tiles, sems):
+def weight_body(ctx_ref, starts, lat_own, w1, hid_own, gate_own, w2, g_own, lat_oth, g_oth, out, grads, tiles, sems):
     ctx = ctx_ref[0]
     oth_rows = pl.ds(pl.multiple_of(SPAN - ctx * SPAN, SPAN), SPAN)
-    grads[0:SPAN, :] = g_own[...]
-    grads[SPAN:ROWS, :] = g_oth[oth_rows, :]
+    place = pl.multiple_of(jnp.where(starts[0] == 0, 0, SPAN), SPAN)
+    grads[pl.ds(place, SPAN), :] = g_own[...]
+    grads[pl.ds(pl.multiple_of(SPAN - place, SPAN), SPAN), :] = g_oth[oth_rows, :]
+    hid_oth, gate_oth = hidden_and_gate(w1[...], lat_oth[...])
+    hid_t = jnp.concatenate([hid_own[...], hid_oth], axis=1)
+    gate = jnp.concatenate([gate_own[...], gate_oth], axis=1)
+    patches = jnp.concatenate([lat_own[...], lat_oth[...]], axis=1)
     for n in range(4):
         half = grads[:, pl.ds(pl.multiple_of(ctx * HALF, HALF) + 256 * n, 256)]
-        strip = dot(hid_t[...], half, 1, 0).astype(BF16)
+        strip = dot(hid_t, half, 1, 0).astype(BF16)
         for j in range(GROUPS):
             for i in range(2):
                 tiles[j, 2 * n + i] = strip[16 * j : 16 * j + 16, 128 * i : 128 * i + 128]
@@ -101,8 +107,8 @@
     copies = [pltpu.make_async_copy(tiles.at[:, part], out.at[:, part], sems.at[i]) for i, part in enumerate((main, rest))]
     copies[0].start()
     back = dot(w2[...], grads[...], 1, 1)
-    grad_pre = (back * gate[...]).astype(BF16)
-    first = dot(patches[...], grad_pre, 1, 1).astype(BF16)
+    grad_pre = (back * gate).astype(BF16)
+    first = dot(patches, grad_pre, 1, 1).astype(BF16)
     for j in range(GROUPS):
         m = j // 4
         tiles[j, 8] = first[16 * (m // 4) : 16 * (m // 4) + 16, 128 * (m % 4) : 128 * (m % 4) + 128]
@@ -128,17 +134,17 @@
 
 def finish_body(got, second, first, second_near, first_near, sems):
     copies = []
-    for n in range(4):
-        for j in range(8 * n, 8 * n + 8):
+    for n in range(8):
+        for j in range(4 * n, 4 * n + 4):
             for t in range(8):
                 second_near[16 * j : 16 * j + 16, 128 * t : 128 * t + 128] = got[j, t].astype(F32) * (1.0 / 128.0)
-        part = pl.ds(128 * n, 128)
+        part = pl.ds(64 * n, 64)
         copies.append(pltpu.make_async_copy(second_near.at[part, :], second.at[part, :], sems.at[n]))
         copies[-1].start()
     for m in range(8):
         rows, cols = 16 * (m // 4), 128 * (m % 4)
         first_near[rows : rows + 16, cols : cols + 128] = got[4 * m, 8].astype(F32) * (1.0 / 128.0)
-    copies.append(pltpu.make_async_copy(first_near, first, sems.at[4]))
+    copies.append(pltpu.make_async_copy(first_near, first, sems.at[8]))
     copies[-1].start()
     for copy in copies:
         copy.wait()
@@ -274,8 +280,7 @@
     q_rows, k_rows, v_rows, g_rows, r_rows = queries[0], keys[0], values[0], grad_out[0], residual[0]
     lat_own = latents[0, 0]
     lat_oth = swapped(lat_own)
-    lat_oth, g_send = lax.optimization_barrier((lat_oth, g_rows))
-    g_oth = swapped(g_send)
+    g_oth = swapped(g_rows)
 
     struct = jax.ShapeDtypeStruct
     anywhere = pl.BlockSpec(memory_space=pl.ANY)
@@ -292,19 +297,18 @@
 
     lat_spec = whole((32, SPAN))
     ready = call(
-        hidden_body, scalars, (lat_own, place_near(lat_oth), w_first, w_second, g_rows),
-        [anywhere, near, anywhere, anywhere, anywhere], [near] * 5,
-        [pltpu.VMEM((32, ROWS), BF16), pltpu.VMEM((CH, ROWS), BF16), pltpu.VMEM((CH, ROWS), F32),
+        hidden_body, scalars[:1], (lat_own, w_first, w_second, g_rows), [anywhere] * 4, [near] * 6,
+        [pltpu.VMEM((32, SPAN), BF16), pltpu.VMEM((32, CH), BF16), pltpu.VMEM((CH, SPAN), BF16), pltpu.VMEM((CH, SPAN), F32),
          pltpu.VMEM((CH, WIDTH), BF16), pltpu.VMEM((SPAN, WIDTH), BF16)],
-        scratch=[pltpu.VMEM((32, SPAN), BF16), pltpu.VMEM((32, CH), BF16), pltpu.SemaphoreType.DMA((4,))],
+        scratch=[pltpu.SemaphoreType.DMA((4,))],
         cost=pl.CostEstimate(flops=4_000_000_000, bytes_accessed=10_000_000, transcendentals=200_000),
     )
-    g_oth, *rest = lax.optimization_barrier((g_oth, *ready, q_rows, k_rows, v_rows))
-    ready, rows = rest[:5], rest[5:]
+    lat_oth, g_oth, *rest = lax.optimization_barrier((lat_oth, g_oth, *ready, q_rows, k_rows, v_rows))
+    ready, rows = rest[:6], rest[6:]
     q_oth, k_oth, v_oth = [swapped(value) for value in rows]
     payload = call(
-        weight_body, scalars[:1], [place_near(value) for value in (*ready, g_oth)],
-        [near] * 6, anywhere, struct((GROUPS, 9, 16, 128), BF16),
+        weight_body, scalars, [place_near(value) for value in (*ready, lat_oth, g_oth)],
+        [near] * 8, anywhere, struct((GROUPS, 9, 16, 128), BF16),
         scratch=[pltpu.VMEM((ROWS, WIDTH), BF16), pltpu.VMEM((GROUPS, 9, 16, 128), BF16), pltpu.SemaphoreType.DMA((2,))],
     )
     block = ("zl", "y", "x")
@@ -354,7 +358,7 @@
     sum_second, sum_first = pl.pallas_call(
         finish_body, in_specs=[near], out_specs=[anywhere, anywhere],
         out_shape=[struct((CH, HALF), F32), struct((32, CH), F32)],
-        scratch_shapes=[pltpu.VMEM((CH, HALF), F32), pltpu.VMEM((32, CH), F32), pltpu.SemaphoreType.DMA((5,))],
+        scratch_shapes=[pltpu.VMEM((CH, HALF), F32), pltpu.VMEM((32, CH), F32), pltpu.SemaphoreType.DMA((9,))],
         compiler_params=pltpu.CompilerParams(vmem_limit_bytes=VMEM),
     )(place_near(got))
 

time: 72.1 us -> 71.4 us (level)
  waiting for transfers between devices: 22.8 us -> 21.9 us
    ppermute x9, waiting for transfers between devices: 1.58 us -> 0.56 us  [swapped(): return lax.ppermute(value, 'ctx', swap)]
  transfers between devices with their start and end apart: 14 -> 14, of which waited for: 6 -> 5; matrix products, arithmetic and copies ran while one was open for 0% -> 0% of each run, Pallas kernels for 30% -> 30%
where the time goes in v9:
time: 71.4 us; the launch traced here: 71 us
  starting transfers between devices  25.3 us (35%)
  Pallas kernels  23.1 us (32%)
  waiting for transfers between devices  21.9 us (31%)
  between operations  0.73 us (1%)
    pallas_call x5, Pallas kernels, call(): pl.pallas_call(body, grid_spec=pltpu.PrefetchScalarGridSpec(num_scalar_pr...  20.4 us
    all_to_all x1, waiting for transfers between devices, local(): got = lax.all_to_all(sums, block, 0, 0, tiled=False)  12.3 us
    ppermute x3, starting transfers between devices, local(): lax.ppermute(one, 'zh', [(z, (z + s) % 4) for z in range(4)])  9.29 us
    all_to_all x1, starting transfers between devices, local(): got = lax.all_to_all(payload, block, 0, 0, tiled=False)  8.58 us
    all_to_all x1, waiting for transfers between devices, local(): got = lax.all_to_all(payload, block, 0, 0, tiled=False)  5.81 us
    all_to_all x1, starting transfers between devices, local(): got = lax.all_to_all(sums, block, 0, 0, tiled=False)  5.13 us
    ppermute x3, waiting for transfers between devices, local(): lax.ppermute(one, 'zh', [(z, (z + s) % 4) for z in range(4)])  3.21 us
    ppermute x9, starting transfers between devices, swapped(): return lax.ppermute(value, 'ctx', swap)  2.34 us
  transfers between devices with their start and end apart: 14, of which 5 were waited for; matrix products, arithmetic and copies ran while one was open for 0% of the time, Pallas kernels for 30%

profile of v9, /device:TPU:32, one launch (start us, length us, event | category | flops | bytes accessed | tf_op | source)
XLA Modules:
  0.0 71.0 jit_solution(15178039380721949120)
XLA Ops:
  0.7 0.5 collective-permute-start
  1.2 1.8 %shard_map.136 = (bf16[32,128]{1,0:T(8,128)(2,1)S(1)}, bf16[32,512]{1,0:T(8,128)(2,1)S(1)}, bf16[512,128]{1,0:T(8,128)(2,1)S(1)}, f32[512,128]{1,0:T(8,128)S(1)}...) custom-call(s32[1]{0:T(128)} %bitcast.ctx_ref, bf16[32,128]{1,0:T(8,128)(2,1)} %bitcast.19, ...), custom_call_target="tpu_custom_call" | custom-call | flops 4000000000 | bytes 10000000 | tf_op jit(solution)/shard_map/pallas_call | solution.py:36
  3.1 0.5 collective-permute-done.lat_oth
  3.6 0.1 collective-permute-start.5
  3.7 0.4 collective-permute-start.6
  4.1 0.1 collective-permute-start.7
  4.3 2.8 %shard_map.137 = bf16[32,9,16,128]{3,2,1,0:T(8,128)(2,1)} custom-call(s32[1]{0:T(128)} %bitcast.ctx_ref, s32[2]{0:T(128)} %bitcast.22, bf16[32,128]{1,0:T(8,128)(2,1)S(1)} %get-tuple-element.53.lat_own, bf16[32,512]{1,0:T(8,128)(2,1)S(1)} %get-tuple-element.54.w1, bf16[512,128]{1,0:T(8,128)(2,1)S(1)} %get-tuple-element.55.hid_own, ...), custom_call_target="tpu_custom_call" | custom-call | tf_op jit(solution)/shard_map/pallas_call | solution.py:36
  7.0 8.6 %all-to-all-start = ((bf16[32,9,16,128]{3,2,1,0:T(8,128)(2,1)}), bf16[32,9,16,128]{3,2,1,0:T(8,128)(2,1)S(1)}, u32[]{:S(2)}, u32[]{:S(2)}) async-start(bf16[32,9,16,128]{3,2,1,0:T(8,128)(2,1)} %shard_map.137), calls=%async_computation | async-start | bytes 2359296 | tf_op jit(solution)/shard_map/all_to_all | solution.py:316
  15.7 11.2 %shard_map.139 = (bf16[256,2048]{1,0:T(8,128)(2,1)}, bf16[256,2048]{1,0:T(8,128)(2,1)}, bf16[256,2048]{1,0:T(8,128)(2,1)}, bf16[256,2048]{1,0:T(8,128)(2,1)}, bf...) custom-call(s32[1]{0:T(128)} %bitcast.ctx_ref, ...), custom_call_target="tpu_custom_call" | custom-call | flops 40000000000 | bytes 100000000 | tf_op jit(solution)/shard_map/pallas_call | solution.py:36
  27.0 0.5 collective-permute-start.9
  27.6 0.4 collective-permute-start.11
  28.0 5.8 %all-to-all-done.got = bf16[32,9,16,128]{3,2,1,0:T(8,128)(2,1)S(1)} async-done(((bf16[32,9,16,128]{3,2,1,0:T(8,128)(2,1)}), bf16[32,9,16,128]{3,2,1,0:T(8,128)(2,1)S(1)}, u32[]{:S(2)}, u32[]{:S(2)}) %all-to-all-start) | async-done | bytes 1179680 | tf_op jit(solution)/shard_map/all_to_all | solution.py:316
  33.8 0.2 shard_map.138.one
  34.0 5.5 %collective-permute-start.4 = (bf16[9,16,128]{2,1,0:T(8,128)(2,1)S(1)}, bf16[9,16,128]{2,1,0:T(8,128)(2,1)S(1)}, u32[]{:S(2)}, u32[]{:S(2)}) collective-permute-start(bf16[9,16,128]{2,1,0:T(8,128)(2,1)S(1)} %shard_map.138.one), channel_id=1, source_target_pairs={{0,192},{64,0},{128,64},{192,128},{1,193},{65,1},{129,65},{193,129... | collective-permute-start | bytes 110600 | tf_op jit(solution)/shard_map/ppermute | solution.py:352
  39.5 1.4 %collective-permute-start.3 = (bf16[9,16,128]{2,1,0:T(8,128)(2,1)S(1)}, bf16[9,16,128]{2,1,0:T(8,128)(2,1)S(1)}, u32[]{:S(2)}, u32[]{:S(2)}) collective-permute-start(bf16[9,16,128]{2,1,0:T(8,128)(2,1)S(1)} %shard_map.138.one), channel_id=1, source_target_pairs={{0,128},{64,192},{128,0},{192,64},{1,129},{65,193},{129,1},{193,65... | collective-permute-start | bytes 110600 | tf_op jit(solution)/shard_map/ppermute | solution.py:352
  40.9 2.4 %collective-permute-start.2 = (bf16[9,16,128]{2,1,0:T(8,128)(2,1)S(1)}, bf16[9,16,128]{2,1,0:T(8,128)(2,1)S(1)}, u32[]{:S(2)}, u32[]{:S(2)}) collective-permute-start(bf16[9,16,128]{2,1,0:T(8,128)(2,1)S(1)} %shard_map.138.one), channel_id=1, source_target_pairs={{0,64},{64,128},{128,192},{192,0},{1,65},{65,129},{129,193},{193,1... | collective-permute-start | bytes 110600 | tf_op jit(solution)/shard_map/ppermute | solution.py:352
  43.3 1.2 %shard_map.140 = (bf16[256,2048]{1,0:T(8,128)(2,1)}, bf16[256,2048]{1,0:T(8,128)(2,1)}, bf16[256,2048]{1,0:T(8,128)(2,1)}) custom-call(s32[1]{0:T(128)} %bitcast.ctx_ref, bf16[256,1024]{1,0:T(8,128)(2,1)S(1)} %collective-permute-done.8.refs_0_, ...), custom_call_target="tpu_custom_call", output_to_operand_aliasing={{0}: (4, {}), {1}: (5, {}), {2}: (6, {})} | custom-call | tf_op jit(solution)/shard_map/pallas_call | solution.py:36
  44.5 2.9 %collective-permute-done.3.next2 = bf16[9,16,128]{2,1,0:T(8,128)(2,1)S(1)} collective-permute-done((bf16[9,16,128]{2,1,0:T(8,128)(2,1)S(1)}, bf16[9,16,128]{2,1,0:T(8,128)(2,1)S(1)}, u32[]{:S(2)}, u32[]{:S(2)}) %collective-permute-start.3) | collective-permute-done | bytes 36896 | tf_op jit(solution)/shard_map/ppermute | solution.py:352
  47.3 0.4 collective-permute-done.2.next1
  47.7 1.1 %shard_map.141 = bf16[32,9,16,128]{3,2,1,0:T(8,128)(2,1)} custom-call(bf16[9,16,128]{2,1,0:T(8,128)(2,1)S(1)} %shard_map.138.one, bf16[9,16,128]{2,1,0:T(8,128)(2,1)S(1)} %collective-permute-done.2.next1, bf16[9,16,128]{2,1,0:T(8,128)(2,1)S(1)} %collective-permute-done.3.next2, bf16[9,16,128]{2,1,0:T(8,128)(2,1)S(1)} %collective-permute-done.4.next3), custom_call_target="tpu_custom_call" | custom-call | tf_op jit(solution)/shard_map/pallas_call | solution.py:293
  48.8 5.1 %all-to-all-start.1 = ((bf16[32,9,16,128]{3,2,1,0:T(8,128)(2,1)}), bf16[32,9,16,128]{3,2,1,0:T(8,128)(2,1)S(1)}, u32[]{:S(2)}, u32[]{:S(2)}) async-start(bf16[32,9,16,128]{3,2,1,0:T(8,128)(2,1)} %shard_map.141), calls=%async_computation.1 | async-start | bytes 2359296 | tf_op jit(solution)/shard_map/all_to_all | solution.py:357
  53.9 3.4 %shard_map.142 = bf16[256,2048]{1,0:T(8,128)(2,1)} custom-call(s32[1]{0:T(128)} %bitcast.ctx_ref, s32[2]{0:T(128)} %bitcast.24, bf16[256,2048]{1,0:T(8,128)(2,1)} %bitcast.13, bf16[32,128]{1,0:T(8,128)(2,1)} %bitcast.21, bf16[32,128]{1,0:T(8,128)(2,1)} %copy-done, bf16[32,512]{1,0:T(8,128)(2,1)} %w1.3, ...), custom_call_target="tpu_custom_call", output_to_operand_aliasing={{}: (8, {})} | custom-call | tf_op jit(solution)/shard_map/pallas_call | solution.py:36
  57.3 12.3 %all-to-all-done.1.got = bf16[32,9,16,128]{3,2,1,0:T(8,128)(2,1)S(1)} async-done(((bf16[32,9,16,128]{3,2,1,0:T(8,128)(2,1)}), bf16[32,9,16,128]{3,2,1,0:T(8,128)(2,1)S(1)}, u32[]{:S(2)}, u32[]{:S(2)}) %all-to-all-start.1) | async-done | bytes 1179680 | tf_op jit(solution)/shard_map/all_to_all | solution.py:357
  69.6 1.4 %shard_map.143 = (f32[512,1024]{1,0:T(8,128)}, f32[32,512]{1,0:T(8,128)}) custom-call(bf16[32,9,16,128]{3,2,1,0:T(8,128)(2,1)S(1)} %all-to-all-done.1.got), custom_call_target="tpu_custom_call" | custom-call | tf_op jit(solution)/shard_map/pallas_call | solution.py:358
  (14 shorter events, 0.3 us)
Async XLA Ops:
  0.6 3.0 %collective-permute-start.1 = (bf16[256,2048]{1,0:T(8,128)(2,1)}, bf16[256,2048]{1,0:T(8,128)(2,1)S(1)}, u32[]{:S(2)}, u32[]{:S(2)}) collective-permute-start(bf16[256,2048]{1,0:T(8,128)(2,1)} %bitcast.25), channel_id=1, source_target_pairs={{0,1},{1,0},{2,3},{3,2},{4,5},{5,4},{6,7},{7,6},{8,9},{9,8},{10,11... | collective-permute-start | bytes 3145736 | tf_op jit(solution)/shard_map/ppermute | solution.py:278
  0.7 2.9 %collective-permute-start = (bf16[32,128]{1,0:T(8,128)(2,1)}, bf16[32,128]{1,0:T(8,128)(2,1)S(1)}, u32[]{:S(2)}, u32[]{:S(2)}) collective-permute-start(bf16[32,128]{1,0:T(8,128)(2,1)} %bitcast.18), channel_id=1, source_target_pairs={{0,1},{1,0},{2,3},{3,2},{4,5},{5,4},{6,7},{7,6},{8,9},{9,8},{10,11... | collective-permute-start | bytes 24584 | tf_op jit(solution)/shard_map/ppermute | solution.py:278
  3.6 3.4 %copy-start = (bf16[32,128]{1,0:T(8,128)(2,1)}, bf16[32,128]{1,0:T(8,128)(2,1)S(1)}, u32[]{:S(2)}) copy-start(bf16[32,128]{1,0:T(8,128)(2,1)S(1)} %collective-permute-done.lat_oth) | copy-start | bytes 24580
  3.6 12.0 %collective-permute-start.5 = (bf16[256,2048]{1,0:T(8,128)(2,1)}, bf16[256,2048]{1,0:T(8,128)(2,1)}, u32[]{:S(2)}, u32[]{:S(2)}) collective-permute-start(bf16[256,2048]{1,0:T(8,128)(2,1)} %bitcast.5.q_own), channel_id=1, source_target_pairs={{0,1},{1,0},{2,3},{3,2},{4,5},{5,4},{6,7},{7,6},{8,9},{9,8},{10,11... | collective-permute-start | bytes 3145736 | tf_op jit(solution)/shard_map/ppermute | solution.py:278
  3.7 11.9 %collective-permute-start.6 = (bf16[256,2048]{1,0:T(8,128)(2,1)}, bf16[256,2048]{1,0:T(8,128)(2,1)}, u32[]{:S(2)}, u32[]{:S(2)}) collective-permute-start(bf16[256,2048]{1,0:T(8,128)(2,1)} %bitcast.6.k_own), channel_id=1, source_target_pairs={{0,1},{1,0},{2,3},{3,2},{4,5},{5,4},{6,7},{7,6},{8,9},{9,8},{10,11... | collective-permute-start | bytes 3145736 | tf_op jit(solution)/shard_map/ppermute | solution.py:278
  4.1 11.5 %collective-permute-start.7 = (bf16[256,2048]{1,0:T(8,128)(2,1)}, bf16[256,2048]{1,0:T(8,128)(2,1)}, u32[]{:S(2)}, u32[]{:S(2)}) collective-permute-start(bf16[256,2048]{1,0:T(8,128)(2,1)} %bitcast.7.v_own), channel_id=1, source_target_pairs={{0,1},{1,0},{2,3},{3,2},{4,5},{5,4},{6,7},{7,6},{8,9},{9,8},{10,11... | collective-permute-start | bytes 3145736 | tf_op jit(solution)/shard_map/ppermute | solution.py:278
  7.0 26.8 %all-to-all-start = ((bf16[32,9,16,128]{3,2,1,0:T(8,128)(2,1)}), bf16[32,9,16,128]{3,2,1,0:T(8,128)(2,1)S(1)}, u32[]{:S(2)}, u32[]{:S(2)}) async-start(bf16[32,9,16,128]{3,2,1,0:T(8,128)(2,1)} %shard_map.137), calls=%async_computation | async-start | bytes 2359296 | tf_op jit(solution)/shard_map/all_to_all | solution.py:316
  26.9 12.6 %collective-permute-start.8 = (bf16[256,1024]{1,0:T(8,128)(2,1)}, bf16[256,1024]{1,0:T(8,128)(2,1)S(1)}, u32[]{:S(2)}, u32[]{:S(2)}) collective-permute-start(bf16[256,1024]{1,0:T(8,128)(2,1)} %get-tuple-element.65), channel_id=1, source_target_pairs={{0,1},{1,0},{2,3},{3,2},{4,5},{5,4},{6,7},{7,6},{8,9},{9,8},{10,11... | collective-permute-start | bytes 1572872 | tf_op jit(solution)/shard_map/ppermute | solution.py:278
  27.0 13.9 %collective-permute-start.9 = (bf16[256,1024]{1,0:T(8,128)(2,1)}, bf16[256,1024]{1,0:T(8,128)(2,1)S(1)}, u32[]{:S(2)}, u32[]{:S(2)}) collective-permute-start(bf16[256,1024]{1,0:T(8,128)(2,1)} %get-tuple-element.66), channel_id=1, source_target_pairs={{0,1},{1,0},{2,3},{3,2},{4,5},{5,4},{6,7},{7,6},{8,9},{9,8},{10,11... | collective-permute-start | bytes 1572872 | tf_op jit(solution)/shard_map/ppermute | solution.py:278
  27.5 15.8 %collective-permute-start.10 = (bf16[256,1024]{1,0:T(8,128)(2,1)}, bf16[256,1024]{1,0:T(8,128)(2,1)S(1)}, u32[]{:S(2)}, u32[]{:S(2)}) collective-permute-start(bf16[256,1024]{1,0:T(8,128)(2,1)} %get-tuple-element.67), channel_id=1, source_target_pairs={{0,1},{1,0},{2,3},{3,2},{4,5},{5,4},{6,7},{7,6},{8,9},{9,8},{10,11... | collective-permute-start | bytes 1572872 | tf_op jit(solution)/shard_map/ppermute | solution.py:278
  27.6 21.2 %collective-permute-start.11 = (bf16[256,1024]{1,0:T(8,128)(2,1)}, bf16[256,1024]{1,0:T(8,128)(2,1)S(1)}, u32[]{:S(2)}, u32[]{:S(2)}) collective-permute-start(bf16[256,1024]{1,0:T(8,128)(2,1)} %get-tuple-element.77), channel_id=1, source_target_pairs={{0,1},{1,0},{2,3},{3,2},{4,5},{5,4},{6,7},{7,6},{8,9},{9,8},{10,11... | collective-permute-start | bytes 1572872 | tf_op jit(solution)/shard_map/ppermute | solution.py:278
  34.0 10.5 %collective-permute-start.4 = (bf16[9,16,128]{2,1,0:T(8,128)(2,1)S(1)}, bf16[9,16,128]{2,1,0:T(8,128)(2,1)S(1)}, u32[]{:S(2)}, u32[]{:S(2)}) collective-permute-start(bf16[9,16,128]{2,1,0:T(8,128)(2,1)S(1)} %shard_map.138.one), channel_id=1, source_target_pairs={{0,192},{64,0},{128,64},{192,128},{1,193},{65,1},{129,65},{193,129... | collective-permute-start | bytes 110600 | tf_op jit(solution)/shard_map/ppermute | solution.py:352
  39.5 7.9 %collective-permute-start.3 = (bf16[9,16,128]{2,1,0:T(8,128)(2,1)S(1)}, bf16[9,16,128]{2,1,0:T(8,128)(2,1)S(1)}, u32[]{:S(2)}, u32[]{:S(2)}) collective-permute-start(bf16[9,16,128]{2,1,0:T(8,128)(2,1)S(1)} %shard_map.138.one), channel_id=1, source_target_pairs={{0,128},{64,192},{128,0},{192,64},{1,129},{65,193},{129,1},{193,65... | collective-permute-start | bytes 110600 | tf_op jit(solution)/shard_map/ppermute | solution.py:352
  40.9 6.8 %collective-permute-start.2 = (bf16[9,16,128]{2,1,0:T(8,128)(2,1)S(1)}, bf16[9,16,128]{2,1,0:T(8,128)(2,1)S(1)}, u32[]{:S(2)}, u32[]{:S(2)}) collective-permute-start(bf16[9,16,128]{2,1,0:T(8,128)(2,1)S(1)} %shard_map.138.one), channel_id=1, source_target_pairs={{0,64},{64,128},{128,192},{192,0},{1,65},{65,129},{129,193},{193,1... | collective-permute-start | bytes 110600 | tf_op jit(solution)/shard_map/ppermute | solution.py:352
  48.8 20.8 %all-to-all-start.1 = ((bf16[32,9,16,128]{3,2,1,0:T(8,128)(2,1)}), bf16[32,9,16,128]{3,2,1,0:T(8,128)(2,1)S(1)}, u32[]{:S(2)}, u32[]{:S(2)}) async-start(bf16[32,9,16,128]{3,2,1,0:T(8,128)(2,1)} %shard_map.141), calls=%async_computation.1 | async-start | bytes 2359296 | tf_op jit(solution)/shard_map/all_to_all | solution.py:357

commit v10 on v9

--- a/solution.py
+++ b/solution.py
@@ -348,13 +348,13 @@
         )
 
     one, = near_call(group_sum_body, (got,), [(9, 16, 128)])
-    one, after = lax.optimization_barrier((one, scalars[0]))
-    others = [lax.ppermute(one, "zh", [(z, (z + s) % 4) for z in range(4)]) for s in (1, 2, 3)]
+    one, sent_dq, sent_dk = lax.optimization_barrier((one, sent_dq, sent_dk))
+    others = [lax.ppermute(one, "zh", [(z, z ^ s) for z in range(4)]) for s in (1, 2, 3)]
+    sums, = near_call(spread_sum_body, (one, *others), [(GROUPS, 9, 16, 128)])
+    sums, sent_att, sent_dq, sent_dk, sent_dv, after = lax.optimization_barrier(
+        (sums, sent_att, sent_dq, sent_dk, sent_dv, scalars[0]))
+    got = lax.all_to_all(sums, block, 0, 0, tiled=False)
     dq, dk, dv = placed(after, (sent_dq, sent_dk, sent_dv), (dq, dk, dv))
-    *others, dq, dk, dv = lax.optimization_barrier((*others, dq, dk, dv))
-    sums, = near_call(spread_sum_body, (one, *others), [(GROUPS, 9, 16, 128)])
-    sums, sent_att = lax.optimization_barrier((sums, sent_att))
-    got = lax.all_to_all(sums, block, 0, 0, tiled=False)
     sum_second, sum_first = pl.pallas_call(
         finish_body, in_specs=[near], out_specs=[anywhere, anywhere],
         out_shape=[struct((CH, HALF), F32), struct((32, CH), F32)],

time: 71.4 us -> 71.7 us (level)
  Pallas kernels: 23.1 us -> 24.4 us
  starting transfers between devices: 25.3 us -> 24.5 us
    all_to_all x1, waiting for transfers between devices: 12.3 us -> 9.87 us  [local(): got = lax.all_to_all(sums, block, 0, 0, tiled=False)]
    ppermute x3, waiting for transfers between devices: 3.21 us -> 5.41 us  [local(): lax.ppermute(one, 'zh', [(z, z ^ s) for z in range(4)])]
    ppermute x3, starting transfers between devices: 9.29 us -> 7.95 us  [local(): lax.ppermute(one, 'zh', [(z, z ^ s) for z in range(4)])]
    pallas_call x5, Pallas kernels: 20.4 us -> 21.7 us  [call(): pl.pallas_call(body, grid_spec=pltpu.PrefetchScalarGridSpec(num_scalar_pr...]
  transfers between devices with their start and end apart: 14 -> 14, of which waited for: 5 -> 4; matrix products, arithmetic and copies ran while one was open for 0% -> 0% of each run, Pallas kernels for 30% -> 32%
where the time goes in v10:
time: 71.7 us; the launch traced here: 71.3 us
  starting transfers between devices  24.5 us (34%)
  Pallas kernels  24.4 us (34%)
  waiting for transfers between devices  21.6 us (30%)
  between operations  0.75 us (1%)
    pallas_call x5, Pallas kernels, call(): pl.pallas_call(body, grid_spec=pltpu.PrefetchScalarGridSpec(num_scalar_pr...  21.7 us
    all_to_all x1, waiting for transfers between devices, local(): got = lax.all_to_all(sums, block, 0, 0, tiled=False)  9.87 us
    all_to_all x1, starting transfers between devices, local(): got = lax.all_to_all(payload, block, 0, 0, tiled=False)  8.57 us
    ppermute x3, starting transfers between devices, local(): lax.ppermute(one, 'zh', [(z, z ^ s) for z in range(4)])  7.95 us
    all_to_all x1, waiting for transfers between devices, local(): got = lax.all_to_all(payload, block, 0, 0, tiled=False)  5.88 us
    all_to_all x1, starting transfers between devices, local(): got = lax.all_to_all(sums, block, 0, 0, tiled=False)  5.6 us
    ppermute x3, waiting for transfers between devices, local(): lax.ppermute(one, 'zh', [(z, z ^ s) for z in range(4)])  5.41 us
    ppermute x9, starting transfers between devices, swapped(): return lax.ppermute(value, 'ctx', swap)  2.39 us
  transfers between devices with their start and end apart: 14, of which 4 were waited for; matrix products, arithmetic and copies ran while one was open for 0% of the time, Pallas kernels for 32%

profile of v10, /device:TPU:32, one launch (start us, length us, event | category | flops | bytes accessed | tf_op | source)
XLA Modules:
  0.0 71.3 jit_solution(2192277762467558313)
XLA Ops:
  0.7 0.5 collective-permute-start
  1.2 1.9 %shard_map.136 = (bf16[32,128]{1,0:T(8,128)(2,1)S(1)}, bf16[32,512]{1,0:T(8,128)(2,1)S(1)}, bf16[512,128]{1,0:T(8,128)(2,1)S(1)}, f32[512,128]{1,0:T(8,128)S(1)}...) custom-call(s32[1]{0:T(128)} %bitcast.ctx_ref, bf16[32,128]{1,0:T(8,128)(2,1)} %bitcast.19, ...), custom_call_target="tpu_custom_call" | custom-call | flops 4000000000 | bytes 10000000 | tf_op jit(solution)/shard_map/pallas_call | solution.py:36
  3.1 0.5 collective-permute-done.lat_oth
  3.6 0.2 collective-permute-start.2
  3.8 0.4 collective-permute-start.3
  4.2 0.1 collective-permute-start.4
  4.3 2.8 %shard_map.137 = bf16[32,9,16,128]{3,2,1,0:T(8,128)(2,1)} custom-call(s32[1]{0:T(128)} %bitcast.ctx_ref, s32[2]{0:T(128)} %bitcast.22, bf16[32,128]{1,0:T(8,128)(2,1)S(1)} %get-tuple-element.52.lat_own, bf16[32,512]{1,0:T(8,128)(2,1)S(1)} %get-tuple-element.53.w1, bf16[512,128]{1,0:T(8,128)(2,1)S(1)} %get-tuple-element.54.hid_own, ...), custom_call_target="tpu_custom_call" | custom-call | tf_op jit(solution)/shard_map/pallas_call | solution.py:36
  7.1 8.6 %all-to-all-start = ((bf16[32,9,16,128]{3,2,1,0:T(8,128)(2,1)}), bf16[32,9,16,128]{3,2,1,0:T(8,128)(2,1)S(1)}, u32[]{:S(2)}, u32[]{:S(2)}) async-start(bf16[32,9,16,128]{3,2,1,0:T(8,128)(2,1)} %shard_map.137), calls=%async_computation | async-start | bytes 2359296 | tf_op jit(solution)/shard_map/all_to_all | solution.py:316
  15.7 11.2 %shard_map.139 = (bf16[256,2048]{1,0:T(8,128)(2,1)}, bf16[256,2048]{1,0:T(8,128)(2,1)}, bf16[256,2048]{1,0:T(8,128)(2,1)}, bf16[256,2048]{1,0:T(8,128)(2,1)}, bf...) custom-call(s32[1]{0:T(128)} %bitcast.ctx_ref, ...), custom_call_target="tpu_custom_call" | custom-call | flops 40000000000 | bytes 100000000 | tf_op jit(solution)/shard_map/pallas_call | solution.py:36
  27.0 0.5 collective-permute-start.6
  27.5 0.1 collective-permute-start.10
  27.6 0.4 collective-permute-start.11
  28.0 5.9 %all-to-all-done.got = bf16[32,9,16,128]{3,2,1,0:T(8,128)(2,1)S(1)} async-done(((bf16[32,9,16,128]{3,2,1,0:T(8,128)(2,1)}), bf16[32,9,16,128]{3,2,1,0:T(8,128)(2,1)S(1)}, u32[]{:S(2)}, u32[]{:S(2)}) %all-to-all-start) | async-done | bytes 1179680 | tf_op jit(solution)/shard_map/all_to_all | solution.py:316
  33.9 0.2 shard_map.138.one
  34.1 5.5 %collective-permute-start.9 = (bf16[9,16,128]{2,1,0:T(8,128)(2,1)S(1)}, bf16[9,16,128]{2,1,0:T(8,128)(2,1)S(1)}, u32[]{:S(2)}, u32[]{:S(2)}) collective-permute-start(bf16[9,16,128]{2,1,0:T(8,128)(2,1)S(1)} %shard_map.138.one), channel_id=1, source_target_pairs={{0,192},{64,128},{128,64},{192,0},{1,193},{65,129},{129,65},{193,1... | collective-permute-start | bytes 110600 | tf_op jit(solution)/shard_map/ppermute | solution.py:352
  39.6 1.4 %collective-permute-start.8 = (bf16[9,16,128]{2,1,0:T(8,128)(2,1)S(1)}, bf16[9,16,128]{2,1,0:T(8,128)(2,1)S(1)}, u32[]{:S(2)}, u32[]{:S(2)}) collective-permute-start(bf16[9,16,128]{2,1,0:T(8,128)(2,1)S(1)} %shard_map.138.one), channel_id=1, source_target_pairs={{0,128},{64,192},{128,0},{192,64},{1,129},{65,193},{129,1},{193,65... | collective-permute-start | bytes 110600 | tf_op jit(solution)/shard_map/ppermute | solution.py:352
  41.0 1.0 %collective-permute-start.7 = (bf16[9,16,128]{2,1,0:T(8,128)(2,1)S(1)}, bf16[9,16,128]{2,1,0:T(8,128)(2,1)S(1)}, u32[]{:S(2)}, u32[]{:S(2)}) collective-permute-start(bf16[9,16,128]{2,1,0:T(8,128)(2,1)S(1)} %shard_map.138.one), channel_id=1, source_target_pairs={{0,64},{64,0},{128,192},{192,128},{1,65},{65,1},{129,193},{193,129... | collective-permute-start | bytes 110600 | tf_op jit(solution)/shard_map/ppermute | solution.py:352
  42.1 5.4 %collective-permute-done.8.next2 = bf16[9,16,128]{2,1,0:T(8,128)(2,1)S(1)} collective-permute-done((bf16[9,16,128]{2,1,0:T(8,128)(2,1)S(1)}, bf16[9,16,128]{2,1,0:T(8,128)(2,1)S(1)}, u32[]{:S(2)}, u32[]{:S(2)}) %collective-permute-start.8) | collective-permute-done | bytes 36896 | tf_op jit(solution)/shard_map/ppermute | solution.py:352
  47.5 1.1 %shard_map.140 = bf16[32,9,16,128]{3,2,1,0:T(8,128)(2,1)} custom-call(bf16[9,16,128]{2,1,0:T(8,128)(2,1)S(1)} %shard_map.138.one, bf16[9,16,128]{2,1,0:T(8,128)(2,1)S(1)} %collective-permute-done.7.next1, bf16[9,16,128]{2,1,0:T(8,128)(2,1)S(1)} %collective-permute-done.8.next2, bf16[9,16,128]{2,1,0:T(8,128)(2,1)S(1)} %collective-permute-done.9.next3), custom_call_target="tpu_custom_call" | custom-call | tf_op jit(solution)/shard_map/pallas_call | solution.py:293
  48.6 5.6 %all-to-all-start.1 = ((bf16[32,9,16,128]{3,2,1,0:T(8,128)(2,1)}), bf16[32,9,16,128]{3,2,1,0:T(8,128)(2,1)S(1)}, u32[]{:S(2)}, u32[]{:S(2)}) async-start(bf16[32,9,16,128]{3,2,1,0:T(8,128)(2,1)} %shard_map.140), calls=%async_computation.1 | async-start | bytes 2359296 | tf_op jit(solution)/shard_map/all_to_all | solution.py:356
  54.2 3.6 %shard_map.141 = bf16[256,2048]{1,0:T(8,128)(2,1)} custom-call(s32[1]{0:T(128)} %bitcast.ctx_ref, s32[2]{0:T(128)} %bitcast.24, bf16[256,2048]{1,0:T(8,128)(2,1)} %bitcast.13, bf16[32,128]{1,0:T(8,128)(2,1)} %bitcast.21, bf16[32,128]{1,0:T(8,128)(2,1)} %copy-done, bf16[32,512]{1,0:T(8,128)(2,1)} %w1.3, ...), custom_call_target="tpu_custom_call", output_to_operand_aliasing={{}: (8, {})} | custom-call | tf_op jit(solution)/shard_map/pallas_call | solution.py:36
  57.8 2.2 %shard_map.142 = (bf16[256,2048]{1,0:T(8,128)(2,1)}, bf16[256,2048]{1,0:T(8,128)(2,1)}, bf16[256,2048]{1,0:T(8,128)(2,1)}) custom-call(s32[1]{0:T(128)} %bitcast.ctx_ref, bf16[256,1024]{1,0:T(8,128)(2,1)S(1)} %collective-permute-done.5.refs_0_, ...), custom_call_target="tpu_custom_call", output_to_operand_aliasing={{0}: (4, {}), {1}: (5, {}), {2}: (6, {})} | custom-call | tf_op jit(solution)/shard_map/pallas_call | solution.py:36
  60.0 9.9 %all-to-all-done.1.got = bf16[32,9,16,128]{3,2,1,0:T(8,128)(2,1)S(1)} async-done(((bf16[32,9,16,128]{3,2,1,0:T(8,128)(2,1)}), bf16[32,9,16,128]{3,2,1,0:T(8,128)(2,1)S(1)}, u32[]{:S(2)}, u32[]{:S(2)}) %all-to-all-start.1) | async-done | bytes 1179680 | tf_op jit(solution)/shard_map/all_to_all | solution.py:356
  69.9 1.4 %shard_map.143 = (f32[512,1024]{1,0:T(8,128)}, f32[32,512]{1,0:T(8,128)}) custom-call(bf16[32,9,16,128]{3,2,1,0:T(8,128)(2,1)S(1)} %all-to-all-done.1.got), custom_call_target="tpu_custom_call" | custom-call | tf_op jit(solution)/shard_map/pallas_call | solution.py:358
  (16 shorter events, 0.2 us)
Async XLA Ops:
  0.6 3.0 %collective-permute-start.1 = (bf16[256,2048]{1,0:T(8,128)(2,1)}, bf16[256,2048]{1,0:T(8,128)(2,1)S(1)}, u32[]{:S(2)}, u32[]{:S(2)}) collective-permute-start(bf16[256,2048]{1,0:T(8,128)(2,1)} %bitcast.27), channel_id=1, source_target_pairs={{0,1},{1,0},{2,3},{3,2},{4,5},{5,4},{6,7},{7,6},{8,9},{9,8},{10,11... | collective-permute-start | bytes 3145736 | tf_op jit(solution)/shard_map/ppermute | solution.py:278
  0.7 2.9 %collective-permute-start = (bf16[32,128]{1,0:T(8,128)(2,1)}, bf16[32,128]{1,0:T(8,128)(2,1)S(1)}, u32[]{:S(2)}, u32[]{:S(2)}) collective-permute-start(bf16[32,128]{1,0:T(8,128)(2,1)} %bitcast.18), channel_id=1, source_target_pairs={{0,1},{1,0},{2,3},{3,2},{4,5},{5,4},{6,7},{7,6},{8,9},{9,8},{10,11... | collective-permute-start | bytes 24584 | tf_op jit(solution)/shard_map/ppermute | solution.py:278
  1.2 2.4 %copy-start.1 = (bf16[1,256,2048]{2,1,0:T(8,128)(2,1)S(1)}, bf16[1,256,2048]{2,1,0:T(8,128)(2,1)}, u32[]{:S(2)}) copy-start(bf16[1,256,2048]{2,1,0:T(8,128)(2,1)} %param.9) | copy-start | bytes 3145732
  3.6 3.5 %copy-start = (bf16[32,128]{1,0:T(8,128)(2,1)}, bf16[32,128]{1,0:T(8,128)(2,1)S(1)}, u32[]{:S(2)}) copy-start(bf16[32,128]{1,0:T(8,128)(2,1)S(1)} %collective-permute-done.lat_oth) | copy-start | bytes 24580
  3.6 12.1 %collective-permute-start.2 = (bf16[256,2048]{1,0:T(8,128)(2,1)S(1)}, bf16[256,2048]{1,0:T(8,128)(2,1)}, u32[]{:S(2)}, u32[]{:S(2)}) collective-permute-start(bf16[256,2048]{1,0:T(8,128)(2,1)S(1)} %bitcast.26), channel_id=1, source_target_pairs={{0,1},{1,0},{2,3},{3,2},{4,5},{5,4},{6,7},{7,6},{8,9},{9,8},{10,11... | collective-permute-start | bytes 3145736 | tf_op jit(solution)/shard_map/ppermute | solution.py:278
  3.8 11.9 %collective-permute-start.3 = (bf16[256,2048]{1,0:T(8,128)(2,1)}, bf16[256,2048]{1,0:T(8,128)(2,1)}, u32[]{:S(2)}, u32[]{:S(2)}) collective-permute-start(bf16[256,2048]{1,0:T(8,128)(2,1)} %bitcast.6.k_own), channel_id=1, source_target_pairs={{0,1},{1,0},{2,3},{3,2},{4,5},{5,4},{6,7},{7,6},{8,9},{9,8},{10,11... | collective-permute-start | bytes 3145736 | tf_op jit(solution)/shard_map/ppermute | solution.py:278
  4.2 11.5 %collective-permute-start.4 = (bf16[256,2048]{1,0:T(8,128)(2,1)}, bf16[256,2048]{1,0:T(8,128)(2,1)}, u32[]{:S(2)}, u32[]{:S(2)}) collective-permute-start(bf16[256,2048]{1,0:T(8,128)(2,1)} %bitcast.7.v_own), channel_id=1, source_target_pairs={{0,1},{1,0},{2,3},{3,2},{4,5},{5,4},{6,7},{7,6},{8,9},{9,8},{10,11... | collective-permute-start | bytes 3145736 | tf_op jit(solution)/shard_map/ppermute | solution.py:278
  7.1 26.8 %all-to-all-start = ((bf16[32,9,16,128]{3,2,1,0:T(8,128)(2,1)}), bf16[32,9,16,128]{3,2,1,0:T(8,128)(2,1)S(1)}, u32[]{:S(2)}, u32[]{:S(2)}) async-start(bf16[32,9,16,128]{3,2,1,0:T(8,128)(2,1)} %shard_map.137), calls=%async_computation | async-start | bytes 2359296 | tf_op jit(solution)/shard_map/all_to_all | solution.py:316
  26.9 7.2 %collective-permute-start.5 = (bf16[256,1024]{1,0:T(8,128)(2,1)}, bf16[256,1024]{1,0:T(8,128)(2,1)S(1)}, u32[]{:S(2)}, u32[]{:S(2)}) collective-permute-start(bf16[256,1024]{1,0:T(8,128)(2,1)} %get-tuple-element.62), channel_id=1, source_target_pairs={{0,1},{1,0},{2,3},{3,2},{4,5},{5,4},{6,7},{7,6},{8,9},{9,8},{10,11... | collective-permute-start | bytes 1572872 | tf_op jit(solution)/shard_map/ppermute | solution.py:278
  27.0 7.1 %collective-permute-start.6 = (bf16[256,1024]{1,0:T(8,128)(2,1)}, bf16[256,1024]{1,0:T(8,128)(2,1)S(1)}, u32[]{:S(2)}, u32[]{:S(2)}) collective-permute-start(bf16[256,1024]{1,0:T(8,128)(2,1)} %get-tuple-element.63), channel_id=1, source_target_pairs={{0,1},{1,0},{2,3},{3,2},{4,5},{5,4},{6,7},{7,6},{8,9},{9,8},{10,11... | collective-permute-start | bytes 1572872 | tf_op jit(solution)/shard_map/ppermute | solution.py:278
  27.5 21.0 %collective-permute-start.10 = (bf16[256,1024]{1,0:T(8,128)(2,1)}, bf16[256,1024]{1,0:T(8,128)(2,1)}, u32[]{:S(2)}, u32[]{:S(2)}) collective-permute-start(bf16[256,1024]{1,0:T(8,128)(2,1)} %get-tuple-element.65), channel_id=1, source_target_pairs={{0,1},{1,0},{2,3},{3,2},{4,5},{5,4},{6,7},{7,6},{8,9},{9,8},{10,11... | collective-permute-start | bytes 1572872 | tf_op jit(solution)/shard_map/ppermute | solution.py:278
  27.6 20.9 %collective-permute-start.11 = (bf16[256,1024]{1,0:T(8,128)(2,1)}, bf16[256,1024]{1,0:T(8,128)(2,1)}, u32[]{:S(2)}, u32[]{:S(2)}) collective-permute-start(bf16[256,1024]{1,0:T(8,128)(2,1)} %get-tuple-element.68), channel_id=1, source_target_pairs={{0,1},{1,0},{2,3},{3,2},{4,5},{5,4},{6,7},{7,6},{8,9},{9,8},{10,11... | collective-permute-start | bytes 1572872 | tf_op jit(solution)/shard_map/ppermute | solution.py:278
  34.1 8.0 %collective-permute-start.9 = (bf16[9,16,128]{2,1,0:T(8,128)(2,1)S(1)}, bf16[9,16,128]{2,1,0:T(8,128)(2,1)S(1)}, u32[]{:S(2)}, u32[]{:S(2)}) collective-permute-start(bf16[9,16,128]{2,1,0:T(8,128)(2,1)S(1)} %shard_map.138.one), channel_id=1, source_target_pairs={{0,192},{64,128},{128,64},{192,0},{1,193},{65,129},{129,65},{193,1... | collective-permute-start | bytes 110600 | tf_op jit(solution)/shard_map/ppermute | solution.py:352
  39.6 7.9 %collective-permute-start.8 = (bf16[9,16,128]{2,1,0:T(8,128)(2,1)S(1)}, bf16[9,16,128]{2,1,0:T(8,128)(2,1)S(1)}, u32[]{:S(2)}, u32[]{:S(2)}) collective-permute-start(bf16[9,16,128]{2,1,0:T(8,128)(2,1)S(1)} %shard_map.138.one), channel_id=1, source_target_pairs={{0,128},{64,192},{128,0},{192,64},{1,129},{65,193},{129,1},{193,65... | collective-permute-start | bytes 110600 | tf_op jit(solution)/shard_map/ppermute | solution.py:352
  41.0 6.4 %collective-permute-start.7 = (bf16[9,16,128]{2,1,0:T(8,128)(2,1)S(1)}, bf16[9,16,128]{2,1,0:T(8,128)(2,1)S(1)}, u32[]{:S(2)}, u32[]{:S(2)}) collective-permute-start(bf16[9,16,128]{2,1,0:T(8,128)(2,1)S(1)} %shard_map.138.one), channel_id=1, source_target_pairs={{0,64},{64,0},{128,192},{192,128},{1,65},{65,1},{129,193},{193,129... | collective-permute-start | bytes 110600 | tf_op jit(solution)/shard_map/ppermute | solution.py:352
  48.6 21.3 %all-to-all-start.1 = ((bf16[32,9,16,128]{3,2,1,0:T(8,128)(2,1)}), bf16[32,9,16,128]{3,2,1,0:T(8,128)(2,1)S(1)}, u32[]{:S(2)}, u32[]{:S(2)}) async-start(bf16[32,9,16,128]{3,2,1,0:T(8,128)(2,1)} %shard_map.140), calls=%async_computation.1 | async-start | bytes 2359296 | tf_op jit(solution)/shard_map/all_to_all | solution.py:356

commit v11 on v9

--- a/solution.py
+++ b/solution.py
@@ -124,12 +124,15 @@
     out[...] = total.astype(BF16)
 
 
-def spread_sum_body(one, next1, next2, next3, out):
+def spread_sum_body(one, next1, next2, next3, out, total, sems):
     even = one[...].astype(F32) + next2[...].astype(F32)
     odd = next1[...].astype(F32) + next3[...].astype(F32)
-    total = (even + odd).astype(BF16)
-    for j in range(GROUPS):
-        out[j] = total
+    total[...] = (even + odd).astype(BF16)
+    copies = [pltpu.make_async_copy(total, out.at[j], sems.at[j]) for j in range(GROUPS)]
+    for copy in copies:
+        copy.start()
+    for copy in copies:
+        copy.wait()
 
 
 def finish_body(got, second, first, second_near, first_near, sems):
@@ -352,7 +355,10 @@
     others = [lax.ppermute(one, "zh", [(z, (z + s) % 4) for z in range(4)]) for s in (1, 2, 3)]
     dq, dk, dv = placed(after, (sent_dq, sent_dk, sent_dv), (dq, dk, dv))
     *others, dq, dk, dv = lax.optimization_barrier((*others, dq, dk, dv))
-    sums, = near_call(spread_sum_body, (one, *others), [(GROUPS, 9, 16, 128)])
+    sums = pl.pallas_call(
+        spread_sum_body, in_specs=[near] * 4, out_specs=anywhere, out_shape=struct((GROUPS, 9, 16, 128), BF16),
+        scratch_shapes=[pltpu.VMEM((9, 16, 128), BF16), pltpu.SemaphoreType.DMA((GROUPS,))],
+    )(*[place_near(value) for value in (one, *others)])
     sums, sent_att = lax.optimization_barrier((sums, sent_att))
     got = lax.all_to_all(sums, block, 0, 0, tiled=False)
     sum_second, sum_first = pl.pallas_call(

time: 71.4 us -> 71.6 us (level)
    pallas_call x0 -> x1, Pallas kernels: none -> 1.3 us  [local(): pl.pallas_call(spread_sum_body, in_specs=[near] * 4, out_specs=anywhere,...]
    pallas_call x2 -> x1, Pallas kernels: 1.26 us -> 0.16 us  [near_call(): pl.pallas_call(body, in_specs=[near] * len(args), out_specs=[near] * len(...]
  transfers between devices with their start and end apart: 14 -> 14, of which waited for: 5 -> 5; matrix products, arithmetic and copies ran while one was open for 0% -> 0% of each run, Pallas kernels for 30% -> 31%
where the time goes in v11:
time: 71.6 us; the launch traced here: 71.2 us
  starting transfers between devices  25.4 us (35%)
  Pallas kernels  23.3 us (33%)
  waiting for transfers between devices  21.9 us (31%)
  between operations  0.74 us (1%)
    pallas_call x5, Pallas kernels, call(): pl.pallas_call(body, grid_spec=pltpu.PrefetchScalarGridSpec(num_scalar_pr...  20.4 us
    all_to_all x1, waiting for transfers between devices, local(): got = lax.all_to_all(sums, block, 0, 0, tiled=False)  12.3 us
    ppermute x3, starting transfers between devices, local(): lax.ppermute(one, 'zh', [(z, (z + s) % 4) for z in range(4)])  9.29 us
    all_to_all x1, starting transfers between devices, local(): got = lax.all_to_all(payload, block, 0, 0, tiled=False)  8.58 us
    all_to_all x1, waiting for transfers between devices, local(): got = lax.all_to_all(payload, block, 0, 0, tiled=False)  5.81 us
    all_to_all x1, starting transfers between devices, local(): got = lax.all_to_all(sums, block, 0, 0, tiled=False)  5.14 us
    ppermute x3, waiting for transfers between devices, local(): lax.ppermute(one, 'zh', [(z, (z + s) % 4) for z in range(4)])  3.21 us
    ppermute x9, starting transfers between devices, swapped(): return lax.ppermute(value, 'ctx', swap)  2.34 us
  transfers between devices with their start and end apart: 14, of which 5 were waited for; matrix products, arithmetic and copies ran while one was open for 0% of the time, Pallas kernels for 31%

profile of v11, /device:TPU:32, one launch (start us, length us, event | category | flops | bytes accessed | tf_op | source)
XLA Modules:
  0.0 71.2 jit_solution(3245569270118241698)
XLA Ops:
  0.7 0.5 collective-permute-start
  1.2 1.8 %shard_map.136 = (bf16[32,128]{1,0:T(8,128)(2,1)S(1)}, bf16[32,512]{1,0:T(8,128)(2,1)S(1)}, bf16[512,128]{1,0:T(8,128)(2,1)S(1)}, f32[512,128]{1,0:T(8,128)S(1)}...) custom-call(s32[1]{0:T(128)} %bitcast.ctx_ref, bf16[32,128]{1,0:T(8,128)(2,1)} %bitcast.19, ...), custom_call_target="tpu_custom_call" | custom-call | flops 4000000000 | bytes 10000000 | tf_op jit(solution)/shard_map/pallas_call | solution.py:36
  3.1 0.5 collective-permute-done.lat_oth
  3.6 0.1 collective-permute-start.5
  3.7 0.4 collective-permute-start.6
  4.1 0.1 collective-permute-start.7
  4.3 2.8 %shard_map.137 = bf16[32,9,16,128]{3,2,1,0:T(8,128)(2,1)} custom-call(s32[1]{0:T(128)} %bitcast.ctx_ref, s32[2]{0:T(128)} %bitcast.22, bf16[32,128]{1,0:T(8,128)(2,1)S(1)} %get-tuple-element.53.lat_own, bf16[32,512]{1,0:T(8,128)(2,1)S(1)} %get-tuple-element.54.w1, bf16[512,128]{1,0:T(8,128)(2,1)S(1)} %get-tuple-element.55.hid_own, ...), custom_call_target="tpu_custom_call" | custom-call | tf_op jit(solution)/shard_map/pallas_call | solution.py:36
  7.0 8.6 %all-to-all-start = ((bf16[32,9,16,128]{3,2,1,0:T(8,128)(2,1)}), bf16[32,9,16,128]{3,2,1,0:T(8,128)(2,1)S(1)}, u32[]{:S(2)}, u32[]{:S(2)}) async-start(bf16[32,9,16,128]{3,2,1,0:T(8,128)(2,1)} %shard_map.137), calls=%async_computation | async-start | bytes 2359296 | tf_op jit(solution)/shard_map/all_to_all | solution.py:319
  15.7 11.2 %shard_map.139 = (bf16[256,2048]{1,0:T(8,128)(2,1)}, bf16[256,2048]{1,0:T(8,128)(2,1)}, bf16[256,2048]{1,0:T(8,128)(2,1)}, bf16[256,2048]{1,0:T(8,128)(2,1)}, bf...) custom-call(s32[1]{0:T(128)} %bitcast.ctx_ref, ...), custom_call_target="tpu_custom_call" | custom-call | flops 40000000000 | bytes 100000000 | tf_op jit(solution)/shard_map/pallas_call | solution.py:36
  27.0 0.5 collective-permute-start.9
  27.6 0.4 collective-permute-start.11
  28.0 5.8 %all-to-all-done.got = bf16[32,9,16,128]{3,2,1,0:T(8,128)(2,1)S(1)} async-done(((bf16[32,9,16,128]{3,2,1,0:T(8,128)(2,1)}), bf16[32,9,16,128]{3,2,1,0:T(8,128)(2,1)S(1)}, u32[]{:S(2)}, u32[]{:S(2)}) %all-to-all-start) | async-done | bytes 1179680 | tf_op jit(solution)/shard_map/all_to_all | solution.py:319
  33.8 0.2 shard_map.138.one
  34.0 5.5 %collective-permute-start.4 = (bf16[9,16,128]{2,1,0:T(8,128)(2,1)S(1)}, bf16[9,16,128]{2,1,0:T(8,128)(2,1)S(1)}, u32[]{:S(2)}, u32[]{:S(2)}) collective-permute-start(bf16[9,16,128]{2,1,0:T(8,128)(2,1)S(1)} %shard_map.138.one), channel_id=1, source_target_pairs={{0,192},{64,0},{128,64},{192,128},{1,193},{65,1},{129,65},{193,129... | collective-permute-start | bytes 110600 | tf_op jit(solution)/shard_map/ppermute | solution.py:355
  39.5 1.4 %collective-permute-start.3 = (bf16[9,16,128]{2,1,0:T(8,128)(2,1)S(1)}, bf16[9,16,128]{2,1,0:T(8,128)(2,1)S(1)}, u32[]{:S(2)}, u32[]{:S(2)}) collective-permute-start(bf16[9,16,128]{2,1,0:T(8,128)(2,1)S(1)} %shard_map.138.one), channel_id=1, source_target_pairs={{0,128},{64,192},{128,0},{192,64},{1,129},{65,193},{129,1},{193,65... | collective-permute-start | bytes 110600 | tf_op jit(solution)/shard_map/ppermute | solution.py:355
  40.9 2.4 %collective-permute-start.2 = (bf16[9,16,128]{2,1,0:T(8,128)(2,1)S(1)}, bf16[9,16,128]{2,1,0:T(8,128)(2,1)S(1)}, u32[]{:S(2)}, u32[]{:S(2)}) collective-permute-start(bf16[9,16,128]{2,1,0:T(8,128)(2,1)S(1)} %shard_map.138.one), channel_id=1, source_target_pairs={{0,64},{64,128},{128,192},{192,0},{1,65},{65,129},{129,193},{193,1... | collective-permute-start | bytes 110600 | tf_op jit(solution)/shard_map/ppermute | solution.py:355
  43.3 1.2 %shard_map.140 = (bf16[256,2048]{1,0:T(8,128)(2,1)}, bf16[256,2048]{1,0:T(8,128)(2,1)}, bf16[256,2048]{1,0:T(8,128)(2,1)}) custom-call(s32[1]{0:T(128)} %bitcast.ctx_ref, bf16[256,1024]{1,0:T(8,128)(2,1)S(1)} %collective-permute-done.8.refs_0_, ...), custom_call_target="tpu_custom_call", output_to_operand_aliasing={{0}: (4, {}), {1}: (5, {}), {2}: (6, {})} | custom-call | tf_op jit(solution)/shard_map/pallas_call | solution.py:36
  44.5 2.9 %collective-permute-done.3.next2 = bf16[9,16,128]{2,1,0:T(8,128)(2,1)S(1)} collective-permute-done((bf16[9,16,128]{2,1,0:T(8,128)(2,1)S(1)}, bf16[9,16,128]{2,1,0:T(8,128)(2,1)S(1)}, u32[]{:S(2)}, u32[]{:S(2)}) %collective-permute-start.3) | collective-permute-done | bytes 36896 | tf_op jit(solution)/shard_map/ppermute | solution.py:355
  47.3 0.4 collective-permute-done.2.next1
  47.7 1.3 %shard_map.141 = bf16[32,9,16,128]{3,2,1,0:T(8,128)(2,1)} custom-call(bf16[9,16,128]{2,1,0:T(8,128)(2,1)S(1)} %shard_map.138.one, bf16[9,16,128]{2,1,0:T(8,128)(2,1)S(1)} %collective-permute-done.2.next1, bf16[9,16,128]{2,1,0:T(8,128)(2,1)S(1)} %collective-permute-done.3.next2, bf16[9,16,128]{2,1,0:T(8,128)(2,1)S(1)} %collective-permute-done.4.next3), custom_call_target="tpu_custom_call" | custom-call | tf_op jit(solution)/shard_map/pallas_call | solution.py:358
  49.0 5.1 %all-to-all-start.1 = ((bf16[32,9,16,128]{3,2,1,0:T(8,128)(2,1)}), bf16[32,9,16,128]{3,2,1,0:T(8,128)(2,1)S(1)}, u32[]{:S(2)}, u32[]{:S(2)}) async-start(bf16[32,9,16,128]{3,2,1,0:T(8,128)(2,1)} %shard_map.141), calls=%async_computation.1 | async-start | bytes 2359296 | tf_op jit(solution)/shard_map/all_to_all | solution.py:363
  54.1 3.4 %shard_map.142 = bf16[256,2048]{1,0:T(8,128)(2,1)} custom-call(s32[1]{0:T(128)} %bitcast.ctx_ref, s32[2]{0:T(128)} %bitcast.24, bf16[256,2048]{1,0:T(8,128)(2,1)} %bitcast.13, bf16[32,128]{1,0:T(8,128)(2,1)} %bitcast.21, bf16[32,128]{1,0:T(8,128)(2,1)} %copy-done, bf16[32,512]{1,0:T(8,128)(2,1)} %w1.3, ...), custom_call_target="tpu_custom_call", output_to_operand_aliasing={{}: (8, {})} | custom-call | tf_op jit(solution)/shard_map/pallas_call | solution.py:36
  57.5 12.3 %all-to-all-done.1.got = bf16[32,9,16,128]{3,2,1,0:T(8,128)(2,1)S(1)} async-done(((bf16[32,9,16,128]{3,2,1,0:T(8,128)(2,1)}), bf16[32,9,16,128]{3,2,1,0:T(8,128)(2,1)S(1)}, u32[]{:S(2)}, u32[]{:S(2)}) %all-to-all-start.1) | async-done | bytes 1179680 | tf_op jit(solution)/shard_map/all_to_all | solution.py:363
  69.8 1.4 %shard_map.143 = (f32[512,1024]{1,0:T(8,128)}, f32[32,512]{1,0:T(8,128)}) custom-call(bf16[32,9,16,128]{3,2,1,0:T(8,128)(2,1)S(1)} %all-to-all-done.1.got), custom_call_target="tpu_custom_call" | custom-call | tf_op jit(solution)/shard_map/pallas_call | solution.py:364
  (14 shorter events, 0.3 us)
Async XLA Ops:
  0.6 3.0 %collective-permute-start.1 = (bf16[256,2048]{1,0:T(8,128)(2,1)}, bf16[256,2048]{1,0:T(8,128)(2,1)S(1)}, u32[]{:S(2)}, u32[]{:S(2)}) collective-permute-start(bf16[256,2048]{1,0:T(8,128)(2,1)} %bitcast.25), channel_id=1, source_target_pairs={{0,1},{1,0},{2,3},{3,2},{4,5},{5,4},{6,7},{7,6},{8,9},{9,8},{10,11... | collective-permute-start | bytes 3145736 | tf_op jit(solution)/shard_map/ppermute | solution.py:281
  0.7 2.9 %collective-permute-start = (bf16[32,128]{1,0:T(8,128)(2,1)}, bf16[32,128]{1,0:T(8,128)(2,1)S(1)}, u32[]{:S(2)}, u32[]{:S(2)}) collective-permute-start(bf16[32,128]{1,0:T(8,128)(2,1)} %bitcast.18), channel_id=1, source_target_pairs={{0,1},{1,0},{2,3},{3,2},{4,5},{5,4},{6,7},{7,6},{8,9},{9,8},{10,11... | collective-permute-start | bytes 24584 | tf_op jit(solution)/shard_map/ppermute | solution.py:281
  3.6 3.4 %copy-start = (bf16[32,128]{1,0:T(8,128)(2,1)}, bf16[32,128]{1,0:T(8,128)(2,1)S(1)}, u32[]{:S(2)}) copy-start(bf16[32,128]{1,0:T(8,128)(2,1)S(1)} %collective-permute-done.lat_oth) | copy-start | bytes 24580
  3.6 12.0 %collective-permute-start.5 = (bf16[256,2048]{1,0:T(8,128)(2,1)}, bf16[256,2048]{1,0:T(8,128)(2,1)}, u32[]{:S(2)}, u32[]{:S(2)}) collective-permute-start(bf16[256,2048]{1,0:T(8,128)(2,1)} %bitcast.5.q_own), channel_id=1, source_target_pairs={{0,1},{1,0},{2,3},{3,2},{4,5},{5,4},{6,7},{7,6},{8,9},{9,8},{10,11... | collective-permute-start | bytes 3145736 | tf_op jit(solution)/shard_map/ppermute | solution.py:281
  3.7 11.9 %collective-permute-start.6 = (bf16[256,2048]{1,0:T(8,128)(2,1)}, bf16[256,2048]{1,0:T(8,128)(2,1)}, u32[]{:S(2)}, u32[]{:S(2)}) collective-permute-start(bf16[256,2048]{1,0:T(8,128)(2,1)} %bitcast.6.k_own), channel_id=1, source_target_pairs={{0,1},{1,0},{2,3},{3,2},{4,5},{5,4},{6,7},{7,6},{8,9},{9,8},{10,11... | collective-permute-start | bytes 3145736 | tf_op jit(solution)/shard_map/ppermute | solution.py:281
  4.1 11.5 %collective-permute-start.7 = (bf16[256,2048]{1,0:T(8,128)(2,1)}, bf16[256,2048]{1,0:T(8,128)(2,1)}, u32[]{:S(2)}, u32[]{:S(2)}) collective-permute-start(bf16[256,2048]{1,0:T(8,128)(2,1)} %bitcast.7.v_own), channel_id=1, source_target_pairs={{0,1},{1,0},{2,3},{3,2},{4,5},{5,4},{6,7},{7,6},{8,9},{9,8},{10,11... | collective-permute-start | bytes 3145736 | tf_op jit(solution)/shard_map/ppermute | solution.py:281
  7.0 26.8 %all-to-all-start = ((bf16[32,9,16,128]{3,2,1,0:T(8,128)(2,1)}), bf16[32,9,16,128]{3,2,1,0:T(8,128)(2,1)S(1)}, u32[]{:S(2)}, u32[]{:S(2)}) async-start(bf16[32,9,16,128]{3,2,1,0:T(8,128)(2,1)} %shard_map.137), calls=%async_computation | async-start | bytes 2359296 | tf_op jit(solution)/shard_map/all_to_all | solution.py:319
  26.9 12.6 %collective-permute-start.8 = (bf16[256,1024]{1,0:T(8,128)(2,1)}, bf16[256,1024]{1,0:T(8,128)(2,1)S(1)}, u32[]{:S(2)}, u32[]{:S(2)}) collective-permute-start(bf16[256,1024]{1,0:T(8,128)(2,1)} %get-tuple-element.65), channel_id=1, source_target_pairs={{0,1},{1,0},{2,3},{3,2},{4,5},{5,4},{6,7},{7,6},{8,9},{9,8},{10,11... | collective-permute-start | bytes 1572872 | tf_op jit(solution)/shard_map/ppermute | solution.py:281
  27.0 13.9 %collective-permute-start.9 = (bf16[256,1024]{1,0:T(8,128)(2,1)}, bf16[256,1024]{1,0:T(8,128)(2,1)S(1)}, u32[]{:S(2)}, u32[]{:S(2)}) collective-permute-start(bf16[256,1024]{1,0:T(8,128)(2,1)} %get-tuple-element.66), channel_id=1, source_target_pairs={{0,1},{1,0},{2,3},{3,2},{4,5},{5,4},{6,7},{7,6},{8,9},{9,8},{10,11... | collective-permute-start | bytes 1572872 | tf_op jit(solution)/shard_map/ppermute | solution.py:281
  27.5 15.8 %collective-permute-start.10 = (bf16[256,1024]{1,0:T(8,128)(2,1)}, bf16[256,1024]{1,0:T(8,128)(2,1)S(1)}, u32[]{:S(2)}, u32[]{:S(2)}) collective-permute-start(bf16[256,1024]{1,0:T(8,128)(2,1)} %get-tuple-element.67), channel_id=1, source_target_pairs={{0,1},{1,0},{2,3},{3,2},{4,5},{5,4},{6,7},{7,6},{8,9},{9,8},{10,11... | collective-permute-start | bytes 1572872 | tf_op jit(solution)/shard_map/ppermute | solution.py:281
  27.6 21.4 %collective-permute-start.11 = (bf16[256,1024]{1,0:T(8,128)(2,1)}, bf16[256,1024]{1,0:T(8,128)(2,1)S(1)}, u32[]{:S(2)}, u32[]{:S(2)}) collective-permute-start(bf16[256,1024]{1,0:T(8,128)(2,1)} %get-tuple-element.77), channel_id=1, source_target_pairs={{0,1},{1,0},{2,3},{3,2},{4,5},{5,4},{6,7},{7,6},{8,9},{9,8},{10,11... | collective-permute-start | bytes 1572872 | tf_op jit(solution)/shard_map/ppermute | solution.py:281
  34.0 10.5 %collective-permute-start.4 = (bf16[9,16,128]{2,1,0:T(8,128)(2,1)S(1)}, bf16[9,16,128]{2,1,0:T(8,128)(2,1)S(1)}, u32[]{:S(2)}, u32[]{:S(2)}) collective-permute-start(bf16[9,16,128]{2,1,0:T(8,128)(2,1)S(1)} %shard_map.138.one), channel_id=1, source_target_pairs={{0,192},{64,0},{128,64},{192,128},{1,193},{65,1},{129,65},{193,129... | collective-permute-start | bytes 110600 | tf_op jit(solution)/shard_map/ppermute | solution.py:355
  39.5 7.9 %collective-permute-start.3 = (bf16[9,16,128]{2,1,0:T(8,128)(2,1)S(1)}, bf16[9,16,128]{2,1,0:T(8,128)(2,1)S(1)}, u32[]{:S(2)}, u32[]{:S(2)}) collective-permute-start(bf16[9,16,128]{2,1,0:T(8,128)(2,1)S(1)} %shard_map.138.one), channel_id=1, source_target_pairs={{0,128},{64,192},{128,0},{192,64},{1,129},{65,193},{129,1},{193,65... | collective-permute-start | bytes 110600 | tf_op jit(solution)/shard_map/ppermute | solution.py:355
  40.9 6.8 %collective-permute-start.2 = (bf16[9,16,128]{2,1,0:T(8,128)(2,1)S(1)}, bf16[9,16,128]{2,1,0:T(8,128)(2,1)S(1)}, u32[]{:S(2)}, u32[]{:S(2)}) collective-permute-start(bf16[9,16,128]{2,1,0:T(8,128)(2,1)S(1)} %shard_map.138.one), channel_id=1, source_target_pairs={{0,64},{64,128},{128,192},{192,0},{1,65},{65,129},{129,193},{193,1... | collective-permute-start | bytes 110600 | tf_op jit(solution)/shard_map/ppermute | solution.py:355
  49.0 20.8 %all-to-all-start.1 = ((bf16[32,9,16,128]{3,2,1,0:T(8,128)(2,1)}), bf16[32,9,16,128]{3,2,1,0:T(8,128)(2,1)S(1)}, u32[]{:S(2)}, u32[]{:S(2)}) async-start(bf16[32,9,16,128]{3,2,1,0:T(8,128)(2,1)} %shard_map.141), calls=%async_computation.1 | async-start | bytes 2359296 | tf_op jit(solution)/shard_map/all_to_all | solution.py:363
